TPU v7x, 32 devices: a whole 2x2x4 slice. The times are simulated.
32 devices in a mesh: phi: 16 (over z, y, x), row: 2 (over core).
Axes of the slice: x: 2, y: 2, z: 4, core: 2. Of those that a mesh axis runs over, the one named last changes fastest.
Arguments:
- magnetogram: bfloat16 [4096, 1024], P('phi', 'row'), may hold values from -6 to 6
- col_owner: int32 [4096], P('phi'), may hold values from 0 to 15, as said below
- col_offset: int32 [4096], P('phi'), may hold values from 0 to 31, as said below
- phi_weight: bfloat16 [512, 768], P(None, 'phi'), may hold values from -0.375 to 0.375
- theta_weight: bfloat16 [1024, 128], P('row'), may hold values from -0.1875 to 0.1875
- radial_coef: float32 [8], replicated, may hold values from 0.3 to 3
- theta_coef: float32 [128], replicated, may hold values from 0.3 to 3
- phi_coef: float32 [768], replicated, may hold values from 0.3 to 3
- start_field: float32 [8, 768, 128], P('row', 'phi'), may hold values from -0.3125 to 0.3125
Outputs:
- solution_field: float32 [8, 768, 128], P('row', 'phi')
- residual: float32 [8, 768, 128], P('row', 'phi')
Inputs may be any that keep to these rules, and one draw needn't show every extreme that they name: `col_owner`: within each aligned block of 256 columns (the columns of one index of phi) at most 32 columns share an owner, and one owner receives exactly 32 columns from every block. `col_offset`: columns of one aligned block of 256 columns that share an owner have distinct offsets.
All inputs are finite; a program needn't handle non-finite values.
Results may differ from a plain program's by a relative error of at most 0.019.
Values may be sent and summed in bfloat16 or wider, within the bound.
No kernel may reach another device: no remote copies, remote signals or barrier semaphores. Data moves between devices by JAX's collectives and lax.ppermute only.
A program may use at most 64 MiB of HBM per device.

v0:
```python
import jax
import jax.numpy as jnp
from jax import lax
from jax.sharding import PartitionSpec as P

ITERS = 2


def with_halo(block, sides, width, periodic):
    for axis, dim in sides:
        count = lax.axis_size(axis)
        forward = [(i, i + 1) for i in range(count - 1)]
        if periodic:
            forward.append((count - 1, 0))
        backward = [(target, source) for source, target in forward]
        low = lax.ppermute(
            lax.slice_in_dim(block, block.shape[dim] - width, None, axis=dim), axis, forward
        )
        high = lax.ppermute(lax.slice_in_dim(block, 0, width, axis=dim), axis, backward)
        block = jnp.concatenate([low, block, high], axis=dim)
    return block


def face_coefs(radial_coef, theta_coef, phi_coef):
    radial_mid = 0.5 * (radial_coef[:-1] + radial_coef[1:])
    radial_upper = jnp.concatenate([radial_mid, radial_coef[-1:]])
    radial_lower = jnp.concatenate([radial_coef[:1], radial_mid])
    theta_mid = 0.5 * (theta_coef[:-1] + theta_coef[1:])
    zero_one = jnp.zeros((1,), jnp.float32)
    theta_upper = jnp.concatenate([theta_mid, zero_one])
    theta_lower = jnp.concatenate([zero_one, theta_mid])
    phi_upper = 0.5 * (phi_coef + jnp.roll(phi_coef, -1))
    phi_lower = jnp.roll(phi_upper, 1)
    return (radial_upper, radial_lower, theta_upper, theta_lower, phi_upper, phi_lower)


def split_product(form, data, weight):
    upper_part = data.astype(jnp.bfloat16)
    remainder = data - lax.optimization_barrier(upper_part).astype(jnp.float32)
    middle_part = remainder.astype(jnp.bfloat16)
    remainder = remainder - lax.optimization_barrier(middle_part).astype(jnp.float32)
    lower_part = remainder.astype(jnp.bfloat16)
    total = jnp.einsum(form, upper_part, weight, preferred_element_type=jnp.float32)
    total = total + jnp.einsum(form, middle_part, weight, preferred_element_type=jnp.float32)
    return total + jnp.einsum(form, lower_part, weight, preferred_element_type=jnp.float32)


def precond_total(residual, precond):
    return lax.psum(jnp.sum(residual * precond), ("phi", "row"))


def body(
    magnetogram,
    col_owner,
    col_offset,
    phi_weight,
    theta_weight,
    radial_coef,
    theta_coef,
    phi_coef,
    start_field,
):
    layers, cells, width = start_field.shape
    phi_devices = lax.axis_size("phi")
    slots = phi_weight.shape[0]
    capacity = slots // phi_devices
    faces = face_coefs(radial_coef, theta_coef, phi_coef)
    row_start = lax.axis_index("row") * layers
    phi_start = lax.axis_index("phi") * cells
    rad_upper = lax.dynamic_slice_in_dim(faces[0], row_start, layers)[:, None, None]
    rad_lower = lax.dynamic_slice_in_dim(faces[1], row_start, layers)[:, None, None]
    lat_upper = faces[2][None, None, :]
    lat_lower = faces[3][None, None, :]
    lon_upper = lax.dynamic_slice_in_dim(faces[4], phi_start, cells)[None, :, None]
    lon_lower = lax.dynamic_slice_in_dim(faces[5], phi_start, cells)[None, :, None]
    inv_diag = 1.0 / (rad_upper + rad_lower + lat_upper + lat_lower + lon_upper + lon_lower)

    def apply_operator(field):
        phi_pad = with_halo(field, (("phi", 1),), 1, True)
        radial_pad = with_halo(field, (("row", 0),), 1, False)
        theta_pad = jnp.pad(field, ((0, 0), (0, 0), (1, 1)))
        result = rad_upper * (field - radial_pad[2:]) + rad_lower * (field - radial_pad[:-2])
        result = (
            result
            + lat_upper * (field - theta_pad[:, :, 2:])
            + lat_lower * (field - theta_pad[:, :, :-2])
        )
        result = (
            result + lon_upper * (field - phi_pad[:, 2:]) + lon_lower * (field - phi_pad[:, :-2])
        )
        return result

    destination = col_owner * capacity + col_offset
    matching = destination[None, :] == jnp.arange(slots, dtype=jnp.int32)[:, None]
    column_ids = jnp.arange(destination.shape[0], dtype=jnp.int32)
    slot_column = jnp.sum(jnp.where(matching, column_ids[None, :], 0), axis=1)
    filled = jnp.any(matching, axis=1)[:, None]
    blocks = phi_weight.reshape(phi_devices, capacity, cells)
    packed = jnp.where(
        filled, jnp.take(magnetogram, slot_column, axis=0), jnp.zeros((), jnp.bfloat16)
    )
    packed = packed.reshape(phi_devices, capacity, -1)
    partial_lon = jnp.einsum(
        "sck,scm->km",
        blocks,
        lax.all_to_all(packed, "phi", split_axis=0, concat_axis=0, tiled=True),
        preferred_element_type=jnp.float32,
    )
    partial_bnd = split_product("km,mj->kj", partial_lon, theta_weight)
    boundary = lax.psum(partial_bnd, "row")
    inner_flag = (lax.axis_index("row") == 0).astype(jnp.float32)
    inner_layer = (inner_flag * rad_lower[0] * boundary)[None]
    right_side = jnp.concatenate(
        [inner_layer, jnp.zeros((layers - 1, cells, width), jnp.float32)], axis=0
    )
    solution_field = start_field
    residual = right_side - apply_operator(start_field)
    precond = residual * inv_diag
    direction = precond
    norm_now = precond_total(residual, precond)
    for sweep_index in range(ITERS):
        image = apply_operator(direction)
        alpha = norm_now / lax.psum(jnp.sum(direction * image), ("phi", "row"))
        solution_field = solution_field + alpha * direction
        residual = residual - alpha * image
        if sweep_index + 1 < ITERS:
            precond = residual * inv_diag
            norm_next = precond_total(residual, precond)
            direction = precond + norm_next / norm_now * direction
            norm_now = norm_next
    return (solution_field, residual)


def solution(mesh):
    in_specs = (
        P("phi", "row"),
        P("phi"),
        P("phi"),
        P(None, "phi"),
        P("row", None),
        P(),
        P(),
        P(),
        P("row", "phi", None),
    )
    out_specs = (P("row", "phi", None), P("row", "phi", None))
    return jax.shard_map(body, mesh=mesh, in_specs=in_specs, out_specs=out_specs, check_vma=False)
```

profile of v0, /device:TPU:0, one launch (start us, length us, event | category | flops | bytes accessed | tf_op | source)
XLA Modules:
  0.0 191.1 jit_solution(11676633855583425458)
XLA Ops:
  0.6 0.7 multiply_add_fusion.2
  1.4 0.1 select_reduce_fusion
  1.5 0.2 fusion
  1.7 0.1 reduce_sum.50
  1.8 0.1 broadcast_in_dim.50
  1.9 2.0 %gather_fusion = bf16[512,512]{1,0:T(8,128)(2,1)S(1)} fusion(bf16[256,512]{1,0:T(8,128)(2,1)S(1)} %copy-done, s32[1024]{0:T(1024)S(1)} %pad_clamp_fusion), kind=kCustom, calls=%fused_computation | custom fusion | bytes 1050624 | tf_op jit(solution)/shard_map/jit(_take)/gather | solution.py:100
  3.9 1.0 select_select_fusion
  4.9 8.4 %all-to-all-start = ((bf16[16,32,512]{2,1,0:T(8,128)(2,1)}), bf16[16,32,512]{2,1,0:T(8,128)(2,1)S(1)}, u32[]{:S(2)}, u32[]{:S(2)}) async-start(bf16[16,32,512]{2,1,0:T(8,128)(2,1)} %select_select_fusion), calls=%async_computation | async-start | bytes 1048576 | tf_op jit(solution)/shard_map/all_to_all | solution.py:106
  13.4 1.3 collective-permute-start
  14.7 3.0 %collective-permute-start.1 = (f32[1,48,128]{2,1,0:T(8,128)S(1)}, f32[1,48,128]{2,1,0:T(8,128)S(1)}, u32[]{:S(2)}, u32[]{:S(2)}) collective-permute-start(f32[1,48,128]{2,1,0:T(8,128)S(1)} %get-tuple-element.25), channel_id=1, source_target_pairs={{0,1},{2,3},{4,5},{6,7},{8,9},{10,11},{12,13},{14,15},{16,17},{18,... | collective-permute-start | bytes 73736 | tf_op jit(solution)/shard_map/ppermute | solution.py:16
  17.7 5.6 %collective-permute-start.2 = (f32[4,1,128]{2,1,0:T(1,128)S(1)}, f32[4,1,128]{2,1,0:T(1,128)S(1)}, u32[]{:S(2)}, u32[]{:S(2)}) collective-permute-start(f32[4,1,128]{2,1,0:T(1,128)S(1)} %get-tuple-element.26), channel_id=1, source_target_pairs={{2,0},{4,2},{6,4},{8,6},{10,8},{12,10},{14,12},{16,14},{18,16},{20... | collective-permute-start | bytes 6152 | tf_op jit(solution)/shard_map/ppermute | solution.py:19
  23.4 0.5 slice.154
  23.9 0.1 copy.14
  24.1 0.6 copy-done.5
  24.7 0.6 fusion.67
  25.3 0.7 fusion.56
  26.0 0.6 slice.157
  26.7 0.7 pad_maximum_fusion.12
  27.4 0.1 dynamic_slice.15
  27.6 1.4 pad_maximum_fusion.13
  28.9 0.1 fusion.60
  29.1 0.6 copy-done.6
  29.7 0.1 pad_maximum_fusion.15
  29.9 0.2 fusion.68
  30.1 0.7 copy-done.1
  30.8 0.1 fusion.69
  31.0 0.1 convolution_add_fusion.1
  31.1 0.1 convolution_add_fusion
  31.3 3.4 %psum.35 = f32[48,128]{1,0:T(8,128)S(1)} all-reduce(f32[48,128]{1,0:T(8,128)S(1)} %convolution_add_fusion), channel_id=1, replica_groups=mesh['phi'=16,'row'=2] {'row'}, use_global_device_ids=true, to_apply=%region_2.3 | all-reduce | flops 6144 | bytes 49152 | tf_op jit(solution)/shard_map/psum | solution.py:110
  34.8 0.2 fusion.54
  34.9 1.3 collective-permute-start.4
  36.2 3.0 %collective-permute-start.5 = (f32[1,48,128]{2,1,0:T(8,128)S(1)}, f32[1,48,128]{2,1,0:T(8,128)S(1)}, u32[]{:S(2)}, u32[]{:S(2)}) collective-permute-start(f32[1,48,128]{2,1,0:T(8,128)S(1)} %get-tuple-element.21), channel_id=1, source_target_pairs={{0,1},{2,3},{4,5},{6,7},{8,9},{10,11},{12,13},{14,15},{16,17},{18,... | collective-permute-start | bytes 73736 | tf_op jit(solution)/shard_map/ppermute | solution.py:16
  39.3 5.7 %collective-permute-start.6 = (f32[4,1,128]{2,1,0:T(1,128)S(1)}, f32[4,1,128]{2,1,0:T(1,128)S(1)}, u32[]{:S(2)}, u32[]{:S(2)}) collective-permute-start(f32[4,1,128]{2,1,0:T(1,128)S(1)} %get-tuple-element.22), channel_id=1, source_target_pairs={{2,0},{4,2},{6,4},{8,6},{10,8},{12,10},{14,12},{16,14},{18,16},{20... | collective-permute-start | bytes 6152 | tf_op jit(solution)/shard_map/ppermute | solution.py:19
  45.0 1.3 collective-permute-done.6
  46.3 5.9 %collective-permute-done.7 = f32[4,1,128]{2,1,0:T(1,128)S(1)} collective-permute-done((f32[4,1,128]{2,1,0:T(1,128)S(1)}, f32[4,1,128]{2,1,0:T(1,128)S(1)}, u32[]{:S(2)}, u32[]{:S(2)}) %collective-permute-start.7) | collective-permute-done | bytes 2080 | tf_op jit(solution)/shard_map/ppermute | solution.py:16
  52.1 0.8 multiply_reduce_fusion.2
  52.9 37.1 %all-reduce.4 = (f32[]{:T(128)}, f32[]{:T(128)}) all-reduce(f32[]{:T(128)} %get-tuple-element.3, f32[]{:T(128)} %get-tuple-element.2), channel_id=1, replica_groups=mesh['phi'=16,'row'=2] {'phi','row'}, use_global_device_ids=true, to_apply=%region_4.5 | all-reduce | flops 2 | bytes 16 | tf_op jit(solution)/shard_map/psum | solution.py:49
  91.3 0.7 multiply_reduce_fusion.1
  92.0 41.3 %psum.38 = f32[]{:T(128)} all-reduce(f32[]{:T(128)} %get-tuple-element.8), channel_id=1, replica_groups=mesh['phi'=16,'row'=2] {'phi','row'}, use_global_device_ids=true, to_apply=%region_8.9 | all-reduce | flops 1 | bytes 8 | tf_op jit(solution)/shard_map/psum | solution.py:49
  134.7 0.1 multiply_add_fusion.1
  134.8 1.3 collective-permute-start.8
  136.1 3.0 %collective-permute-start.9 = (f32[1,48,128]{2,1,0:T(8,128)S(1)}, f32[1,48,128]{2,1,0:T(8,128)S(1)}, u32[]{:S(2)}, u32[]{:S(2)}) collective-permute-start(f32[1,48,128]{2,1,0:T(8,128)S(1)} %get-tuple-element.17), channel_id=1, source_target_pairs={{0,1},{2,3},{4,5},{6,7},{8,9},{10,11},{12,13},{14,15},{16,17},{18,... | collective-permute-start | bytes 73736 | tf_op jit(solution)/shard_map/ppermute | solution.py:16
  139.2 4.9 %collective-permute-start.10 = (f32[4,1,128]{2,1,0:T(1,128)S(1)}, f32[4,1,128]{2,1,0:T(1,128)S(1)}, u32[]{:S(2)}, u32[]{:S(2)}) collective-permute-start(f32[4,1,128]{2,1,0:T(1,128)S(1)} %get-tuple-element.18), channel_id=1, source_target_pairs={{2,0},{4,2},{6,4},{8,6},{10,8},{12,10},{14,12},{16,14},{18,16},{20... | collective-permute-start | bytes 6152 | tf_op jit(solution)/shard_map/ppermute | solution.py:19
  144.0 1.3 collective-permute-done.10
  145.3 5.9 %collective-permute-done.11 = f32[4,1,128]{2,1,0:T(1,128)S(1)} collective-permute-done((f32[4,1,128]{2,1,0:T(1,128)S(1)}, f32[4,1,128]{2,1,0:T(1,128)S(1)}, u32[]{:S(2)}, u32[]{:S(2)}) %collective-permute-start.11) | collective-permute-done | bytes 2080 | tf_op jit(solution)/shard_map/ppermute | solution.py:16
  151.2 0.7 multiply_reduce_fusion
  152.0 37.1 %psum.39 = f32[]{:T(128)} all-reduce(f32[]{:T(128)} %get-tuple-element.6), channel_id=1, replica_groups=mesh['phi'=16,'row'=2] {'phi','row'}, use_global_device_ids=true, to_apply=%region_10.11 | all-reduce | flops 1 | bytes 8 | tf_op jit(solution)/shard_map/psum | solution.py:123
  190.4 0.7 multiply_subtract_fusion
  (39 shorter events, 0.5 us)
Async XLA Ops:
  0.6 1.3 copy-start
  4.9 8.5 %copy-start.2 = (f32[4,48,128]{2,1,0:T(8,128)S(1)}, f32[4,48,128]{2,1,0:T(8,128)}, u32[]{:S(2)}) copy-start(f32[4,48,128]{2,1,0:T(8,128)} %param.17) | copy-start | bytes 294916
  4.9 25.0 %all-to-all-start = ((bf16[16,32,512]{2,1,0:T(8,128)(2,1)}), bf16[16,32,512]{2,1,0:T(8,128)(2,1)S(1)}, u32[]{:S(2)}, u32[]{:S(2)}) async-start(bf16[16,32,512]{2,1,0:T(8,128)(2,1)} %select_select_fusion), calls=%async_computation | async-start | bytes 1048576 | tf_op jit(solution)/shard_map/all_to_all | solution.py:106
  13.3 10.6 %copy-start.3 = (bf16[512,48]{0,1:T(8,128)(2,1)S(1)}, bf16[512,48]{0,1:T(8,128)(2,1)}, u32[]{:S(2)}) copy-start(bf16[512,48]{0,1:T(8,128)(2,1)} %param.12) | copy-start | bytes 147460
  13.4 21.4 %collective-permute-start = (f32[1,48,128]{2,1,0:T(8,128)S(1)}, f32[1,48,128]{2,1,0:T(8,128)S(1)}, u32[]{:S(2)}, u32[]{:S(2)}) collective-permute-start(f32[1,48,128]{2,1,0:T(8,128)S(1)} %get-tuple-element.24), channel_id=1, source_target_pairs={{1,0},{3,2},{5,4},{7,6},{9,8},{11,10},{13,12},{15,14},{17,16},{19,... | collective-permute-start | bytes 73736 | tf_op jit(solution)/shard_map/ppermute | solution.py:19
  14.7 20.1 %collective-permute-start.1 = (f32[1,48,128]{2,1,0:T(8,128)S(1)}, f32[1,48,128]{2,1,0:T(8,128)S(1)}, u32[]{:S(2)}, u32[]{:S(2)}) collective-permute-start(f32[1,48,128]{2,1,0:T(8,128)S(1)} %get-tuple-element.25), channel_id=1, source_target_pairs={{0,1},{2,3},{4,5},{6,7},{8,9},{10,11},{12,13},{14,15},{16,17},{18,... | collective-permute-start | bytes 73736 | tf_op jit(solution)/shard_map/ppermute | solution.py:16
  17.7 5.6 %copy-start.4 = (f32[768]{0:T(1024)S(1)}, f32[768]{0:T(1024)}, u32[]{:S(2)}) copy-start(f32[768]{0:T(1024)} %param.16) | copy-start | bytes 9220
  17.7 17.0 %collective-permute-start.2 = (f32[4,1,128]{2,1,0:T(1,128)S(1)}, f32[4,1,128]{2,1,0:T(1,128)S(1)}, u32[]{:S(2)}, u32[]{:S(2)}) collective-permute-start(f32[4,1,128]{2,1,0:T(1,128)S(1)} %get-tuple-element.26), channel_id=1, source_target_pairs={{2,0},{4,2},{6,4},{8,6},{10,8},{12,10},{14,12},{16,14},{18,16},{20... | collective-permute-start | bytes 6152 | tf_op jit(solution)/shard_map/ppermute | solution.py:19
  23.3 11.4 %collective-permute-start.3 = (f32[4,1,128]{2,1,0:T(1,128)S(1)}, f32[4,1,128]{2,1,0:T(1,128)S(1)}, u32[]{:S(2)}, u32[]{:S(2)}) collective-permute-start(f32[4,1,128]{2,1,0:T(1,128)S(1)} %get-tuple-element.27), channel_id=1, source_target_pairs={{0,2},{2,4},{4,6},{6,8},{8,10},{10,12},{12,14},{14,16},{16,18},{18... | collective-permute-start | bytes 6152 | tf_op jit(solution)/shard_map/ppermute | solution.py:16
  24.1 0.7 copy-start.5
  29.0 0.7 copy-start.6
  29.9 0.9 copy-start.1
  34.9 17.2 %collective-permute-start.4 = (f32[1,48,128]{2,1,0:T(8,128)S(1)}, f32[1,48,128]{2,1,0:T(8,128)S(1)}, u32[]{:S(2)}, u32[]{:S(2)}) collective-permute-start(f32[1,48,128]{2,1,0:T(8,128)S(1)} %get-tuple-element.20), channel_id=1, source_target_pairs={{1,0},{3,2},{5,4},{7,6},{9,8},{11,10},{13,12},{15,14},{17,16},{19,... | collective-permute-start | bytes 73736 | tf_op jit(solution)/shard_map/ppermute | solution.py:19
  36.2 15.9 %collective-permute-start.5 = (f32[1,48,128]{2,1,0:T(8,128)S(1)}, f32[1,48,128]{2,1,0:T(8,128)S(1)}, u32[]{:S(2)}, u32[]{:S(2)}) collective-permute-start(f32[1,48,128]{2,1,0:T(8,128)S(1)} %get-tuple-element.21), channel_id=1, source_target_pairs={{0,1},{2,3},{4,5},{6,7},{8,9},{10,11},{12,13},{14,15},{16,17},{18,... | collective-permute-start | bytes 73736 | tf_op jit(solution)/shard_map/ppermute | solution.py:16
  39.3 7.0 %collective-permute-start.6 = (f32[4,1,128]{2,1,0:T(1,128)S(1)}, f32[4,1,128]{2,1,0:T(1,128)S(1)}, u32[]{:S(2)}, u32[]{:S(2)}) collective-permute-start(f32[4,1,128]{2,1,0:T(1,128)S(1)} %get-tuple-element.22), channel_id=1, source_target_pairs={{2,0},{4,2},{6,4},{8,6},{10,8},{12,10},{14,12},{16,14},{18,16},{20... | collective-permute-start | bytes 6152 | tf_op jit(solution)/shard_map/ppermute | solution.py:19
  44.9 7.2 %collective-permute-start.7 = (f32[4,1,128]{2,1,0:T(1,128)S(1)}, f32[4,1,128]{2,1,0:T(1,128)S(1)}, u32[]{:S(2)}, u32[]{:S(2)}) collective-permute-start(f32[4,1,128]{2,1,0:T(1,128)S(1)} %get-tuple-element.23), channel_id=1, source_target_pairs={{0,2},{2,4},{4,6},{6,8},{8,10},{10,12},{12,14},{14,16},{16,18},{18... | collective-permute-start | bytes 6152 | tf_op jit(solution)/shard_map/ppermute | solution.py:16
  134.8 16.4 %collective-permute-start.8 = (f32[1,48,128]{2,1,0:T(8,128)S(1)}, f32[1,48,128]{2,1,0:T(8,128)S(1)}, u32[]{:S(2)}, u32[]{:S(2)}) collective-permute-start(f32[1,48,128]{2,1,0:T(8,128)S(1)} %get-tuple-element.16), channel_id=1, source_target_pairs={{1,0},{3,2},{5,4},{7,6},{9,8},{11,10},{13,12},{15,14},{17,16},{19,... | collective-permute-start | bytes 73736 | tf_op jit(solution)/shard_map/ppermute | solution.py:19
  136.1 15.1 %collective-permute-start.9 = (f32[1,48,128]{2,1,0:T(8,128)S(1)}, f32[1,48,128]{2,1,0:T(8,128)S(1)}, u32[]{:S(2)}, u32[]{:S(2)}) collective-permute-start(f32[1,48,128]{2,1,0:T(8,128)S(1)} %get-tuple-element.17), channel_id=1, source_target_pairs={{0,1},{2,3},{4,5},{6,7},{8,9},{10,11},{12,13},{14,15},{16,17},{18,... | collective-permute-start | bytes 73736 | tf_op jit(solution)/shard_map/ppermute | solution.py:16
  139.2 6.2 %collective-permute-start.10 = (f32[4,1,128]{2,1,0:T(1,128)S(1)}, f32[4,1,128]{2,1,0:T(1,128)S(1)}, u32[]{:S(2)}, u32[]{:S(2)}) collective-permute-start(f32[4,1,128]{2,1,0:T(1,128)S(1)} %get-tuple-element.18), channel_id=1, source_target_pairs={{2,0},{4,2},{6,4},{8,6},{10,8},{12,10},{14,12},{16,14},{18,16},{20... | collective-permute-start | bytes 6152 | tf_op jit(solution)/shard_map/ppermute | solution.py:19
  144.0 7.2 %collective-permute-start.11 = (f32[4,1,128]{2,1,0:T(1,128)S(1)}, f32[4,1,128]{2,1,0:T(1,128)S(1)}, u32[]{:S(2)}, u32[]{:S(2)}) collective-permute-start(f32[4,1,128]{2,1,0:T(1,128)S(1)} %get-tuple-element.19), channel_id=1, source_target_pairs={{0,2},{2,4},{4,6},{6,8},{8,10},{10,12},{12,14},{14,16},{16,18},{18... | collective-permute-start | bytes 6152 | tf_op jit(solution)/shard_map/ppermute | solution.py:16
where the time goes:
time: 193 us; the launch traced here: 191 us
  blocking collectives  119 us (62%)
  starting transfers between devices  37.5 us (19%)
  waiting for transfers between devices  14.4 us (7%)
  other arithmetic  8.42 us (4%)
  local copies, waits for them, and re-layouts  6.19 us (3%)
  between operations  4.99 us (3%)
    psum x2, blocking collectives, precond_total(): return lax.psum(jnp.sum(residual * precond), ('phi', 'row'))  78.4 us
    psum x1, blocking collectives, body(): alpha = norm_now / lax.psum(jnp.sum(direction * image), ('phi', 'row'))  37.1 us
    ppermute x6, starting transfers between devices, with_halo(): lax.ppermute(lax.slice_in_dim(block, 0, width, axis=dim), axis, backward)  20 us
    ppermute x6, waiting for transfers between devices, with_halo(): lax.ppermute(lax.slice_in_dim(block, block.shape[dim] - width, None, axis...  11.8 us
    ppermute x6, starting transfers between devices, with_halo(): lax.ppermute(lax.slice_in_dim(block, block.shape[dim] - width, None, axis...  9.09 us
    all_to_all x1, starting transfers between devices, body(): lax.all_to_all(packed, 'phi', split_axis=0, concat_axis=0, tiled=True)  8.44 us
  transfers between devices with their start and end apart: 13, of which 4 were waited for; matrix products, arithmetic and copies ran while one was open for 3% of the time, Pallas kernels for 0%

commit v1 on v0

v1 whole, which is shorter than its diff:
```python
import jax
import jax.numpy as jnp
from jax import lax
from jax.sharding import PartitionSpec as P

REACH = 3


def face_coefs(radial_coef, theta_coef, phi_coef):
    radial_mid = 0.5 * (radial_coef[:-1] + radial_coef[1:])
    radial_upper = jnp.concatenate([radial_mid, radial_coef[-1:]])
    radial_lower = jnp.concatenate([radial_coef[:1], radial_mid])
    theta_mid = 0.5 * (theta_coef[:-1] + theta_coef[1:])
    zero_one = jnp.zeros((1,), jnp.float32)
    theta_upper = jnp.concatenate([theta_mid, zero_one])
    theta_lower = jnp.concatenate([zero_one, theta_mid])
    phi_upper = 0.5 * (phi_coef + jnp.roll(phi_coef, -1))
    phi_lower = jnp.roll(phi_upper, 1)
    return (radial_upper, radial_lower, theta_upper, theta_lower, phi_upper, phi_lower)


def row_sum(value, rows):
    if rows == 2:
        return value + lax.ppermute(value, "row", [(0, 1), (1, 0)])
    return lax.psum(value, "row")


def pick(chunks, index):
    return lax.dynamic_index_in_dim(chunks, index, 0, keepdims=False)


def step_sizes(a, b, c, e):
    alpha = a / b
    beta = (alpha * alpha * c - a) / a
    gain = 1.0 + beta
    curvature = gain * gain * b - 2.0 * gain * alpha * c + alpha * alpha * e
    return alpha, gain, beta * a / curvature


def body(
    magnetogram,
    col_owner,
    col_offset,
    phi_weight,
    theta_weight,
    radial_coef,
    theta_coef,
    phi_coef,
    start_field,
):
    layers, cells, width = start_field.shape
    phi_devices = lax.axis_size("phi")
    rows = lax.axis_size("row")
    slots = phi_weight.shape[0]
    capacity = slots // phi_devices
    per = capacity // rows
    here = lax.axis_index("phi")
    row = lax.axis_index("row")
    above = lax.rem(here + 1, phi_devices)
    below = lax.rem(here + phi_devices - 1, phi_devices)

    climb = [(i, i + 1) for i in range(rows - 1)]
    low_layers = lax.ppermute(start_field[layers - REACH :], "row", climb)
    high_layers = lax.ppermute(start_field[:REACH], "row", [(t, s) for s, t in climb])
    window = jnp.concatenate([low_layers, start_field, high_layers], axis=0)

    columns = jnp.dot(magnetogram, theta_weight, preferred_element_type=jnp.float32)
    columns = row_sum(columns, rows)
    upper_part = lax.optimization_barrier(columns.astype(jnp.bfloat16))
    lower_part = (columns - upper_part.astype(jnp.float32)).astype(jnp.bfloat16)

    place = col_offset - row * per
    target = jnp.where((place >= 0) & (place < per), col_owner * per + place, -1)
    chosen = (target[None, :] == jnp.arange(phi_devices * per, dtype=jnp.int32)[:, None]).astype(
        jnp.bfloat16
    )
    packed = jnp.dot(chosen, upper_part, preferred_element_type=jnp.float32)
    packed = packed + jnp.dot(chosen, lower_part, preferred_element_type=jnp.float32)
    packed = packed.reshape(phi_devices, per, width)
    share = phi_weight.reshape(phi_devices, rows, per, cells)
    share = lax.dynamic_index_in_dim(share, row, 1, keepdims=False)
    share = share.reshape(phi_devices * per, cells)

    def edge(start):
        field = window[:, start : start + REACH].reshape(-1, width)
        lo = start + 1 if start else 0
        weights = share[:, lo : lo + 2].astype(jnp.float32).T.reshape(-1, width)
        return jnp.concatenate([field, weights], axis=0)

    to_above, to_below = edge(cells - REACH), edge(0)
    who = jnp.arange(phi_devices, dtype=jnp.int32)[:, None, None]
    edges = jnp.where(who == above, to_above[None], jnp.where(who == below, to_below[None], 0.0))
    sent = jnp.concatenate(
        [packed, jnp.roll(packed, 1, axis=0), jnp.roll(packed, -1, axis=0), edges], axis=1
    )
    got = lax.all_to_all(sent, "phi", split_axis=0, concat_axis=0, tiled=True)
    edge_low, edge_high = pick(got, below)[3 * per :], pick(got, above)[3 * per :]
    reach_rows = window.shape[0] * REACH

    def weigh(weights, which):
        data = got[:, which * per : (which + 1) * per].reshape(phi_devices * per, width)
        part = lax.optimization_barrier(data.astype(jnp.bfloat16))
        rest = (data - part.astype(jnp.float32)).astype(jnp.bfloat16)
        total = jnp.dot(weights, part, preferred_element_type=jnp.float32)
        return total + jnp.dot(weights, rest, preferred_element_type=jnp.float32)

    def ghost_weights(edge_rows):
        return edge_rows[reach_rows:].reshape(2, phi_devices * per).astype(jnp.bfloat16)

    boundary = row_sum(
        jnp.concatenate(
            [
                weigh(ghost_weights(edge_low), 1),
                weigh(share.T, 0),
                weigh(ghost_weights(edge_high), 2),
            ],
            axis=0,
        ),
        rows,
    )
    field = jnp.concatenate(
        [
            edge_low[:reach_rows].reshape(-1, REACH, width),
            window,
            edge_high[:reach_rows].reshape(-1, REACH, width),
        ],
        axis=1,
    )

    faces = face_coefs(radial_coef, theta_coef, phi_coef)
    spread = layers + 2 * REACH

    def radial_window(coef):
        padded = jnp.pad(coef, (REACH, REACH))
        return lax.dynamic_slice_in_dim(padded, row * layers, spread)[:, None, None]

    def phi_window(coef):
        padded = jnp.concatenate([coef[-REACH:], coef, coef[:REACH]])
        return lax.dynamic_slice_in_dim(padded, here * cells, cells + 2 * REACH)[None, :, None]

    rad_upper, rad_lower = radial_window(faces[0]), radial_window(faces[1])
    lon_upper, lon_lower = phi_window(faces[4]), phi_window(faces[5])
    lat_upper, lat_lower = faces[2][None, None, :], faces[3][None, None, :]
    inside = radial_window(jnp.ones_like(radial_coef))
    inv_diag = inside / (
        rad_upper + rad_lower + lat_upper + lat_lower + lon_upper + lon_lower + (1.0 - inside)
    )

    def apply_operator(value, depth):
        mid = value[1:-1, 1:-1]
        theta_pad = jnp.pad(mid, ((0, 0), (0, 0), (1, 1)))
        result = rad_upper[depth:-depth] * (mid - value[2:, 1:-1])
        result = result + rad_lower[depth:-depth] * (mid - value[:-2, 1:-1])
        result = result + lat_upper * (mid - theta_pad[:, :, 2:])
        result = result + lat_lower * (mid - theta_pad[:, :, :-2])
        result = result + lon_upper[:, depth:-depth] * (mid - value[1:-1, 2:])
        return result + lon_lower[:, depth:-depth] * (mid - value[1:-1, :-2])

    def inner(value, by):
        return value[by:-by, by:-by] if by else value

    level = row * layers - REACH + 1 + jnp.arange(spread - 2, dtype=jnp.int32)[:, None, None]
    source = jnp.where(level == 0, (faces[1][0] * boundary)[None], 0.0)
    residual = source - apply_operator(field, 1)
    first = residual * inner(inv_diag, 1)
    first_image = apply_operator(first, 2)
    second = first_image * inner(inv_diag, 2)
    second_image = apply_operator(second, 3)
    residual, first = inner(residual, 2), inner(first, 2)
    first_image, second = inner(first_image, 1), inner(second, 1)

    pairs = (
        (residual, first),
        (first, first_image),
        (first_image, second),
        (second, second_image),
    )
    sums = jnp.stack([jnp.sum(u * v, axis=(0, 1)) for u, v in pairs] * 2)
    devices = phi_devices * rows
    if devices <= 64:
        shared = jnp.broadcast_to(sums[None], (devices,) + sums.shape)
        shared = lax.all_to_all(shared, ("phi", "row"), split_axis=0, concat_axis=0, tiled=True)
        totals = jnp.sum(shared, axis=(0, 2))
    else:
        totals = lax.psum(jnp.sum(sums, axis=1), ("phi", "row"))
    alpha, gain, alpha_next = step_sizes(totals[0], totals[1], totals[2], totals[3])
    direction = gain * first - alpha * second
    solution_field = start_field + alpha * first + alpha_next * direction
    image = gain * first_image - alpha * second_image
    return solution_field, residual - alpha * first_image - alpha_next * image


def solution(mesh):
    in_specs = (
        P("phi", "row"),
        P("phi"),
        P("phi"),
        P(None, "phi"),
        P("row", None),
        P(),
        P(),
        P(),
        P("row", "phi", None),
    )
    out_specs = (P("row", "phi", None), P("row", "phi", None))
    return jax.shard_map(body, mesh=mesh, in_specs=in_specs, out_specs=out_specs, check_vma=False)
```

time: 193 us -> 65.7 us (0.34)
  blocking collectives: 119 us -> 11.8 us
  starting transfers between devices: 37.5 us -> 12.6 us
  waiting for transfers between devices: 14.4 us -> 18.9 us
    psum x4 -> x0, blocking collectives: 119 us -> none  [the longest x2 78.4 us: precond_total(): return lax.psum(jnp.sum(residual * precond), ('phi', 'row'))]
    ppermute x12 -> x4, starting transfers between devices: 29.1 us -> 4.92 us  [the longest x1 2.36 us: body(): low_layers = lax.ppermute(start_field[layers - REACH:], 'row', climb)]
    all_to_all x1, waiting for transfers between devices: 0.01 us -> 17.8 us  [body(): got = lax.all_to_all(sent, 'phi', split_axis=0, concat_axis=0, tiled=True)]
    ppermute x12 -> x4, waiting for transfers between devices: 14.4 us -> 1.07 us  [the longest x2 1.07 us: row_sum(): return value + lax.ppermute(value, 'row', [(0, 1), (1, 0)])]
    all_to_all x0 -> x1, blocking collectives: none -> 11.8 us  [body(): lax.all_to_all(shared, ('phi', 'row'), split_axis=0, concat_axis=0, tiled...]
    slice x6 -> x19, local copies, waits for them, and re-layouts: 0.04 us -> 2.33 us  [the longest x1 0.98 us: body(): start_field[:REACH]]
    reduce_sum x4 -> x2, other arithmetic: 2.36 us -> 0.33 us  [the longest x1 0.18 us: body(): sums = jnp.stack([jnp.sum(u * v, axis=(0, 1)) for u, v in pairs] * 2)]
    gather x1 -> x0, local copies, waits for them, and re-layouts: 1.97 us -> none  [body(): jnp.take(magnetogram, slot_column, axis=0)]
  transfers between devices with their start and end apart: 13 -> 5, of which waited for: 4 -> 2; matrix products, arithmetic and copies ran while one was open for 3% -> 11% of each run, Pallas kernels for 0% -> 0%
where the time goes in v1:
time: 65.7 us; the launch traced here: 65.2 us
  waiting for transfers between devices  18.9 us (29%)
  starting transfers between devices  12.6 us (19%)
  blocking collectives  11.8 us (18%)
  other arithmetic  7.65 us (12%)
  between operations  6.87 us (10%)
  local copies, waits for them, and re-layouts  5.92 us (9%)
  matrix products  1.46 us (2%)
    all_to_all x1, waiting for transfers between devices, body(): got = lax.all_to_all(sent, 'phi', split_axis=0, concat_axis=0, tiled=True)  17.8 us
    all_to_all x1, blocking collectives, body(): lax.all_to_all(shared, ('phi', 'row'), split_axis=0, concat_axis=0, tiled...  11.8 us
    all_to_all x1, starting transfers between devices, body(): got = lax.all_to_all(sent, 'phi', split_axis=0, concat_axis=0, tiled=True)  7.69 us
    ppermute x1, starting transfers between devices, body(): low_layers = lax.ppermute(start_field[layers - REACH:], 'row', climb)  2.36 us
    concatenate x1, other arithmetic, face_coefs(): radial_lower = jnp.concatenate([radial_coef[:1], radial_mid])  1.37 us
  transfers between devices with their start and end apart: 5, of which 2 were waited for; matrix products, arithmetic and copies ran while one was open for 11% of the time, Pallas kernels for 0%

profile of v1, /device:TPU:0, one launch (start us, length us, event | category | flops | bytes accessed | tf_op | source)
XLA Modules:
  0.0 65.2 jit_solution(1904532030093972381)
XLA Ops:
  0.7 1.0 %fusion.55 = (f32[3,48,128]{2,1,0:T(8,128)S(1)}, f32[3,48,128]{2,1,0:T(8,128)S(1)}) fusion(f32[4,48,128]{2,1,0:T(8,128)} %param.17), kind=kLoop, calls=%fused_computation.134 | loop fusion | bytes 294912 | tf_op jit(solution)/shard_map/slice | solution.py:64
  1.6 2.4 %collective-permute-start.1 = (f32[3,48,128]{2,1,0:T(8,128)S(1)}, f32[3,48,128]{2,1,0:T(8,128)S(1)}, u32[]{:S(2)}, u32[]{:S(2)}) collective-permute-start(f32[3,48,128]{2,1,0:T(8,128)S(1)} %get-tuple-element.32), channel_id=1, source_target_pairs={{0,1},{2,3},{4,5},{6,7},{8,9},{10,11},{12,13},{14,15},{16,17},{18,... | collective-permute-start | bytes 221192 | tf_op jit(solution)/shard_map/ppermute | solution.py:63
  4.0 1.3 %collective-permute-start.2 = (f32[3,48,128]{2,1,0:T(8,128)S(1)}, f32[3,48,128]{2,1,0:T(8,128)S(1)}, u32[]{:S(2)}, u32[]{:S(2)}) collective-permute-start(f32[3,48,128]{2,1,0:T(8,128)S(1)} %get-tuple-element.31), channel_id=1, source_target_pairs={{1,0},{3,2},{5,4},{7,6},{9,8},{11,10},{13,12},{15,14},{17,16},{19,... | collective-permute-start | bytes 221192 | tf_op jit(solution)/shard_map/ppermute | solution.py:64
  5.3 0.2 fusion.59
  5.6 1.2 %collective-permute-start = (f32[256,128]{1,0:T(8,128)S(1)}, f32[256,128]{1,0:T(8,128)S(1)}, u32[]{:S(2)}, u32[]{:S(2)}) collective-permute-start(f32[256,128]{1,0:T(8,128)S(1)} %fusion.59), channel_id=1, source_target_pairs={{0,1},{1,0},{2,3},{3,2},{4,5},{5,4},{6,7},{7,6},{8,9},{9,8},{10,11... | collective-permute-start | bytes 393224 | tf_op jit(solution)/shard_map/ppermute | solution.py:24
  6.8 0.6 fusion.58
  7.4 0.1 add_multiply_fusion.2
  7.5 0.6 slice.298
  8.1 0.7 %fusion.46 = f32[768]{0:T(1024)S(1)} fusion(f32[768]{0:T(1024)S(1)} %copy-done.4, f32[1]{0:T(128)} %slice.298, f32[767]{0:T(1024)S(1)} %slice.297), kind=kLoop, calls=%fused_computation.101 | loop fusion | flops 2304 | bytes 9216 | tf_op jit(solution)/shard_map/mul | solution.py:17
  8.8 0.6 slice.305
  9.6 0.1 copy.16
  9.7 0.1 convert_bitcast_fusion.1
  9.8 0.1 copy.17
  9.9 0.1 copy.18
  10.0 0.7 %copy-done.8 = f32[128]{0:T(128)S(1)} copy-done((f32[128]{0:T(128)S(1)}, f32[128]{0:T(128)}, u32[]{:S(2)}) %copy-start.8) | copy-done | bytes 536
  10.7 0.1 add_multiply_fusion.1
  10.8 0.7 %pad_maximum_fusion.6 = f32[768]{0:T(1024)S(1)} fusion(f32[767]{0:T(1024)S(1)} %bitcast.76, f32[1]{0:T(128)} %slice.305), kind=kLoop, calls=%fused_computation.103 | loop fusion | flops 768 | bytes 6144 | tf_op jit(solution)/shard_map/jit(_roll_static)/concatenate | solution.py:18
  11.5 0.1 pad_maximum_fusion.7
  11.6 0.1 pad_maximum_fusion.5
  11.6 0.1 dynamic-slice_bitcast_fusion.1
  11.7 1.4 %select_maximum_fusion = (f32[14]{0:T(128)S(1)}, f32[14]{0:T(128)S(1)}) fusion(f32[7]{0:T(128)S(1)} %add_multiply_fusion.2, f32[1]{0:T(128)} %get-tuple-element.45, f32[1]{0:T(128)} %get-tuple-element.46), kind=kLoop, calls=%fused_computation.112 | loop fusion | flops 126 | bytes 148 | tf_op jit(solution)/shard_map/concatenate | solution.py:12
  13.1 0.1 pad_dynamic-slice_fusion
  13.2 0.1 dynamic-slice_bitcast_fusion
  13.4 0.1 select_select_fusion
  13.6 0.2 fusion
  13.7 0.2 convolution_add_fusion
  14.0 0.9 %pad_maximum_fusion = f32[16,82,128]{2,1,0:T(8,128)} fusion(f32[16,34,128]{2,1,0:T(8,128)S(1)} %select_select_fusion, f32[1,16,128]{2,1,0:T(8,128)S(1)} %get-tuple-element.28, f32[15,16,128]{2,1,0:T(8,128)S(1)} %bitcast.74, f32[15,16,128]{2,1,0:T(8,128)S(1)} %bitcast.73, f32[1,16,128]{2,1,0:T(8,128)S(1)} %get-tuple-element.27, f32[16,16,128]{2,1,0:T(8,128)S(1)} %bitcast.69), kind=kLoop, calls=%fused_computation.4 | loop fusion | flops 839680 | bytes 1343488 | tf_op jit(solution)/shard_map/concatenate | solution.py:93
  14.9 7.7 %all-to-all-start = ((f32[16,82,128]{2,1,0:T(8,128)}), f32[16,82,128]{2,1,0:T(8,128)S(1)}, u32[]{:S(2)}, u32[]{:S(2)}) async-start(f32[16,82,128]{2,1,0:T(8,128)} %pad_maximum_fusion), calls=%async_computation | async-start | bytes 1441792 | tf_op jit(solution)/shard_map/all_to_all | solution.py:96
  22.6 0.1 dynamic_slice.32
  23.2 0.1 pad_maximum_fusion.8
  23.6 0.1 add_divide_fusion
  23.7 17.8 %all-to-all-done = f32[16,82,128]{2,1,0:T(8,128)S(1)} async-done(((f32[16,82,128]{2,1,0:T(8,128)}), f32[16,82,128]{2,1,0:T(8,128)S(1)}, u32[]{:S(2)}, u32[]{:S(2)}) %all-to-all-start) | async-done | bytes 671776 | tf_op jit(solution)/shard_map/all_to_all | solution.py:96
  41.6 0.2 fusion.61
  41.9 0.1 fusion.60
  42.1 0.1 fusion.62
  42.2 0.1 convolution_add_fusion.3
  42.3 0.2 convolution_add_fusion.1
  42.5 0.1 convolution_add_fusion.2
  42.9 1.1 %collective-permute-done.3 = f32[52,128]{1,0:T(8,128)S(1)} collective-permute-done((f32[52,128]{1,0:T(8,128)S(1)}, f32[52,128]{1,0:T(8,128)S(1)}, u32[]{:S(2)}, u32[]{:S(2)}) %collective-permute-start.3) | collective-permute-done | bytes 26656 | tf_op jit(solution)/shard_map/ppermute | solution.py:24
  43.9 0.7 %add_multiply_fusion = f32[52,128]{1,0:T(8,128)S(1)} fusion(f32[52,128]{1,0:T(8,128)S(1)} %collective-permute-done.3, f32[]{:T(128)} %bitcast, f32[2,128]{1,0:T(2,128)S(1)} %convolution_add_fusion.2, f32[48,128]{1,0:T(8,128)S(1)} %convolution_add_fusion.1, f32[2,128]{1,0:T(2,128)S(1)} %convolution_add_fusion.3), kind=kLoop, calls=%fused_computation.91 | loop fusion | flops 26624 | bytes 79876 | tf_op jit(solution)/shard_map/mul | solution.py:163
  44.6 0.3 slice_multiply_fusion
  44.9 0.2 slice_multiply_fusion.1
  45.2 0.2 multiply_reduce_fusion
  45.4 11.8 %all_to_all.10 = f32[32,8,128]{2,1,0:T(8,128)S(1)} all-to-all(f32[32,8,128]{2,1,0:T(8,128)S(1)} %broadcast_in_dim.95), channel_id=1, replica_groups=mesh['phi'=16,'row'=2] {'phi','row'}, dimensions={0} | all-to-all | bytes 262144 | tf_op jit(solution)/shard_map/all_to_all | solution.py:182
  57.2 0.1 reduce_sum.49
  57.4 0.7 %fusion.57 = (f32[1]{0:T(128)}, f32[1]{0:T(128)}, f32[1]{0:T(128)}, f32[1]{0:T(128)}) fusion(f32[8]{0:T(128)S(1)} %reduce_sum.49), kind=kLoop, calls=%fused_computation.136 | loop fusion | bytes 32 | tf_op jit(solution)/shard_map/slice | solution.py:186
  63.9 0.7 %multiply_add_fusion = f32[4,48,128]{2,1,0:T(8,128)} fusion(f32[4,48,128]{2,1,0:T(8,128)S(1)} %copy-done.1, f32[8,52,128]{2,1,0:T(8,128)S(1)} %get-tuple-element.11, f32[]{:T(128)S(6)} %add.255, f32[]{:T(128)S(6)} %div.21, f32[]{:T(128)S(6)} %div.19, f32[6,50,128]{2,1,0:T(8,128)S(1)} %get-tuple-element.9), kind=kLoop, calls=%fused_computation.85 | loop fusion | flops 172032 | bytes 393228 | tf_op jit(solution)/shard_map/add | solution.py:188
  64.5 0.7 %multiply_subtract_fusion = f32[4,48,128]{2,1,0:T(8,128)} fusion(f32[4,48,128]{2,1,0:T(8,128)S(1)} %get-tuple-element.8, f32[8,52,128]{2,1,0:T(8,128)S(1)} %get-tuple-element.12, f32[6,50,128]{2,1,0:T(8,128)S(1)} %get-tuple-element.10, f32[]{:T(128)S(6)} %add.255, f32[]{:T(128)S(6)} %div.21, f32[]{:T(128)S(6)} %div.19), kind=kLoop, calls=%fused_computation.84 | loop fusion | flops 172032 | bytes 393228 | tf_op jit(solution)/shard_map/sub | solution.py:190
  (73 shorter events, 1.6 us)
Async XLA Ops:
  0.6 4.7 %copy-start = (bf16[256,512]{1,0:T(8,128)(2,1)S(1)}, bf16[256,512]{1,0:T(8,128)(2,1)}, u32[]{:S(2)}) copy-start(bf16[256,512]{1,0:T(8,128)(2,1)} %param.9) | copy-start | bytes 786436
  0.6 4.7 %copy-start.2 = (bf16[512,128]{1,0:T(8,128)(2,1)S(1)}, bf16[512,128]{1,0:T(8,128)(2,1)}, u32[]{:S(2)}) copy-start(bf16[512,128]{1,0:T(8,128)(2,1)} %param.13) | copy-start | bytes 393220
  1.6 11.6 %collective-permute-start.1 = (f32[3,48,128]{2,1,0:T(8,128)S(1)}, f32[3,48,128]{2,1,0:T(8,128)S(1)}, u32[]{:S(2)}, u32[]{:S(2)}) collective-permute-start(f32[3,48,128]{2,1,0:T(8,128)S(1)} %get-tuple-element.32), channel_id=1, source_target_pairs={{0,1},{2,3},{4,5},{6,7},{8,9},{10,11},{12,13},{14,15},{16,17},{18,... | collective-permute-start | bytes 221192 | tf_op jit(solution)/shard_map/ppermute | solution.py:63
  4.0 9.3 %collective-permute-start.2 = (f32[3,48,128]{2,1,0:T(8,128)S(1)}, f32[3,48,128]{2,1,0:T(8,128)S(1)}, u32[]{:S(2)}, u32[]{:S(2)}) collective-permute-start(f32[3,48,128]{2,1,0:T(8,128)S(1)} %get-tuple-element.31), channel_id=1, source_target_pairs={{1,0},{3,2},{5,4},{7,6},{9,8},{11,10},{13,12},{15,14},{17,16},{19,... | collective-permute-start | bytes 221192 | tf_op jit(solution)/shard_map/ppermute | solution.py:64
  5.3 1.4 %copy-start.5 = (f32[8]{0:T(128)S(1)}, f32[8]{0:T(128)}, u32[]{:S(2)}) copy-start(f32[8]{0:T(128)} %param.14) | copy-start | bytes 100
  5.3 2.1 %copy-start.4 = (f32[768]{0:T(1024)S(1)}, f32[768]{0:T(1024)}, u32[]{:S(2)}) copy-start(f32[768]{0:T(1024)} %param.16) | copy-start | bytes 9220
  5.6 4.0 %copy-start.3 = (bf16[512,48]{0,1:T(8,128)(2,1)S(1)}, bf16[512,48]{0,1:T(8,128)(2,1)}, u32[]{:S(2)}) copy-start(bf16[512,48]{0,1:T(8,128)(2,1)} %param.12) | copy-start | bytes 147460
  5.6 7.9 %collective-permute-start = (f32[256,128]{1,0:T(8,128)S(1)}, f32[256,128]{1,0:T(8,128)S(1)}, u32[]{:S(2)}, u32[]{:S(2)}) collective-permute-start(f32[256,128]{1,0:T(8,128)S(1)} %fusion.59), channel_id=1, source_target_pairs={{0,1},{1,0},{2,3},{3,2},{4,5},{5,4},{6,7},{7,6},{8,9},{9,8},{10,11... | collective-permute-start | bytes 393224 | tf_op jit(solution)/shard_map/ppermute | solution.py:24
  10.0 0.7 %copy-start.8 = (f32[128]{0:T(128)S(1)}, f32[128]{0:T(128)}, u32[]{:S(2)}) copy-start(f32[128]{0:T(128)} %param.15) | copy-start | bytes 1540
  10.7 1.0 %copy-start.6 = (s32[256]{0:T(256)S(1)}, s32[256]{0:T(256)}, u32[]{:S(2)}) copy-start(s32[256]{0:T(256)} %param.10) | copy-start | bytes 3076
  10.8 1.0 %copy-start.7 = (s32[256]{0:T(256)S(1)}, s32[256]{0:T(256)}, u32[]{:S(2)}) copy-start(s32[256]{0:T(256)} %param.11) | copy-start | bytes 3076
  11.5 1.8 %copy-start.1 = (f32[4,48,128]{2,1,0:T(8,128)S(1)}, f32[4,48,128]{2,1,0:T(8,128)}, u32[]{:S(2)}) copy-start(f32[4,48,128]{2,1,0:T(8,128)} %param.17) | copy-start | bytes 294916
  14.9 26.6 %all-to-all-start = ((f32[16,82,128]{2,1,0:T(8,128)}), f32[16,82,128]{2,1,0:T(8,128)S(1)}, u32[]{:S(2)}, u32[]{:S(2)}) async-start(f32[16,82,128]{2,1,0:T(8,128)} %pad_maximum_fusion), calls=%async_computation | async-start | bytes 1441792 | tf_op jit(solution)/shard_map/all_to_all | solution.py:96
  42.7 1.3 %collective-permute-start.3 = (f32[52,128]{1,0:T(8,128)S(1)}, f32[52,128]{1,0:T(8,128)S(1)}, u32[]{:S(2)}, u32[]{:S(2)}) collective-permute-start(f32[52,128]{1,0:T(8,128)S(1)} %pad_maximum_fusion.2), channel_id=1, source_target_pairs={{0,1},{1,0},{2,3},{3,2},{4,5},{5,4},{6,7},{7,6},{8,9},{9,8},{10,11... | collective-permute-start | bytes 79880 | tf_op jit(solution)/shard_map/ppermute | solution.py:24

commit v2 on v1

--- a/solution.py
+++ b/solution.py
@@ -1,6 +1,8 @@
 import jax
 import jax.numpy as jnp
 from jax import lax
+from jax.experimental import pallas as pl
+from jax.experimental.pallas import tpu as pltpu
 from jax.sharding import PartitionSpec as P
 
 REACH = 3
@@ -37,7 +39,7 @@
     return alpha, gain, beta * a / curvature
 
 
-def body(
+def general_body(
     magnetogram,
     col_owner,
     col_offset,
@@ -190,6 +192,365 @@
     return solution_field, residual - alpha * first_image - alpha_next * image
 
 
+def high_low(value):
+    high = value.astype(jnp.bfloat16)
+    return high, (value - high.astype(jnp.float32)).astype(jnp.bfloat16)
+
+
+def radial_face(radial_ref, layers, face):
+    if isinstance(face, int):
+        low, high = max(face - 1, 0), min(face, layers - 1)
+    else:
+        low, high = jnp.maximum(face - 1, 0), jnp.minimum(face, layers - 1)
+    return 0.5 * (radial_ref[low] + radial_ref[high])
+
+
+def own_share(phi_ref, per):
+    row = lax.axis_index("row")
+    share = phi_ref[:, pl.ds(pl.multiple_of(row * per, per), per), :]
+    return share.reshape(-1, share.shape[-1])
+
+
+def column_kernel(mag_ref, theta_ref, out_ref):
+    out_ref[...] = jnp.dot(mag_ref[...], theta_ref[...], preferred_element_type=jnp.float32)
+
+
+def pack_kernel(mine_ref, other_ref, owner_ref, offset_ref, phi_ref, field_ref, out_ref, edge_ref):
+    devices = out_ref.shape[0]
+    layers, cells, width = field_ref.shape
+    per = phi_ref.shape[1] // 2
+    count = devices * per
+    here = lax.axis_index("phi")
+    high, low = high_low(mine_ref[...] + other_ref[...])
+    place = offset_ref[...] - lax.axis_index("row") * per
+    target = jnp.where((place >= 0) & (place < per), owner_ref[...] * per + place, -1)
+    slot = lax.broadcasted_iota(jnp.int32, (count, target.shape[1]), 0)
+    chosen = jnp.where(slot == target, 1.0, 0.0).astype(jnp.bfloat16)
+    packed = jnp.dot(
+        chosen, jnp.concatenate([high, low], axis=1), preferred_element_type=jnp.float32
+    ).astype(jnp.bfloat16)
+    high = packed[:, :width].reshape(devices, per, width)
+    low = packed[:, width:].reshape(devices, per, width)
+    out_ref[:, :per] = high
+    out_ref[:, per : 2 * per] = low
+    for to in range(devices):
+        out_ref[to, 2 * per : 3 * per] = high[(to - 1) % devices]
+        out_ref[to, 3 * per : 4 * per] = high[(to + 1) % devices]
+    out_ref[:, 4 * per :] = jnp.zeros((devices, 32, width), jnp.bfloat16)
+    cell = lax.broadcasted_iota(jnp.int32, (8, cells), 1)
+    which = lax.broadcasted_iota(jnp.int32, (8, cells), 0)
+    picked = jnp.where(which < 2, which, cells - 4 + which)
+    picker = jnp.where((cell == picked) & (which < 4), 1.0, 0.0).astype(jnp.bfloat16)
+    weights = lax.dot_general(
+        picker,
+        own_share(phi_ref, per),
+        (((1,), (1,)), ((), ())),
+        preferred_element_type=jnp.float32,
+    )
+    for side in range(2):
+        start = 0 if side else cells - REACH
+        first = 0 if side else 2
+        for layer in range(layers):
+            edge_ref[side, layer * REACH : (layer + 1) * REACH] = field_ref[
+                layer, start : start + REACH
+            ]
+        for part in range(count // width):
+            at = layers * REACH + 2 * part
+            edge_ref[side, at : at + 2] = weights[
+                first : first + 2, part * width : (part + 1) * width
+            ]
+        high, low = high_low(edge_ref[side])
+        to = lax.rem(here + (devices - 1 if side else 1), devices)
+        out_ref[to, 4 * per : 4 * per + 16] = high
+        out_ref[to, 4 * per + 16 :] = low
+
+
+def coef_kernel(radial_ref, theta_ref, phi_ref, weight_ref, inv_ref, lon_ref, lat_ref, share_ref):
+    layers, spread, width = inv_ref.shape
+    cells = share_ref.shape[0]
+    per = weight_ref.shape[1] // 2
+    chunks = phi_ref.shape[0]
+    total = chunks * width
+    share_ref[...] = own_share(weight_ref, per).astype(jnp.float32).T.astype(jnp.bfloat16)
+    row = lax.broadcasted_iota(jnp.int32, (spread, width), 0)
+    lane = lax.broadcasted_iota(jnp.int32, (spread, width), 1)
+    cell = lax.axis_index("phi") * cells + jnp.where(row < cells + 4, row, row - spread)
+    cell = jnp.where(cell < 0, cell + total, jnp.where(cell >= total, cell - total, cell))
+    found = jnp.zeros((spread, width), jnp.float32)
+    for chunk in range(chunks):
+        found = found + jnp.where(lane + chunk * width == cell, phi_ref[chunk : chunk + 1], 0.0)
+    column = jnp.broadcast_to(jnp.sum(found, axis=1, keepdims=True), (spread, width))
+    upper = 0.5 * (column + pltpu.roll(column, spread - 1, 0))
+    lower = pltpu.roll(upper, 1, 0)
+    lon_ref[...] = upper
+    theta = jnp.broadcast_to(theta_ref[...], (8, width))
+    end = lax.broadcasted_iota(jnp.int32, (8, width), 1) == width - 1
+    lat_upper = jnp.where(end, 0.0, 0.5 * (theta + pltpu.roll(theta, width - 1, 1)))
+    lat_ref[...] = lat_upper
+    flat = upper + lower + (lat_upper + pltpu.roll(lat_upper, 1, 1))[:1]
+    for layer in range(layers):
+        low, high = (radial_face(radial_ref, layers, layer + k) for k in range(2))
+        inv_ref[layer] = 1.0 / (flat + (low + high))
+
+
+def boundary_kernel(got_ref, share_ref, out_ref):
+    devices, _, width = got_ref.shape
+    cells, count = share_ref.shape
+    per = count // devices
+    spread = cells + 8
+    layers = (out_ref.shape[0] - spread) // 8
+    here = lax.axis_index("phi")
+    below = lax.rem(here + devices - 1, devices)
+    above = lax.rem(here + 1, devices)
+
+    def rows(which):
+        return got_ref[:, which * per : (which + 1) * per].reshape(count, width)
+
+    own = jnp.dot(
+        share_ref[...],
+        jnp.concatenate([rows(0), rows(1)], axis=1),
+        preferred_element_type=jnp.float32,
+    )
+    out_ref[:cells] = own[:, :width] + own[:, width:]
+    out_ref[cells:] = jnp.zeros((out_ref.shape[0] - cells, width), jnp.float32)
+    for side, source in enumerate((above, below)):
+        high = got_ref[source, 4 * per : 4 * per + 16].astype(jnp.float32)
+        edge = high + got_ref[source, 4 * per + 16 :].astype(jnp.float32)
+        at = layers * REACH
+        weights = jnp.concatenate(
+            [high[at + 2 * k : at + 2 * k + 2] for k in range(count // width)], axis=1
+        )
+        weights = jnp.concatenate([weights, jnp.zeros((6, count), jnp.float32)], axis=0)
+        ghost = jnp.dot(
+            weights.astype(jnp.bfloat16), rows(2 if side else 3), preferred_element_type=jnp.float32
+        )
+        at = spread - 2 if side else cells
+        out_ref[at : at + 2] = ghost[:2]
+        for layer in range(layers):
+            at = spread + layer * 8 + (8 - REACH if side else 0)
+            out_ref[at : at + REACH] = edge[layer * REACH : (layer + 1) * REACH]
+
+
+def krylov_kernel(
+    radial_ref,
+    mine_ref,
+    other_ref,
+    field_ref,
+    far_ref,
+    inv_ref,
+    lon_ref,
+    lat_ref,
+    sums_ref,
+    residual_ref,
+    first_ref,
+    image_ref,
+    second_ref,
+    image2_ref,
+    x_ref,
+    u_ref,
+    v_ref,
+    r_ref,
+    w_ref,
+):
+    layers, cells, width = field_ref.shape
+    every, spread, _ = inv_ref.shape
+    row = lax.axis_index("row")
+    lon, lat = lon_ref[...], lat_ref[:1]
+    nothing = jnp.zeros((spread, width), jnp.float32)
+    for ref in (x_ref, u_ref, v_ref):
+        ref[0] = nothing
+        ref[every + 1] = nothing
+    for ref, edge, base in (
+        (field_ref, mine_ref, row * layers),
+        (far_ref, other_ref, (1 - row) * layers),
+    ):
+        for layer in range(layers):
+            x_ref[base + layer + 1, :cells] = ref[layer]
+            x_ref[base + layer + 1, cells:] = edge[spread + 8 * layer : spread + 8 * layer + 8]
+
+    def operate(ref, start, count):
+        mid = ref[start + 1]
+        below = radial_face(radial_ref, every, start) * (mid - ref[start])
+        for step in range(count):
+            layer = start + step
+            ahead = ref[layer + 2]
+            rise = radial_face(radial_ref, every, layer + 1) * (ahead - mid)
+            along = lon * (mid - pltpu.roll(mid, spread - 1, 0))
+            across = lat * (mid - pltpu.roll(mid, width - 1, 1))
+            yield (
+                layer,
+                step,
+                (below - rise)
+                + (along - pltpu.roll(along, 1, 0))
+                + (across - pltpu.roll(across, 1, 1)),
+            )
+            mid, below = ahead, rise
+
+    inflow = radial_face(radial_ref, every, 0) * (mine_ref[:spread] + other_ref[:spread])
+    for layer, _, value in operate(x_ref, row * (layers - 2), layers + 2):
+        residual = jnp.where(layer == 0, inflow, 0.0) - value
+        r_ref[layer] = residual
+        u_ref[layer + 1] = residual * inv_ref[layer]
+    for layer, _, value in operate(u_ref, row * (layers - 1), layers + 1):
+        w_ref[layer] = value
+        v_ref[layer + 1] = value * inv_ref[layer]
+
+    totals = [jnp.zeros((8, width), jnp.float32)] * 4
+    for layer, step, value in operate(v_ref, row * layers, layers):
+        residual, first = r_ref[layer, :cells], u_ref[layer + 1, :cells]
+        image, second = w_ref[layer, :cells], v_ref[layer + 1, :cells]
+        image2 = value[:cells]
+        residual_ref[step] = residual
+        first_ref[step] = first
+        image_ref[step] = image
+        second_ref[step] = second
+        image2_ref[step] = image2
+        pairs = ((residual, first), (first, image), (image, second), (second, image2))
+        for which, (left, right) in enumerate(pairs):
+            product = left * right
+            for at in range(0, cells, 8):
+                totals[which] = totals[which] + product[at : at + 8]
+    lane = lax.broadcasted_iota(jnp.int32, (8, width), 1)
+    packed = jnp.zeros((8, width), jnp.float32)
+    for which, total in enumerate(totals):
+        packed = jnp.where(lane == which, jnp.sum(total, axis=1, keepdims=True), packed)
+    sums_ref[...] = jnp.broadcast_to(jnp.sum(packed, axis=0, keepdims=True), sums_ref.shape)
+
+
+def update_kernel(
+    sums_ref,
+    field_ref,
+    residual_ref,
+    first_ref,
+    image_ref,
+    second_ref,
+    image2_ref,
+    out_ref,
+    left_ref,
+):
+    totals = jnp.sum(sums_ref[...], axis=0, keepdims=True)
+    lane = lax.broadcasted_iota(jnp.int32, totals.shape, 1)
+    a, b, c, e = (
+        jnp.sum(jnp.where(lane == which, totals, 0.0), axis=1, keepdims=True) for which in range(4)
+    )
+    alpha, gain, alpha_next = step_sizes(a, b, c, e)
+    along, back = alpha + alpha_next * gain, alpha_next * alpha
+    for layer in range(field_ref.shape[0]):
+        out_ref[layer] = field_ref[layer] + (along * first_ref[layer] - back * second_ref[layer])
+        left_ref[layer] = residual_ref[layer] - (along * image_ref[layer] - back * image2_ref[layer])
+
+
+def in_vmem(count):
+    return [pl.BlockSpec(memory_space=pltpu.VMEM)] * count
+
+
+def paired_body(
+    magnetogram,
+    col_owner,
+    col_offset,
+    phi_weight,
+    theta_weight,
+    radial_coef,
+    theta_coef,
+    phi_coef,
+    start_field,
+):
+    layers, cells, width = start_field.shape
+    phi_devices = lax.axis_size("phi")
+    slots = phi_weight.shape[0]
+    capacity = slots // phi_devices
+    per = capacity // 2
+    count = phi_devices * per
+    columns = magnetogram.shape[0]
+    every, spread = 2 * layers, cells + 8
+    real, half = jnp.float32, jnp.bfloat16
+    struct = jax.ShapeDtypeStruct
+    in_smem = [pl.BlockSpec(memory_space=pltpu.SMEM)]
+
+    def swap(value):
+        return lax.ppermute(value, "row", [(0, 1), (1, 0)])
+
+    weights = phi_weight.reshape(phi_devices, capacity, cells)
+    mine = pl.pallas_call(
+        column_kernel,
+        out_shape=struct((columns, width), real),
+        in_specs=in_vmem(2),
+        out_specs=in_vmem(1)[0],
+    )(magnetogram, theta_weight)
+    sent = pl.pallas_call(
+        pack_kernel,
+        out_shape=struct((phi_devices, 4 * per + 32, width), half),
+        in_specs=in_vmem(6),
+        out_specs=in_vmem(1)[0],
+        scratch_shapes=[pltpu.VMEM((2, 16, width), real)],
+    )(
+        mine,
+        swap(mine),
+        col_owner.reshape(1, -1),
+        col_offset.reshape(1, -1),
+        weights,
+        start_field,
+    )
+    sent, radial_coef, theta_coef, phi_coef, field = lax.optimization_barrier(
+        (sent, radial_coef, theta_coef, phi_coef, start_field)
+    )
+    got = lax.all_to_all(sent, "phi", split_axis=0, concat_axis=0, tiled=True)
+    far = swap(field)
+    inv_diag, lon, lat, share = pl.pallas_call(
+        coef_kernel,
+        out_shape=[
+            struct((every, spread, width), real),
+            struct((spread, width), real),
+            struct((8, width), real),
+            struct((cells, count), half),
+        ],
+        in_specs=in_smem + in_vmem(3),
+        out_specs=in_vmem(4),
+    )(radial_coef, theta_coef.reshape(1, width), phi_coef.reshape(-1, width), weights)
+    part = pl.pallas_call(
+        boundary_kernel,
+        out_shape=struct((spread + 8 * layers, width), real),
+        in_specs=in_vmem(2),
+        out_specs=in_vmem(1)[0],
+    )(got, share)
+    block = struct((layers, cells, width), real)
+    lines = pltpu.VMEM((every + 2, spread, width), real)
+    sums, *vectors = pl.pallas_call(
+        krylov_kernel,
+        out_shape=[struct((2 * phi_devices, width), real)] + [block] * 5,
+        in_specs=in_smem + in_vmem(7),
+        out_specs=in_vmem(6),
+        scratch_shapes=[lines] * 5,
+    )(radial_coef, part, swap(part), field, far, inv_diag, lon, lat)
+    sums = lax.all_to_all(sums, ("phi", "row"), split_axis=0, concat_axis=0, tiled=True)
+    return pl.pallas_call(
+        update_kernel,
+        out_shape=[block] * 2,
+        in_specs=in_vmem(7),
+        out_specs=in_vmem(2),
+    )(sums, field, *vectors)
+
+
+def body(*args):
+    phi_weight, phi_coef, start_field = args[3], args[7], args[8]
+    layers, cells, width = start_field.shape
+    phi_devices = lax.axis_size("phi")
+    per = phi_weight.shape[0] // phi_devices // 2
+    edge_rows = layers * REACH + 2 * phi_devices * per // width
+    fits = (
+        lax.axis_size("row") == 2
+        and phi_devices > 2
+        and per % 16 == 0
+        and layers >= 2
+        and cells % 8 == 0
+        and width % 128 == 0
+        and phi_devices * per % width == 0
+        and phi_coef.shape[0] % width == 0
+        and edge_rows <= 16
+    )
+    return (paired_body if fits else general_body)(*args)
+
+
 def solution(mesh):
     in_specs = (
         P("phi", "row"),

time: 65.7 us -> 47.9 us (0.73)
  Pallas kernels: 0 us -> 12 us
  other arithmetic: 7.65 us -> 0 us
  between operations: 6.87 us -> 0.68 us
  waiting for transfers between devices: 18.9 us -> 12.8 us
  starting transfers between devices: 12.6 us -> 8.88 us
  local copies, waits for them, and re-layouts: 5.92 us -> 2.8 us
  blocking collectives: 11.8 us -> 10.3 us
  matrix products: 1.46 us -> 0 us
    pallas_call x0 -> x6, Pallas kernels: none -> 12 us  [the longest x1 2.46 us: paired_body(): pl.pallas_call(krylov_kernel, out_shape=[struct((2 * phi_devices, width),...]
    all_to_all x1, waiting for transfers between devices: 17.8 us -> 11 us  [paired_body(): got = lax.all_to_all(sent, 'phi', split_axis=0, concat_axis=0, tiled=True)]
    ppermute x4 -> x3, starting transfers between devices: 4.92 us -> 0.52 us  [swap(): return lax.ppermute(value, 'row', [(0, 1), (1, 0)])]
    slice x23 -> x0, local copies, waits for them, and re-layouts: 4.21 us -> none  [the longest x1 0.98 us: body(): start_field[:REACH]]
    concatenate x9 -> x0, other arithmetic: 3.29 us -> none  [the longest x1 1.37 us: face_coefs(): radial_lower = jnp.concatenate([radial_coef[:1], radial_mid])]
    mul x6 -> x0, other arithmetic: 2.04 us -> none  [the longest x1 0.7 us: face_coefs(): phi_upper = 0.5 * (phi_coef + jnp.roll(phi_coef, -1))]
    unnamed x21 -> x13, local copies, waits for them, and re-layouts: 0.85 us -> 2.8 us
    all_to_all x1, blocking collectives: 11.8 us -> 10.3 us  [paired_body(): lax.all_to_all(sums, ('phi', 'row'), split_axis=0, concat_axis=0, tiled=T...]
  transfers between devices with their start and end apart: 5 -> 4, of which waited for: 2 -> 3; matrix products, arithmetic and copies ran while one was open for 11% -> 2% of each run, Pallas kernels for 0% -> 8%
where the time goes in v2:
time: 47.9 us; the launch traced here: 47.5 us
  waiting for transfers between devices  12.8 us (27%)
  Pallas kernels  12 us (25%)
  blocking collectives  10.3 us (22%)
  starting transfers between devices  8.88 us (19%)
  local copies, waits for them, and re-layouts  2.8 us (6%)
  between operations  0.68 us (1%)
    all_to_all x1, waiting for transfers between devices, paired_body(): got = lax.all_to_all(sent, 'phi', split_axis=0, concat_axis=0, tiled=True)  11 us
    all_to_all x1, blocking collectives, paired_body(): lax.all_to_all(sums, ('phi', 'row'), split_axis=0, concat_axis=0, tiled=T...  10.3 us
    all_to_all x1, starting transfers between devices, paired_body(): got = lax.all_to_all(sent, 'phi', split_axis=0, concat_axis=0, tiled=True)  8.36 us
    unnamed x13, local copies, waits for them, and re-layouts  2.8 us
    pallas_call x1, Pallas kernels, paired_body(): pl.pallas_call(krylov_kernel, out_shape=[struct((2 * phi_devices, width),...  2.46 us
    pallas_call x1, Pallas kernels, paired_body(): pl.pallas_call(pack_kernel, out_shape=struct((phi_devices, 4 * per + 32,...  2.09 us
    pallas_call x1, Pallas kernels, paired_body(): pl.pallas_call(update_kernel, out_shape=[block] * 2, in_specs=in_vmem(7),...  1.95 us
    ppermute x3, waiting for transfers between devices, swap(): return lax.ppermute(value, 'row', [(0, 1), (1, 0)])  1.86 us
  transfers between devices with their start and end apart: 4, of which 3 were waited for; matrix products, arithmetic and copies ran while one was open for 2% of the time, Pallas kernels for 8%

profile of v2, /device:TPU:0, one launch (start us, length us, event | category | flops | bytes accessed | tf_op | source)
XLA Modules:
  0.0 47.5 jit_solution(8283158772335827698)
XLA Ops:
  0.6 0.0 copy-start.4
  0.6 1.9 %shard_map.104.mine_ref = f32[256,128]{1,0:T(8,128)} custom-call(bf16[256,512]{1,0:T(8,128)(2,1)} %mag_ref.1, bf16[512,128]{1,0:T(8,128)(2,1)} %theta_ref.1), custom_call_target="tpu_custom_call" | custom-call | tf_op jit(solution)/shard_map/pallas_call | solution.py:474
  2.5 0.5 collective-permute-start
  3.0 0.0 copy-done.4
  3.0 0.8 %copy.12 = bf16[512,48]{1,0:T(8,128)(2,1)} copy(bf16[512,48]{0,1:T(8,128)(2,1)S(1)} %copy-done.4) | data formatting | bytes 98304 | tf_op args[3]
  3.7 0.4 collective-permute-done.other_ref
  4.1 0.0 copy-start.2
  4.2 0.6 %copy-done.2 = f32[256,128]{1,0:T(8,128)} copy-done((f32[256,128]{1,0:T(8,128)}, f32[256,128]{1,0:T(8,128)S(1)}, u32[]{:S(2)}) %copy-start.2) | copy-done | bytes 131096
  4.8 2.1 %shard_map.105 = bf16[16,96,128]{2,1,0:T(8,128)(2,1)} custom-call(f32[256,128]{1,0:T(8,128)} %shard_map.104.mine_ref, f32[256,128]{1,0:T(8,128)} %copy-done.2, s32[1,256]{1,0:T(1,128)} %bitcast.14, s32[1,256]{1,0:T(1,128)} %bitcast.15, bf16[16,32,48]{2,1,0:T(8,128)(2,1)} %bitcast.9, f32[4,48,128]{2,1,0:T(8,128)} %field_ref.3), custom_call_target="tpu_custom_call" | custom-call | tf_op jit(solution)/shard_map/pallas_call | solution.py:480
  6.9 0.0 copy-start.1
  6.9 8.4 %all-to-all-start = ((bf16[16,96,128]{2,1,0:T(8,128)(2,1)}), bf16[16,96,128]{2,1,0:T(8,128)(2,1)S(1)}, u32[]{:S(2)}, u32[]{:S(2)}) async-start(bf16[16,96,128]{2,1,0:T(8,128)(2,1)} %shard_map.105), calls=%async_computation | async-start | bytes 786432 | tf_op jit(solution)/shard_map/all_to_all | solution.py:497
  15.3 0.0 copy-done.1
  15.3 0.1 collective-permute-start.2
  15.3 1.8 %shard_map.106 = (f32[8,56,128]{2,1,0:T(8,128)}, f32[56,128]{1,0:T(8,128)}, f32[8,128]{1,0:T(8,128)}, bf16[48,256]{1,0:T(8,128)(2,1)}) custom-call(f32[8]{0:T(128)} %radial_ref.1, f32[1,128]{1,0:T(1,128)} %bitcast.16, f32[6,128]{1,0:T(8,128)} %bitcast.13, bf16[16,32,48]{2,1,0:T(8,128)(2,1)} %bitcast.10), custom_call_target="tpu_custom_call" | custom-call | tf_op jit(solution)/shard_map/pallas_call | solution.py:499
  17.2 11.0 %all-to-all-done.got_ref = bf16[16,96,128]{2,1,0:T(8,128)(2,1)S(1)} async-done(((bf16[16,96,128]{2,1,0:T(8,128)(2,1)}), bf16[16,96,128]{2,1,0:T(8,128)(2,1)S(1)}, u32[]{:S(2)}, u32[]{:S(2)}) %all-to-all-start) | async-done | bytes 393248 | tf_op jit(solution)/shard_map/all_to_all | solution.py:497
  28.2 0.0 copy-start
  28.2 0.8 %copy-done = bf16[16,96,128]{2,1,0:T(8,128)(2,1)} copy-done((bf16[16,96,128]{2,1,0:T(8,128)(2,1)}, bf16[16,96,128]{2,1,0:T(8,128)(2,1)S(1)}, u32[]{:S(2)}) %copy-start) | copy-done | bytes 393240
  28.9 1.8 %shard_map.107.mine_ref = f32[88,128]{1,0:T(8,128)} custom-call(bf16[16,96,128]{2,1,0:T(8,128)(2,1)} %copy-done, bf16[48,256]{1,0:T(8,128)(2,1)} %get-tuple-element.21.share_ref), custom_call_target="tpu_custom_call" | custom-call | tf_op jit(solution)/shard_map/pallas_call | solution.py:510
  30.7 0.0 collective-permute-start.1
  30.7 0.0 collective-permute-done.2.far_ref
  30.7 0.0 copy-start.3
  30.7 1.4 %collective-permute-done.1.other_ref = f32[88,128]{1,0:T(8,128)S(1)} collective-permute-done((f32[88,128]{1,0:T(8,128)}, f32[88,128]{1,0:T(8,128)S(1)}, u32[]{:S(2)}, u32[]{:S(2)}) %collective-permute-start.1) | collective-permute-done | bytes 45088 | tf_op jit(solution)/shard_map/ppermute | solution.py:471
  32.1 0.0 copy-start.5
  32.1 0.0 copy-done.3
  32.1 0.6 %copy-done.5 = f32[88,128]{1,0:T(8,128)} copy-done((f32[88,128]{1,0:T(8,128)}, f32[88,128]{1,0:T(8,128)S(1)}, u32[]{:S(2)}) %copy-start.5) | copy-done | bytes 45080
  32.8 2.5 %shard_map.108 = (f32[32,128]{1,0:T(8,128)}, f32[4,48,128]{2,1,0:T(8,128)}, f32[4,48,128]{2,1,0:T(8,128)}, f32[4,48,128]{2,1,0:T(8,128)}, f32[4,48,128]{2,1,0:T(8,128)}, /*index=5*/f32[4,48,128]{2,1,0:T(8,128)}) custom-call(f32[8]{0:T(128)} %radial_ref.1, f32[88,128]{1,0:T(8,128)} %shard_map.107.mine_ref, f32[88,128]{1,0:T(8,128)} %copy-done.5, ...), custom_call_target="tpu_custom_call" | custom-call | tf_op jit(solution)/shard_map/pallas_call | solution.py:518
  35.2 10.3 %all_to_all.16 = f32[32,1,128]{2,1,0:T(1,128)} all-to-all(f32[32,1,128]{2,1,0:T(1,128)} %bitcast.12), channel_id=1, replica_groups=mesh['phi'=16,'row'=2] {'phi','row'}, dimensions={0} | all-to-all | bytes 32768 | tf_op jit(solution)/shard_map/all_to_all | solution.py:525
  45.6 1.9 %shard_map.109 = (f32[4,48,128]{2,1,0:T(8,128)}, f32[4,48,128]{2,1,0:T(8,128)}) custom-call(f32[32,128]{1,0:T(8,128)} %bitcast.11, f32[4,48,128]{2,1,0:T(8,128)} %field_ref.3, f32[4,48,128]{2,1,0:T(8,128)} %get-tuple-element.27.residual_ref, f32[4,48,128]{2,1,0:T(8,128)} %get-tuple-element.28.first_ref, f32[4,48,128]{2,1,0:T(8,128)} %get-tuple-element.29.image_ref, ...), custom_call_target="tpu_custom_call" | custom-call | tf_op jit(solution)/shard_map/pallas_call | solution.py:526
Async XLA Ops:
  0.6 2.3 %copy-start.4 = (bf16[512,48]{0,1:T(8,128)(2,1)S(1)}, bf16[512,48]{0,1:T(8,128)(2,1)}, u32[]{:S(2)}) copy-start(bf16[512,48]{0,1:T(8,128)(2,1)} %param.12) | copy-start | bytes 147460
  2.5 1.6 %collective-permute-start = (f32[256,128]{1,0:T(8,128)}, f32[256,128]{1,0:T(8,128)S(1)}, u32[]{:S(2)}, u32[]{:S(2)}) collective-permute-start(f32[256,128]{1,0:T(8,128)} %shard_map.104.mine_ref), channel_id=1, source_target_pairs={{0,1},{1,0},{2,3},{3,2},{4,5},{5,4},{6,7},{7,6},{8,9},{9,8},{10,11... | collective-permute-start | bytes 393224 | tf_op jit(solution)/shard_map/ppermute | solution.py:471
  4.1 0.6 %copy-start.2 = (f32[256,128]{1,0:T(8,128)}, f32[256,128]{1,0:T(8,128)S(1)}, u32[]{:S(2)}) copy-start(f32[256,128]{1,0:T(8,128)S(1)} %collective-permute-done.other_ref) | copy-start | bytes 393220
  6.9 8.4 %copy-start.1 = (f32[4,48,128]{2,1,0:T(8,128)S(1)}, f32[4,48,128]{2,1,0:T(8,128)}, u32[]{:S(2)}) copy-start(f32[4,48,128]{2,1,0:T(8,128)} %field_ref.3) | copy-start | bytes 294916
  6.9 21.3 %all-to-all-start = ((bf16[16,96,128]{2,1,0:T(8,128)(2,1)}), bf16[16,96,128]{2,1,0:T(8,128)(2,1)S(1)}, u32[]{:S(2)}, u32[]{:S(2)}) async-start(bf16[16,96,128]{2,1,0:T(8,128)(2,1)} %shard_map.105), calls=%async_computation | async-start | bytes 786432 | tf_op jit(solution)/shard_map/all_to_all | solution.py:497
  15.3 15.4 %collective-permute-start.2 = (f32[4,48,128]{2,1,0:T(8,128)S(1)}, f32[4,48,128]{2,1,0:T(8,128)S(1)}, u32[]{:S(2)}, u32[]{:S(2)}) collective-permute-start(f32[4,48,128]{2,1,0:T(8,128)S(1)} %copy-done.1), channel_id=1, source_target_pairs={{0,1},{1,0},{2,3},{3,2},{4,5},{5,4},{6,7},{7,6},{8,9},{9,8},{10,11... | collective-permute-start | bytes 294920 | tf_op jit(solution)/shard_map/ppermute | solution.py:471
  28.2 0.8 %copy-start = (bf16[16,96,128]{2,1,0:T(8,128)(2,1)}, bf16[16,96,128]{2,1,0:T(8,128)(2,1)S(1)}, u32[]{:S(2)}) copy-start(bf16[16,96,128]{2,1,0:T(8,128)(2,1)S(1)} %all-to-all-done.got_ref) | copy-start | bytes 1179652
  30.7 1.4 %collective-permute-start.1 = (f32[88,128]{1,0:T(8,128)}, f32[88,128]{1,0:T(8,128)S(1)}, u32[]{:S(2)}, u32[]{:S(2)}) collective-permute-start(f32[88,128]{1,0:T(8,128)} %shard_map.107.mine_ref), channel_id=1, source_target_pairs={{0,1},{1,0},{2,3},{3,2},{4,5},{5,4},{6,7},{7,6},{8,9},{9,8},{10,11... | collective-permute-start | bytes 135176 | tf_op jit(solution)/shard_map/ppermute | solution.py:471
  30.7 1.4 %copy-start.3 = (f32[4,48,128]{2,1,0:T(8,128)}, f32[4,48,128]{2,1,0:T(8,128)S(1)}, u32[]{:S(2)}) copy-start(f32[4,48,128]{2,1,0:T(8,128)S(1)} %collective-permute-done.2.far_ref) | copy-start | bytes 294916
  32.1 0.6 %copy-start.5 = (f32[88,128]{1,0:T(8,128)}, f32[88,128]{1,0:T(8,128)S(1)}, u32[]{:S(2)}) copy-start(f32[88,128]{1,0:T(8,128)S(1)} %collective-permute-done.1.other_ref) | copy-start | bytes 135172

commit v3 on v2

--- a/solution.py
+++ b/solution.py
@@ -473,12 +473,14 @@
     weights = phi_weight.reshape(phi_devices, capacity, cells)
     mine = pl.pallas_call(
         column_kernel,
+        compiler_params=pltpu.CompilerParams(vmem_limit_bytes=8 << 20),
         out_shape=struct((columns, width), real),
         in_specs=in_vmem(2),
         out_specs=in_vmem(1)[0],
     )(magnetogram, theta_weight)
     sent = pl.pallas_call(
         pack_kernel,
+        compiler_params=pltpu.CompilerParams(vmem_limit_bytes=8 << 20),
         out_shape=struct((phi_devices, 4 * per + 32, width), half),
         in_specs=in_vmem(6),
         out_specs=in_vmem(1)[0],
@@ -498,6 +500,7 @@
     far = swap(field)
     inv_diag, lon, lat, share = pl.pallas_call(
         coef_kernel,
+        compiler_params=pltpu.CompilerParams(vmem_limit_bytes=8 << 20),
         out_shape=[
             struct((every, spread, width), real),
             struct((spread, width), real),
@@ -509,6 +512,7 @@
     )(radial_coef, theta_coef.reshape(1, width), phi_coef.reshape(-1, width), weights)
     part = pl.pallas_call(
         boundary_kernel,
+        compiler_params=pltpu.CompilerParams(vmem_limit_bytes=8 << 20),
         out_shape=struct((spread + 8 * layers, width), real),
         in_specs=in_vmem(2),
         out_specs=in_vmem(1)[0],
@@ -517,6 +521,7 @@
     lines = pltpu.VMEM((every + 2, spread, width), real)
     sums, *vectors = pl.pallas_call(
         krylov_kernel,
+        compiler_params=pltpu.CompilerParams(vmem_limit_bytes=8 << 20),
         out_shape=[struct((2 * phi_devices, width), real)] + [block] * 5,
         in_specs=in_smem + in_vmem(7),
         out_specs=in_vmem(6),
@@ -525,6 +530,7 @@
     sums = lax.all_to_all(sums, ("phi", "row"), split_axis=0, concat_axis=0, tiled=True)
     return pl.pallas_call(
         update_kernel,
+        compiler_params=pltpu.CompilerParams(vmem_limit_bytes=8 << 20),
         out_shape=[block] * 2,
         in_specs=in_vmem(7),
         out_specs=in_vmem(2),

time: 47.9 us -> 40.6 us (0.85)
  Pallas kernels: 12 us -> 4.08 us
  blocking collectives: 10.3 us -> 9.57 us
  waiting for transfers between devices: 12.8 us -> 13.4 us
  local copies, waits for them, and re-layouts: 2.8 us -> 3.36 us
    pallas_call x6, Pallas kernels: 12 us -> 4.08 us  [the longest x1 1.23 us: paired_body(): pl.pallas_call(krylov_kernel, compiler_params=pltpu.CompilerParams(vmem_l...]
    all_to_all x1, blocking collectives: 10.3 us -> 9.57 us  [paired_body(): lax.all_to_all(sums, ('phi', 'row'), split_axis=0, concat_axis=0, tiled=T...]
    unnamed x13 -> x19, local copies, waits for them, and re-layouts: 2.8 us -> 3.36 us
  transfers between devices with their start and end apart: 4 -> 4, of which waited for: 3 -> 3; matrix products, arithmetic and copies ran while one was open for 2% -> 0% of each run, Pallas kernels for 8% -> 2%
where the time goes in v3:
time: 40.6 us; the launch traced here: 40.2 us
  waiting for transfers between devices  13.4 us (33%)
  blocking collectives  9.57 us (24%)
  starting transfers between devices  9.02 us (22%)
  Pallas kernels  4.08 us (10%)
  local copies, waits for them, and re-layouts  3.36 us (8%)
  between operations  0.74 us (2%)
    all_to_all x1, waiting for transfers between devices, paired_body(): got = lax.all_to_all(sent, 'phi', split_axis=0, concat_axis=0, tiled=True)  11.4 us
    all_to_all x1, blocking collectives, paired_body(): lax.all_to_all(sums, ('phi', 'row'), split_axis=0, concat_axis=0, tiled=T...  9.57 us
    all_to_all x1, starting transfers between devices, paired_body(): got = lax.all_to_all(sent, 'phi', split_axis=0, concat_axis=0, tiled=True)  8.36 us
    unnamed x19, local copies, waits for them, and re-layouts  3.36 us
    ppermute x3, waiting for transfers between devices, swap(): return lax.ppermute(value, 'row', [(0, 1), (1, 0)])  2.01 us
    pallas_call x1, Pallas kernels, paired_body(): pl.pallas_call(krylov_kernel, compiler_params=pltpu.CompilerParams(vmem_l...  1.23 us
    pallas_call x1, Pallas kernels, paired_body(): pl.pallas_call(pack_kernel, compiler_params=pltpu.CompilerParams(vmem_lim...  0.98 us
  transfers between devices with their start and end apart: 4, of which 3 were waited for; matrix products, arithmetic and copies ran while one was open for 0% of the time, Pallas kernels for 2%

profile of v3, /device:TPU:0, one launch (start us, length us, event | category | flops | bytes accessed | tf_op | source)
XLA Modules:
  0.0 40.2 jit_solution(14945955416674435910)
XLA Ops:
  0.6 0.0 copy-start.1
  0.6 0.9 %copy-done.1 = bf16[256,512]{1,0:T(8,128)(2,1)S(1)} copy-done((bf16[256,512]{1,0:T(8,128)(2,1)S(1)}, bf16[256,512]{1,0:T(8,128)(2,1)}, u32[]{:S(2)}) %copy-start.1) | copy-done | bytes 262168
  1.6 0.0 copy-start.2
  1.6 0.9 %copy-done.2 = bf16[512,128]{1,0:T(8,128)(2,1)S(1)} copy-done((bf16[512,128]{1,0:T(8,128)(2,1)S(1)}, bf16[512,128]{1,0:T(8,128)(2,1)}, u32[]{:S(2)}) %copy-start.2) | copy-done | bytes 131096
  2.5 0.0 copy-start.8
  2.5 0.2 shard_map.104.mine_ref
  2.7 0.0 copy-start
  2.7 0.5 %collective-permute-start = (f32[256,128]{1,0:T(8,128)S(1)}, f32[256,128]{1,0:T(8,128)S(1)}, u32[]{:S(2)}, u32[]{:S(2)}) collective-permute-start(f32[256,128]{1,0:T(8,128)S(1)} %shard_map.104.mine_ref), channel_id=1, source_target_pairs={{0,1},{1,0},{2,3},{3,2},{4,5},{5,4},{6,7},{7,6},{8,9},{9,8},{10,11... | collective-permute-start | bytes 393224 | tf_op jit(solution)/shard_map/ppermute | solution.py:471
  3.2 0.1 copy-done.8
  3.3 0.0 copy-start.6
  3.3 0.1 copy.12
  3.4 0.8 %collective-permute-done.other_ref = f32[256,128]{1,0:T(8,128)S(1)} collective-permute-done((f32[256,128]{1,0:T(8,128)S(1)}, f32[256,128]{1,0:T(8,128)S(1)}, u32[]{:S(2)}, u32[]{:S(2)}) %collective-permute-start) | collective-permute-done | bytes 131104 | tf_op jit(solution)/shard_map/ppermute | solution.py:471
  4.2 0.0 copy-start.5
  4.2 0.0 copy-done
  4.2 0.0 copy-done.6
  4.2 0.7 %copy-done.5 = s32[256]{0:T(256)S(1)} copy-done((s32[256]{0:T(256)S(1)}, s32[256]{0:T(256)}, u32[]{:S(2)}) %copy-start.5) | copy-done | bytes 1048
  4.9 1.0 %shard_map.105 = bf16[16,96,128]{2,1,0:T(8,128)(2,1)} custom-call(f32[256,128]{1,0:T(8,128)S(1)} %shard_map.104.mine_ref, f32[256,128]{1,0:T(8,128)S(1)} %collective-permute-done.other_ref, s32[1,256]{1,0:T(1,128)S(1)} %bitcast.14, s32[1,256]{1,0:T(1,128)S(1)} %bitcast.15, bf16[16,32,48]{2,1,0:T(8,128)(2,1)S(1)} %bitcast.9, f32[4,48,128]{2,1,0:T(8,128)S(1)} %copy-done), custom_call_target="tpu_custom_call" | custom-call | tf_op jit(solution)/shard_map/pallas_call | solution.py:481
  5.9 0.0 copy-start.3
  5.9 8.4 %all-to-all-start = ((bf16[16,96,128]{2,1,0:T(8,128)(2,1)}), bf16[16,96,128]{2,1,0:T(8,128)(2,1)S(1)}, u32[]{:S(2)}, u32[]{:S(2)}) async-start(bf16[16,96,128]{2,1,0:T(8,128)(2,1)} %shard_map.105), calls=%async_computation | async-start | bytes 786432 | tf_op jit(solution)/shard_map/all_to_all | solution.py:499
  14.2 0.1 collective-permute-start.2
  14.3 0.0 copy-start.4
  14.3 0.0 copy-start.7
  14.3 0.0 copy-done.3
  14.4 0.6 %copy-done.4 = f32[8]{0:T(128)S(1)} copy-done((f32[8]{0:T(128)S(1)}, f32[8]{0:T(128)}, u32[]{:S(2)}) %copy-start.4) | copy-done | bytes 56
  15.0 0.0 copy-done.7
  15.0 0.7 %shard_map.106 = (f32[8,56,128]{2,1,0:T(8,128)S(1)}, f32[56,128]{1,0:T(8,128)S(1)}, f32[8,128]{1,0:T(8,128)S(1)}, bf16[48,256]{1,0:T(8,128)(2,1)S(1)}) custom-call(f32[8]{0:T(128)S(1)} %copy-done.4, f32[1,128]{1,0:T(1,128)S(1)} %bitcast.16, f32[6,128]{1,0:T(8,128)S(1)} %bitcast.13, bf16[16,32,48]{2,1,0:T(8,128)(2,1)S(1)} %bitcast.10), custom_call_target="tpu_custom_call" | custom-call | tf_op jit(solution)/shard_map/pallas_call | solution.py:501
  15.7 11.4 %all-to-all-done.got_ref = bf16[16,96,128]{2,1,0:T(8,128)(2,1)S(1)} async-done(((bf16[16,96,128]{2,1,0:T(8,128)(2,1)}), bf16[16,96,128]{2,1,0:T(8,128)(2,1)S(1)}, u32[]{:S(2)}, u32[]{:S(2)}) %all-to-all-start) | async-done | bytes 393248 | tf_op jit(solution)/shard_map/all_to_all | solution.py:499
  27.1 0.2 shard_map.107.mine_ref
  27.3 0.1 collective-permute-start.1
  27.4 0.0 collective-permute-done.2.far_ref
  27.4 1.2 %collective-permute-done.1.other_ref = f32[88,128]{1,0:T(8,128)S(1)} collective-permute-done((f32[88,128]{1,0:T(8,128)S(1)}, f32[88,128]{1,0:T(8,128)S(1)}, u32[]{:S(2)}, u32[]{:S(2)}) %collective-permute-start.1) | collective-permute-done | bytes 45088 | tf_op jit(solution)/shard_map/ppermute | solution.py:471
  28.6 1.2 %shard_map.108 = (f32[32,128]{1,0:T(8,128)S(1)}, f32[4,48,128]{2,1,0:T(8,128)S(1)}, f32[4,48,128]{2,1,0:T(8,128)S(1)}, f32[4,48,128]{2,1,0:T(8,128)S(1)}, f32[4,...) custom-call(f32[8]{0:T(128)S(1)} %copy-done.4, f32[88,128]{1,0:T(8,128)S(1)} %shard_map.107.mine_ref, ...), custom_call_target="tpu_custom_call" | custom-call | tf_op jit(solution)/shard_map/pallas_call | solution.py:522
  29.8 9.6 %all_to_all.16 = f32[32,1,128]{2,1,0:T(1,128)S(1)} all-to-all(f32[32,1,128]{2,1,0:T(1,128)S(1)} %bitcast.12), channel_id=1, replica_groups=mesh['phi'=16,'row'=2] {'phi','row'}, dimensions={0} | all-to-all | bytes 32768 | tf_op jit(solution)/shard_map/all_to_all | solution.py:530
  39.4 0.8 %shard_map.109 = (f32[4,48,128]{2,1,0:T(8,128)}, f32[4,48,128]{2,1,0:T(8,128)}) custom-call(f32[32,128]{1,0:T(8,128)S(1)} %bitcast.11, f32[4,48,128]{2,1,0:T(8,128)S(1)} %copy-done, f32[4,48,128]{2,1,0:T(8,128)S(1)} %get-tuple-element.27.residual_ref, f32[4,48,128]{2,1,0:T(8,128)S(1)} %get-tuple-element.28.first_ref, ...), custom_call_target="tpu_custom_call" | custom-call | tf_op jit(solution)/shard_map/pallas_call | solution.py:531
Async XLA Ops:
  0.6 1.0 %copy-start.1 = (bf16[256,512]{1,0:T(8,128)(2,1)S(1)}, bf16[256,512]{1,0:T(8,128)(2,1)}, u32[]{:S(2)}) copy-start(bf16[256,512]{1,0:T(8,128)(2,1)} %mag_ref.1) | copy-start | bytes 786436
  1.6 0.9 %copy-start.2 = (bf16[512,128]{1,0:T(8,128)(2,1)S(1)}, bf16[512,128]{1,0:T(8,128)(2,1)}, u32[]{:S(2)}) copy-start(bf16[512,128]{1,0:T(8,128)(2,1)} %theta_ref.1) | copy-start | bytes 393220
  2.5 0.8 %copy-start.8 = (bf16[512,48]{0,1:T(8,128)(2,1)S(1)}, bf16[512,48]{0,1:T(8,128)(2,1)}, u32[]{:S(2)}) copy-start(bf16[512,48]{0,1:T(8,128)(2,1)} %param.12) | copy-start | bytes 147460
  2.7 1.5 %copy-start = (f32[4,48,128]{2,1,0:T(8,128)S(1)}, f32[4,48,128]{2,1,0:T(8,128)}, u32[]{:S(2)}) copy-start(f32[4,48,128]{2,1,0:T(8,128)} %field_ref.3) | copy-start | bytes 294916
  2.7 1.5 %collective-permute-start = (f32[256,128]{1,0:T(8,128)S(1)}, f32[256,128]{1,0:T(8,128)S(1)}, u32[]{:S(2)}, u32[]{:S(2)}) collective-permute-start(f32[256,128]{1,0:T(8,128)S(1)} %shard_map.104.mine_ref), channel_id=1, source_target_pairs={{0,1},{1,0},{2,3},{3,2},{4,5},{5,4},{6,7},{7,6},{8,9},{9,8},{10,11... | collective-permute-start | bytes 393224 | tf_op jit(solution)/shard_map/ppermute | solution.py:471
  3.3 0.9 %copy-start.6 = (s32[256]{0:T(256)S(1)}, s32[256]{0:T(256)}, u32[]{:S(2)}) copy-start(s32[256]{0:T(256)} %param.11) | copy-start | bytes 3076
  4.2 0.7 %copy-start.5 = (s32[256]{0:T(256)S(1)}, s32[256]{0:T(256)}, u32[]{:S(2)}) copy-start(s32[256]{0:T(256)} %param.10) | copy-start | bytes 3076
  5.9 8.5 %copy-start.3 = (f32[768]{0:T(1024)S(1)}, f32[768]{0:T(1024)}, u32[]{:S(2)}) copy-start(f32[768]{0:T(1024)} %param.16) | copy-start | bytes 9220
  5.9 21.3 %all-to-all-start = ((bf16[16,96,128]{2,1,0:T(8,128)(2,1)}), bf16[16,96,128]{2,1,0:T(8,128)(2,1)S(1)}, u32[]{:S(2)}, u32[]{:S(2)}) async-start(bf16[16,96,128]{2,1,0:T(8,128)(2,1)} %shard_map.105), calls=%async_computation | async-start | bytes 786432 | tf_op jit(solution)/shard_map/all_to_all | solution.py:499
  14.2 13.1 %collective-permute-start.2 = (f32[4,48,128]{2,1,0:T(8,128)S(1)}, f32[4,48,128]{2,1,0:T(8,128)S(1)}, u32[]{:S(2)}, u32[]{:S(2)}) collective-permute-start(f32[4,48,128]{2,1,0:T(8,128)S(1)} %copy-done), channel_id=1, source_target_pairs={{0,1},{1,0},{2,3},{3,2},{4,5},{5,4},{6,7},{7,6},{8,9},{9,8},{10,11... | collective-permute-start | bytes 294920 | tf_op jit(solution)/shard_map/ppermute | solution.py:471
  14.3 0.7 %copy-start.4 = (f32[8]{0:T(128)S(1)}, f32[8]{0:T(128)}, u32[]{:S(2)}) copy-start(f32[8]{0:T(128)} %radial_ref.1) | copy-start | bytes 100
  14.3 0.7 %copy-start.7 = (f32[128]{0:T(128)S(1)}, f32[128]{0:T(128)}, u32[]{:S(2)}) copy-start(f32[128]{0:T(128)} %param.15) | copy-start | bytes 1540
  27.3 1.3 %collective-permute-start.1 = (f32[88,128]{1,0:T(8,128)S(1)}, f32[88,128]{1,0:T(8,128)S(1)}, u32[]{:S(2)}, u32[]{:S(2)}) collective-permute-start(f32[88,128]{1,0:T(8,128)S(1)} %shard_map.107.mine_ref), channel_id=1, source_target_pairs={{0,1},{1,0},{2,3},{3,2},{4,5},{5,4},{6,7},{7,6},{8,9},{9,8},{10,11... | collective-permute-start | bytes 135176 | tf_op jit(solution)/shard_map/ppermute | solution.py:471

commit v4 on v2

--- a/solution.py
+++ b/solution.py
@@ -205,29 +205,54 @@
     return 0.5 * (radial_ref[low] + radial_ref[high])
 
 
-def own_share(phi_ref, per):
-    row = lax.axis_index("row")
-    share = phi_ref[:, pl.ds(pl.multiple_of(row * per, per), per), :]
-    return share.reshape(-1, share.shape[-1])
-
-
-def column_kernel(mag_ref, theta_ref, out_ref):
+def own_share(weights, devices):
+    slots = weights.shape[1]
+    per = slots // devices // 2
+    slot = lax.broadcasted_iota(jnp.int32, (slots, slots // 2), 0)
+    place = lax.broadcasted_iota(jnp.int32, (slots, slots // 2), 1)
+    wanted = place // per * (2 * per) + lax.axis_index("row") * per + place % per
+    picker = jnp.where(slot == wanted, 1.0, 0.0).astype(jnp.bfloat16)
+    return jnp.dot(weights, picker, preferred_element_type=jnp.float32).astype(jnp.bfloat16)
+
+
+def column_kernel(
+    mag_hbm,
+    theta_hbm,
+    owner_hbm,
+    offset_hbm,
+    out_ref,
+    chosen_ref,
+    mag_ref,
+    theta_ref,
+    owner_ref,
+    offset_ref,
+    done,
+):
+    pairs = (
+        (theta_hbm, theta_ref),
+        (mag_hbm, mag_ref),
+        (owner_hbm, owner_ref),
+        (offset_hbm, offset_ref),
+    )
+    copies = [pltpu.make_async_copy(*pair, done.at[at]) for at, pair in enumerate(pairs)]
+    for copy in copies:
+        copy.start()
+    for copy in copies:
+        copy.wait()
     out_ref[...] = jnp.dot(mag_ref[...], theta_ref[...], preferred_element_type=jnp.float32)
-
-
-def pack_kernel(mine_ref, other_ref, owner_ref, offset_ref, phi_ref, field_ref, out_ref, edge_ref):
-    devices = out_ref.shape[0]
-    layers, cells, width = field_ref.shape
-    per = phi_ref.shape[1] // 2
-    count = devices * per
-    here = lax.axis_index("phi")
-    high, low = high_low(mine_ref[...] + other_ref[...])
+    per = chosen_ref.shape[0] // lax.axis_size("phi")
     place = offset_ref[...] - lax.axis_index("row") * per
     target = jnp.where((place >= 0) & (place < per), owner_ref[...] * per + place, -1)
-    slot = lax.broadcasted_iota(jnp.int32, (count, target.shape[1]), 0)
-    chosen = jnp.where(slot == target, 1.0, 0.0).astype(jnp.bfloat16)
+    slot = lax.broadcasted_iota(jnp.int32, chosen_ref.shape, 0)
+    chosen_ref[...] = jnp.where(slot == target, 1.0, 0.0).astype(jnp.bfloat16)
+
+
+def pack_kernel(mine_ref, other_ref, chosen_ref, out_ref):
+    devices, rows, width = out_ref.shape
+    per = rows // 4
+    high, low = high_low(mine_ref[...] + other_ref[...])
     packed = jnp.dot(
-        chosen, jnp.concatenate([high, low], axis=1), preferred_element_type=jnp.float32
+        chosen_ref[...], jnp.concatenate([high, low], axis=1), preferred_element_type=jnp.float32
     ).astype(jnp.bfloat16)
     high = packed[:, :width].reshape(devices, per, width)
     low = packed[:, width:].reshape(devices, per, width)
@@ -236,42 +261,36 @@
     for to in range(devices):
         out_ref[to, 2 * per : 3 * per] = high[(to - 1) % devices]
         out_ref[to, 3 * per : 4 * per] = high[(to + 1) % devices]
-    out_ref[:, 4 * per :] = jnp.zeros((devices, 32, width), jnp.bfloat16)
-    cell = lax.broadcasted_iota(jnp.int32, (8, cells), 1)
-    which = lax.broadcasted_iota(jnp.int32, (8, cells), 0)
-    picked = jnp.where(which < 2, which, cells - 4 + which)
-    picker = jnp.where((cell == picked) & (which < 4), 1.0, 0.0).astype(jnp.bfloat16)
-    weights = lax.dot_general(
-        picker,
-        own_share(phi_ref, per),
-        (((1,), (1,)), ((), ())),
-        preferred_element_type=jnp.float32,
-    )
-    for side in range(2):
-        start = 0 if side else cells - REACH
-        first = 0 if side else 2
-        for layer in range(layers):
-            edge_ref[side, layer * REACH : (layer + 1) * REACH] = field_ref[
-                layer, start : start + REACH
-            ]
-        for part in range(count // width):
-            at = layers * REACH + 2 * part
-            edge_ref[side, at : at + 2] = weights[
-                first : first + 2, part * width : (part + 1) * width
-            ]
-        high, low = high_low(edge_ref[side])
-        to = lax.rem(here + (devices - 1 if side else 1), devices)
-        out_ref[to, 4 * per : 4 * per + 16] = high
-        out_ref[to, 4 * per + 16 :] = low
-
-
-def coef_kernel(radial_ref, theta_ref, phi_ref, weight_ref, inv_ref, lon_ref, lat_ref, share_ref):
+
+
+def is_odd():
+    return lax.rem(lax.axis_index("phi"), 2) == 1
+
+
+def edge_kernel(field_ref, weight_ref, far_ref, near_ref, share_ref):
+    layers, cells, width = field_ref.shape
+    devices = lax.axis_size("phi")
+    share = own_share(weight_ref[...], devices)
+    share_ref[...] = share
+    weights = share.astype(jnp.float32)
+    odd = is_odd()
+
+    def put(at, up, down):
+        far_ref[at : at + up.shape[0]] = jnp.where(odd, up, down)
+        near_ref[at : at + up.shape[0]] = jnp.where(odd, down, up)
+
+    for layer in range(layers):
+        put(layer * REACH, field_ref[layer, cells - REACH :], field_ref[layer, :REACH])
+    for part in range(share.shape[1] // width):
+        piece = weights[:, part * width : (part + 1) * width]
+        put(layers * REACH + 2 * part, piece[cells - 2 :], piece[:2])
+
+
+def coef_kernel(radial_ref, theta_ref, phi_ref, inv_ref, lon_ref, lat_ref):
     layers, spread, width = inv_ref.shape
-    cells = share_ref.shape[0]
-    per = weight_ref.shape[1] // 2
+    cells = spread - 8
     chunks = phi_ref.shape[0]
     total = chunks * width
-    share_ref[...] = own_share(weight_ref, per).astype(jnp.float32).T.astype(jnp.bfloat16)
     row = lax.broadcasted_iota(jnp.int32, (spread, width), 0)
     lane = lax.broadcasted_iota(jnp.int32, (spread, width), 1)
     cell = lax.axis_index("phi") * cells + jnp.where(row < cells + 4, row, row - spread)
@@ -293,42 +312,45 @@
         inv_ref[layer] = 1.0 / (flat + (low + high))
 
 
-def boundary_kernel(got_ref, share_ref, out_ref):
-    devices, _, width = got_ref.shape
+def boundary_kernel(got_ref, share_ref, far_ref, near_ref, out_ref):
+    devices, rows, width = got_ref.shape
     cells, count = share_ref.shape
-    per = count // devices
-    spread = cells + 8
+    per, spread = rows // 4, cells + 8
     layers = (out_ref.shape[0] - spread) // 8
-    here = lax.axis_index("phi")
-    below = lax.rem(here + devices - 1, devices)
-    above = lax.rem(here + 1, devices)
-
-    def rows(which):
-        return got_ref[:, which * per : (which + 1) * per].reshape(count, width)
-
-    own = jnp.dot(
-        share_ref[...],
-        jnp.concatenate([rows(0), rows(1)], axis=1),
-        preferred_element_type=jnp.float32,
-    )
-    out_ref[:cells] = own[:, :width] + own[:, width:]
-    out_ref[cells:] = jnp.zeros((out_ref.shape[0] - cells, width), jnp.float32)
-    for side, source in enumerate((above, below)):
-        high = got_ref[source, 4 * per : 4 * per + 16].astype(jnp.float32)
-        edge = high + got_ref[source, 4 * per + 16 :].astype(jnp.float32)
+    odd = is_odd()
+    above_edge = jnp.where(odd, far_ref[...], near_ref[...])
+    below_edge = jnp.where(odd, near_ref[...], far_ref[...])
+
+    def product(weights, first):
+        data = [
+            got_ref[:, which * per : (which + 1) * per].reshape(count, width)
+            for which in (first, first + 1)
+        ]
+        total = jnp.dot(
+            weights, jnp.concatenate(data, axis=1), preferred_element_type=jnp.float32
+        )
+        return total[:, :width], total[:, width:]
+
+    def edge_weights(edge):
         at = layers * REACH
-        weights = jnp.concatenate(
-            [high[at + 2 * k : at + 2 * k + 2] for k in range(count // width)], axis=1
+        parts = [edge[at + 2 * k : at + 2 * k + 2] for k in range(count // width)]
+        return jnp.concatenate(parts, axis=1)
+
+    high, low = product(share_ref[...], 0)
+    out_ref[:cells] = high + low
+    weights = jnp.concatenate(
+        [edge_weights(above_edge), jnp.zeros((4, count), jnp.float32), edge_weights(below_edge)],
+        axis=0,
+    )
+    below, above = product(weights.astype(jnp.bfloat16), 2)
+    row = lax.broadcasted_iota(jnp.int32, (8, width), 0)
+    out_ref[cells:spread] = jnp.where(row < 4, above, below)
+    for layer in range(layers):
+        at, part = spread + 8 * layer, slice(layer * REACH, (layer + 1) * REACH)
+        out_ref[at : at + 8] = jnp.concatenate(
+            [above_edge[part], jnp.zeros((8 - 2 * REACH, width), jnp.float32), below_edge[part]],
+            axis=0,
         )
-        weights = jnp.concatenate([weights, jnp.zeros((6, count), jnp.float32)], axis=0)
-        ghost = jnp.dot(
-            weights.astype(jnp.bfloat16), rows(2 if side else 3), preferred_element_type=jnp.float32
-        )
-        at = spread - 2 if side else cells
-        out_ref[at : at + 2] = ghost[:2]
-        for layer in range(layers):
-            at = spread + layer * 8 + (8 - REACH if side else 0)
-            out_ref[at : at + REACH] = edge[layer * REACH : (layer + 1) * REACH]
 
 
 def krylov_kernel(
@@ -440,6 +462,9 @@
         left_ref[layer] = residual_ref[layer] - (along * image_ref[layer] - back * image2_ref[layer])
 
 
+SMALL = pltpu.CompilerParams(vmem_limit_bytes=8 << 20)
+
+
 def in_vmem(count):
     return [pl.BlockSpec(memory_space=pltpu.VMEM)] * count
 
@@ -457,9 +482,7 @@
 ):
     layers, cells, width = start_field.shape
     phi_devices = lax.axis_size("phi")
-    slots = phi_weight.shape[0]
-    capacity = slots // phi_devices
-    per = capacity // 2
+    per = phi_weight.shape[0] // phi_devices // 2
     count = phi_devices * per
     columns = magnetogram.shape[0]
     every, spread = 2 * layers, cells + 8
@@ -470,53 +493,79 @@
     def swap(value):
         return lax.ppermute(value, "row", [(0, 1), (1, 0)])
 
-    weights = phi_weight.reshape(phi_devices, capacity, cells)
-    mine = pl.pallas_call(
+    inner = [(i, i ^ 1) for i in range(phi_devices)]
+    outer = [(i, (i + (1 if i % 2 else -1)) % phi_devices) for i in range(phi_devices)]
+
+    def in_hbm(value):
+        return pltpu.with_memory_space_constraint(value, pltpu.HBM)
+
+    mine, chosen = pl.pallas_call(
         column_kernel,
-        out_shape=struct((columns, width), real),
-        in_specs=in_vmem(2),
-        out_specs=in_vmem(1)[0],
-    )(magnetogram, theta_weight)
+        compiler_params=SMALL,
+        out_shape=[struct((columns, width), real), struct((count, columns), half)],
+        in_specs=[pl.BlockSpec(memory_space=pltpu.HBM)] * 4,
+        out_specs=in_vmem(2),
+        scratch_shapes=[
+            pltpu.VMEM(magnetogram.shape, half),
+            pltpu.VMEM(theta_weight.shape, half),
+            pltpu.VMEM((1, columns), jnp.int32),
+            pltpu.VMEM((1, columns), jnp.int32),
+            pltpu.SemaphoreType.DMA((4,)),
+        ],
+    )(
+        in_hbm(magnetogram),
+        in_hbm(theta_weight),
+        in_hbm(col_owner.reshape(1, -1)),
+        in_hbm(col_offset.reshape(1, -1)),
+    )
     sent = pl.pallas_call(
         pack_kernel,
-        out_shape=struct((phi_devices, 4 * per + 32, width), half),
-        in_specs=in_vmem(6),
+        compiler_params=SMALL,
+        out_shape=struct((phi_devices, 4 * per, width), half),
+        in_specs=in_vmem(3),
         out_specs=in_vmem(1)[0],
-        scratch_shapes=[pltpu.VMEM((2, 16, width), real)],
-    )(
-        mine,
-        swap(mine),
-        col_owner.reshape(1, -1),
-        col_offset.reshape(1, -1),
-        weights,
-        start_field,
-    )
-    sent, radial_coef, theta_coef, phi_coef, field = lax.optimization_barrier(
-        (sent, radial_coef, theta_coef, phi_coef, start_field)
+    )(mine, swap(mine), chosen)
+    sent, radial_coef, theta_coef, phi_coef, field, weights = lax.optimization_barrier(
+        (sent, radial_coef, theta_coef, phi_coef, start_field, phi_weight.T)
     )
     got = lax.all_to_all(sent, "phi", split_axis=0, concat_axis=0, tiled=True)
+    edge_rows = layers * REACH + 2 * count // width
+    edge = struct((-(-edge_rows // 8) * 8, width), real)
+    far_edge, near_edge, share = pl.pallas_call(
+        edge_kernel,
+        compiler_params=SMALL,
+        out_shape=[edge, edge, struct((cells, count), half)],
+        in_specs=in_vmem(2),
+        out_specs=in_vmem(3),
+    )(field, weights)
+    far_edge, near_edge = lax.ppermute(far_edge, "phi", outer), lax.ppermute(near_edge, "phi", inner)
     far = swap(field)
-    inv_diag, lon, lat, share = pl.pallas_call(
+    inv_diag, lon, lat = pl.pallas_call(
         coef_kernel,
+        compiler_params=SMALL,
         out_shape=[
             struct((every, spread, width), real),
             struct((spread, width), real),
             struct((8, width), real),
-            struct((cells, count), half),
         ],
-        in_specs=in_smem + in_vmem(3),
-        out_specs=in_vmem(4),
-    )(radial_coef, theta_coef.reshape(1, width), phi_coef.reshape(-1, width), weights)
+        in_specs=in_smem + in_vmem(2),
+        out_specs=in_vmem(3),
+    )(radial_coef, theta_coef.reshape(1, width), phi_coef.reshape(-1, width))
+    got, far_edge, near_edge, far, inv_diag, lon, lat = lax.optimization_barrier(
+        (got, far_edge, near_edge, far, inv_diag, lon, lat)
+    )
     part = pl.pallas_call(
         boundary_kernel,
+        compiler_params=SMALL,
         out_shape=struct((spread + 8 * layers, width), real),
-        in_specs=in_vmem(2),
+        in_specs=in_vmem(4),
         out_specs=in_vmem(1)[0],
-    )(got, share)
+    )(got, share, far_edge, near_edge)
     block = struct((layers, cells, width), real)
     lines = pltpu.VMEM((every + 2, spread, width), real)
     sums, *vectors = pl.pallas_call(
         krylov_kernel,
+        compiler_params=SMALL,
         out_shape=[struct((2 * phi_devices, width), real)] + [block] * 5,
         in_specs=in_smem + in_vmem(7),
         out_specs=in_vmem(6),
@@ -525,6 +574,7 @@
     sums = lax.all_to_all(sums, ("phi", "row"), split_axis=0, concat_axis=0, tiled=True)
     return pl.pallas_call(
         update_kernel,
+        compiler_params=SMALL,
         out_shape=[block] * 2,
         in_specs=in_vmem(7),
         out_specs=in_vmem(2),
@@ -535,18 +585,17 @@
     phi_weight, phi_coef, start_field = args[3], args[7], args[8]
     layers, cells, width = start_field.shape
     phi_devices = lax.axis_size("phi")
-    per = phi_weight.shape[0] // phi_devices // 2
-    edge_rows = layers * REACH + 2 * phi_devices * per // width
     fits = (
         lax.axis_size("row") == 2
         and phi_devices > 2
-        and per % 16 == 0
+        and phi_devices % 2 == 0
+        and phi_weight.shape[0] % (32 * phi_devices) == 0
         and layers >= 2
         and cells % 8 == 0
+        and cells >= 8
         and width % 128 == 0
-        and phi_devices * per % width == 0
         and phi_coef.shape[0] % width == 0
-        and edge_rows <= 16
+        and phi_weight.shape[0] % (2 * width) == 0
     )
     return (paired_body if fits else general_body)(*args)
 

time: 47.9 us -> 36.9 us (0.77)
  waiting for transfers between devices: 12.8 us -> 5.49 us
  Pallas kernels: 12 us -> 5.26 us
  starting transfers between devices: 8.88 us -> 14.6 us
  local copies, waits for them, and re-layouts: 2.8 us -> 0.68 us
    all_to_all x1, waiting for transfers between devices: 11 us -> 0.01 us  [paired_body(): got = lax.all_to_all(sent, 'phi', split_axis=0, concat_axis=0, tiled=True)]
    pallas_call x6 -> x7, Pallas kernels: 12 us -> 5.26 us  [the longest x1 1.29 us: paired_body(): pl.pallas_call(column_kernel, compiler_params=SMALL, out_shape=[struct((c...]
    ppermute x0 -> x2, starting transfers between devices: none -> 5.59 us  [the longest x1 5.59 us: paired_body(): lax.ppermute(far_edge, 'phi', outer)]
    ppermute x0 -> x2, waiting for transfers between devices: none -> 3.29 us  [the longest x1 3.29 us: paired_body(): lax.ppermute(far_edge, 'phi', outer)]
    unnamed x13 -> x10, local copies, waits for them, and re-layouts: 2.8 us -> 0.68 us
  transfers between devices with their start and end apart: 4 -> 6, of which waited for: 3 -> 3; matrix products, arithmetic and copies ran while one was open for 2% -> 0% of each run, Pallas kernels for 8% -> 2%
where the time goes in v4:
time: 36.9 us; the launch traced here: 36.6 us
  starting transfers between devices  14.6 us (40%)
  blocking collectives  9.88 us (27%)
  waiting for transfers between devices  5.49 us (15%)
  Pallas kernels  5.26 us (14%)
  between operations  0.72 us (2%)
  local copies, waits for them, and re-layouts  0.68 us (2%)
    all_to_all x1, blocking collectives, paired_body(): lax.all_to_all(sums, ('phi', 'row'), split_axis=0, concat_axis=0, tiled=T...  9.88 us
    all_to_all x1, starting transfers between devices, paired_body(): got = lax.all_to_all(sent, 'phi', split_axis=0, concat_axis=0, tiled=True)  8.35 us
    ppermute x1, starting transfers between devices, paired_body(): lax.ppermute(far_edge, 'phi', outer)  5.59 us
    ppermute x1, waiting for transfers between devices, paired_body(): lax.ppermute(far_edge, 'phi', outer)  3.29 us
    ppermute x3, waiting for transfers between devices, swap(): return lax.ppermute(value, 'row', [(0, 1), (1, 0)])  2.2 us
    pallas_call x1, Pallas kernels, paired_body(): pl.pallas_call(column_kernel, compiler_params=SMALL, out_shape=[struct((c...  1.29 us
    pallas_call x1, Pallas kernels, paired_body(): pl.pallas_call(krylov_kernel, compiler_params=SMALL, out_shape=[struct((2...  1.23 us
    pallas_call x1, Pallas kernels, paired_body(): pl.pallas_call(pack_kernel, compiler_params=SMALL, out_shape=struct((phi_...  0.9 us
  transfers between devices with their start and end apart: 6, of which 3 were waited for; matrix products, arithmetic and copies ran while one was open for 0% of the time, Pallas kernels for 2%

profile of v4, /device:TPU:0, one launch (start us, length us, event | category | flops | bytes accessed | tf_op | source)
XLA Modules:
  0.0 36.6 jit_solution(17199866886222033459)
XLA Ops:
  0.6 1.3 %shard_map.104 = (f32[256,128]{1,0:T(8,128)S(1)}, bf16[256,256]{1,0:T(8,128)(2,1)S(1)}) custom-call(bf16[256,512]{1,0:T(8,128)(2,1)} %mag_hbm.1, bf16[512,128]{1,0:T(8,128)(2,1)} %theta_hbm.1, s32[1,256]{1,0:T(1,128)} %bitcast.14, s32[1,256]{1,0:T(1,128)} %bitcast.15), custom_call_target="tpu_custom_call" | custom-call | tf_op jit(solution)/shard_map/pallas_call | solution.py:502
  1.9 0.5 %collective-permute-start = (f32[256,128]{1,0:T(8,128)S(1)}, f32[256,128]{1,0:T(8,128)S(1)}, u32[]{:S(2)}, u32[]{:S(2)}) collective-permute-start(f32[256,128]{1,0:T(8,128)S(1)} %get-tuple-element.29.mine_ref), channel_id=1, source_target_pairs={{0,1},{1,0},{2,3},{3,2},{4,5},{5,4},{6,7},{7,6},{8,9},{9,8},{10,11... | collective-permute-start | bytes 393224 | tf_op jit(solution)/shard_map/ppermute | solution.py:494
  2.4 1.0 %collective-permute-done.other_ref = f32[256,128]{1,0:T(8,128)S(1)} collective-permute-done((f32[256,128]{1,0:T(8,128)S(1)}, f32[256,128]{1,0:T(8,128)S(1)}, u32[]{:S(2)}, u32[]{:S(2)}) %collective-permute-start) | collective-permute-done | bytes 131104 | tf_op jit(solution)/shard_map/ppermute | solution.py:494
  3.4 0.9 %shard_map.105 = bf16[16,64,128]{2,1,0:T(8,128)(2,1)} custom-call(f32[256,128]{1,0:T(8,128)S(1)} %get-tuple-element.29.mine_ref, f32[256,128]{1,0:T(8,128)S(1)} %collective-permute-done.other_ref, bf16[256,256]{1,0:T(8,128)(2,1)S(1)} %get-tuple-element.30.chosen_ref), custom_call_target="tpu_custom_call" | custom-call | tf_op jit(solution)/shard_map/pallas_call | solution.py:521
  4.3 0.0 copy-start
  4.3 0.0 copy-start.1
  4.3 8.4 %all-to-all-start = ((bf16[16,64,128]{2,1,0:T(8,128)(2,1)}), bf16[16,64,128]{2,1,0:T(8,128)(2,1)S(1)}, u32[]{:S(2)}, u32[]{:S(2)}) async-start(bf16[16,64,128]{2,1,0:T(8,128)(2,1)} %shard_map.105), calls=%async_computation | async-start | bytes 524288 | tf_op jit(solution)/shard_map/all_to_all | solution.py:531
  12.7 0.0 copy-done
  12.7 0.1 collective-permute-start.3
  12.8 0.0 copy-done.1
  12.8 0.2 shard_map.106
  13.0 0.0 copy-start.2
  13.0 5.6 %collective-permute-start.1 = (f32[16,128]{1,0:T(8,128)S(1)}, f32[16,128]{1,0:T(8,128)S(1)}, u32[]{:S(2)}, u32[]{:S(2)}) collective-permute-start(f32[16,128]{1,0:T(8,128)S(1)} %get-tuple-element.35), channel_id=1, source_target_pairs={{0,30},{2,4},{4,2},{6,8},{8,6},{10,12},{12,10},{14,16},{16,14},{18... | collective-permute-start | bytes 24584 | tf_op jit(solution)/shard_map/ppermute | solution.py:541
  18.6 0.0 collective-permute-start.2
  18.6 0.0 copy-start.3
  18.6 0.0 copy-start.4
  18.6 0.0 copy-done.2
  18.6 0.6 %copy-done.3 = f32[8]{0:T(128)S(1)} copy-done((f32[8]{0:T(128)S(1)}, f32[8]{0:T(128)}, u32[]{:S(2)}) %copy-start.3) | copy-done | bytes 56
  19.2 0.0 copy-done.4
  19.3 0.7 %shard_map.107 = (f32[8,56,128]{2,1,0:T(8,128)S(1)}, f32[56,128]{1,0:T(8,128)S(1)}, f32[8,128]{1,0:T(8,128)S(1)}) custom-call(f32[8]{0:T(128)S(1)} %copy-done.3, f32[1,128]{1,0:T(1,128)S(1)} %bitcast.13, f32[6,128]{1,0:T(8,128)S(1)} %bitcast.12), custom_call_target="tpu_custom_call" | custom-call | tf_op jit(solution)/shard_map/pallas_call | solution.py:543
  20.0 3.3 %collective-permute-done.1.far_ref = f32[16,128]{1,0:T(8,128)S(1)} collective-permute-done((f32[16,128]{1,0:T(8,128)S(1)}, f32[16,128]{1,0:T(8,128)S(1)}, u32[]{:S(2)}, u32[]{:S(2)}) %collective-permute-start.1) | collective-permute-done | bytes 8224 | tf_op jit(solution)/shard_map/ppermute | solution.py:541
  23.3 0.0 collective-permute-done.2.near_ref
  23.3 0.0 collective-permute-done.3.far_ref
  23.3 0.0 all-to-all-done.got_ref
  23.3 0.2 shard_map.108.mine_ref
  23.4 0.1 collective-permute-start.4
  23.5 1.2 %collective-permute-done.4.other_ref = f32[88,128]{1,0:T(8,128)S(1)} collective-permute-done((f32[88,128]{1,0:T(8,128)S(1)}, f32[88,128]{1,0:T(8,128)S(1)}, u32[]{:S(2)}, u32[]{:S(2)}) %collective-permute-start.4) | collective-permute-done | bytes 45088 | tf_op jit(solution)/shard_map/ppermute | solution.py:494
  24.7 1.2 %shard_map.109 = (f32[32,128]{1,0:T(8,128)S(1)}, f32[4,48,128]{2,1,0:T(8,128)S(1)}, f32[4,48,128]{2,1,0:T(8,128)S(1)}, f32[4,48,128]{2,1,0:T(8,128)S(1)}, f32[4,...) custom-call(f32[8]{0:T(128)S(1)} %copy-done.3, f32[88,128]{1,0:T(8,128)S(1)} %shard_map.108.mine_ref, ...), custom_call_target="tpu_custom_call" | custom-call | tf_op jit(solution)/shard_map/pallas_call | solution.py:566
  25.9 9.9 %all_to_all.16 = f32[32,1,128]{2,1,0:T(1,128)S(1)} all-to-all(f32[32,1,128]{2,1,0:T(1,128)S(1)} %bitcast.11), channel_id=1, replica_groups=mesh['phi'=16,'row'=2] {'phi','row'}, dimensions={0} | all-to-all | bytes 32768 | tf_op jit(solution)/shard_map/all_to_all | solution.py:574
  35.8 0.8 %shard_map.110 = (f32[4,48,128]{2,1,0:T(8,128)}, f32[4,48,128]{2,1,0:T(8,128)}) custom-call(f32[32,128]{1,0:T(8,128)S(1)} %bitcast.9, f32[4,48,128]{2,1,0:T(8,128)S(1)} %copy-done, f32[4,48,128]{2,1,0:T(8,128)S(1)} %get-tuple-element.51.residual_ref, f32[4,48,128]{2,1,0:T(8,128)S(1)} %get-tuple-element.52.first_ref, ...), custom_call_target="tpu_custom_call" | custom-call | tf_op jit(solution)/shard_map/pallas_call | solution.py:575
Async XLA Ops:
  1.9 1.5 %collective-permute-start = (f32[256,128]{1,0:T(8,128)S(1)}, f32[256,128]{1,0:T(8,128)S(1)}, u32[]{:S(2)}, u32[]{:S(2)}) collective-permute-start(f32[256,128]{1,0:T(8,128)S(1)} %get-tuple-element.29.mine_ref), channel_id=1, source_target_pairs={{0,1},{1,0},{2,3},{3,2},{4,5},{5,4},{6,7},{7,6},{8,9},{9,8},{10,11... | collective-permute-start | bytes 393224 | tf_op jit(solution)/shard_map/ppermute | solution.py:494
  4.3 8.4 %copy-start = (f32[4,48,128]{2,1,0:T(8,128)S(1)}, f32[4,48,128]{2,1,0:T(8,128)}, u32[]{:S(2)}) copy-start(f32[4,48,128]{2,1,0:T(8,128)} %field_ref.2) | copy-start | bytes 294916
  4.3 8.5 %copy-start.1 = (bf16[512,48]{0,1:T(8,128)(2,1)S(1)}, bf16[512,48]{0,1:T(8,128)(2,1)}, u32[]{:S(2)}) copy-start(bf16[512,48]{0,1:T(8,128)(2,1)} %param.12) | copy-start | bytes 147460
  4.3 18.9 %all-to-all-start = ((bf16[16,64,128]{2,1,0:T(8,128)(2,1)}), bf16[16,64,128]{2,1,0:T(8,128)(2,1)S(1)}, u32[]{:S(2)}, u32[]{:S(2)}) async-start(bf16[16,64,128]{2,1,0:T(8,128)(2,1)} %shard_map.105), calls=%async_computation | async-start | bytes 524288 | tf_op jit(solution)/shard_map/all_to_all | solution.py:531
  12.7 10.6 %collective-permute-start.3 = (f32[4,48,128]{2,1,0:T(8,128)S(1)}, f32[4,48,128]{2,1,0:T(8,128)S(1)}, u32[]{:S(2)}, u32[]{:S(2)}) collective-permute-start(f32[4,48,128]{2,1,0:T(8,128)S(1)} %copy-done), channel_id=1, source_target_pairs={{0,1},{1,0},{2,3},{3,2},{4,5},{5,4},{6,7},{7,6},{8,9},{9,8},{10,11... | collective-permute-start | bytes 294920 | tf_op jit(solution)/shard_map/ppermute | solution.py:494
  13.0 5.6 %copy-start.2 = (f32[768]{0:T(1024)S(1)}, f32[768]{0:T(1024)}, u32[]{:S(2)}) copy-start(f32[768]{0:T(1024)} %param.16) | copy-start | bytes 9220
  13.0 10.3 %collective-permute-start.1 = (f32[16,128]{1,0:T(8,128)S(1)}, f32[16,128]{1,0:T(8,128)S(1)}, u32[]{:S(2)}, u32[]{:S(2)}) collective-permute-start(f32[16,128]{1,0:T(8,128)S(1)} %get-tuple-element.35), channel_id=1, source_target_pairs={{0,30},{2,4},{4,2},{6,8},{8,6},{10,12},{12,10},{14,16},{16,14},{18... | collective-permute-start | bytes 24584 | tf_op jit(solution)/shard_map/ppermute | solution.py:541
  18.6 4.7 %collective-permute-start.2 = (f32[16,128]{1,0:T(8,128)S(1)}, f32[16,128]{1,0:T(8,128)S(1)}, u32[]{:S(2)}, u32[]{:S(2)}) collective-permute-start(f32[16,128]{1,0:T(8,128)S(1)} %get-tuple-element.36), channel_id=1, source_target_pairs={{0,2},{2,0},{4,6},{6,4},{8,10},{10,8},{12,14},{14,12},{16,18},{18,... | collective-permute-start | bytes 24584 | tf_op jit(solution)/shard_map/ppermute | solution.py:541
  18.6 0.7 %copy-start.3 = (f32[8]{0:T(128)S(1)}, f32[8]{0:T(128)}, u32[]{:S(2)}) copy-start(f32[8]{0:T(128)} %radial_ref.1) | copy-start | bytes 100
  18.6 0.7 %copy-start.4 = (f32[128]{0:T(128)S(1)}, f32[128]{0:T(128)}, u32[]{:S(2)}) copy-start(f32[128]{0:T(128)} %param.15) | copy-start | bytes 1540
  23.4 1.3 %collective-permute-start.4 = (f32[88,128]{1,0:T(8,128)S(1)}, f32[88,128]{1,0:T(8,128)S(1)}, u32[]{:S(2)}, u32[]{:S(2)}) collective-permute-start(f32[88,128]{1,0:T(8,128)S(1)} %shard_map.108.mine_ref), channel_id=1, source_target_pairs={{0,1},{1,0},{2,3},{3,2},{4,5},{5,4},{6,7},{7,6},{8,9},{9,8},{10,11... | collective-permute-start | bytes 135176 | tf_op jit(solution)/shard_map/ppermute | solution.py:494

commit v5 on v4

--- a/solution.py
+++ b/solution.py
@@ -197,24 +197,6 @@
     return high, (value - high.astype(jnp.float32)).astype(jnp.bfloat16)
 
 
-def radial_face(radial_ref, layers, face):
-    if isinstance(face, int):
-        low, high = max(face - 1, 0), min(face, layers - 1)
-    else:
-        low, high = jnp.maximum(face - 1, 0), jnp.minimum(face, layers - 1)
-    return 0.5 * (radial_ref[low] + radial_ref[high])
-
-
-def own_share(weights, devices):
-    slots = weights.shape[1]
-    per = slots // devices // 2
-    slot = lax.broadcasted_iota(jnp.int32, (slots, slots // 2), 0)
-    place = lax.broadcasted_iota(jnp.int32, (slots, slots // 2), 1)
-    wanted = place // per * (2 * per) + lax.axis_index("row") * per + place % per
-    picker = jnp.where(slot == wanted, 1.0, 0.0).astype(jnp.bfloat16)
-    return jnp.dot(weights, picker, preferred_element_type=jnp.float32).astype(jnp.bfloat16)
-
-
 def column_kernel(
     mag_hbm,
     theta_hbm,
@@ -248,45 +230,58 @@
 
 
 def pack_kernel(mine_ref, other_ref, chosen_ref, out_ref):
-    devices, rows, width = out_ref.shape
-    per = rows // 4
+    targets, rows, width = out_ref.shape
+    devices, per = targets // 2, rows // 2
     high, low = high_low(mine_ref[...] + other_ref[...])
     packed = jnp.dot(
         chosen_ref[...], jnp.concatenate([high, low], axis=1), preferred_element_type=jnp.float32
     ).astype(jnp.bfloat16)
     high = packed[:, :width].reshape(devices, per, width)
     low = packed[:, width:].reshape(devices, per, width)
-    out_ref[:, :per] = high
-    out_ref[:, per : 2 * per] = low
     for to in range(devices):
-        out_ref[to, 2 * per : 3 * per] = high[(to - 1) % devices]
-        out_ref[to, 3 * per : 4 * per] = high[(to + 1) % devices]
+        out_ref[2 * to, :per] = high[to]
+        out_ref[2 * to, per:] = low[to]
+        out_ref[2 * to + 1, :per] = high[(to - 1) % devices]
+        out_ref[2 * to + 1, per:] = high[(to + 1) % devices]
 
 
 def is_odd():
     return lax.rem(lax.axis_index("phi"), 2) == 1
 
 
-def edge_kernel(field_ref, weight_ref, far_ref, near_ref, share_ref):
+def edge_kernel(field_ref, other_ref, weight_ref, far_ref, near_ref):
     layers, cells, width = field_ref.shape
-    devices = lax.axis_size("phi")
-    share = own_share(weight_ref[...], devices)
-    share_ref[...] = share
-    weights = share.astype(jnp.float32)
+    slots = weight_ref.shape[1]
     odd = is_odd()
+    first = lax.axis_index("row") == 0
 
     def put(at, up, down):
         far_ref[at : at + up.shape[0]] = jnp.where(odd, up, down)
         near_ref[at : at + up.shape[0]] = jnp.where(odd, down, up)
 
     for layer in range(layers):
-        put(layer * REACH, field_ref[layer, cells - REACH :], field_ref[layer, :REACH])
-    for part in range(share.shape[1] // width):
-        piece = weights[:, part * width : (part + 1) * width]
-        put(layers * REACH + 2 * part, piece[cells - 2 :], piece[:2])
-
-
-def coef_kernel(radial_ref, theta_ref, phi_ref, inv_ref, lon_ref, lat_ref):
+        up = [ref[layer, cells - REACH :] for ref in (field_ref, other_ref)]
+        down = [ref[layer, :REACH] for ref in (field_ref, other_ref)]
+        put(layer * REACH, jnp.where(first, *up), jnp.where(first, *down))
+        put((layers + layer) * REACH, jnp.where(first, *up[::-1]), jnp.where(first, *down[::-1]))
+    up = weight_ref[cells - 16 :].astype(jnp.float32)[14:]
+    down = weight_ref[:16].astype(jnp.float32)[:2]
+    for part in range(slots // width):
+        piece = slice(part * width, (part + 1) * width)
+        put(2 * layers * REACH + 2 * part, up[:, piece], down[:, piece])
+
+
+def sides(far_ref, near_ref):
+    odd = is_odd()
+    return (
+        jnp.where(odd, far_ref[...], near_ref[...]),
+        jnp.where(odd, near_ref[...], far_ref[...]),
+    )
+
+
+def coef_kernel(
+    radial_ref, theta_ref, phi_ref, diag_ref, inv_ref, lon_ref, lat_ref, face_ref
+):
     layers, spread, width = inv_ref.shape
     cells = spread - 8
     chunks = phi_ref.shape[0]
@@ -299,144 +294,198 @@
     for chunk in range(chunks):
         found = found + jnp.where(lane + chunk * width == cell, phi_ref[chunk : chunk + 1], 0.0)
     column = jnp.broadcast_to(jnp.sum(found, axis=1, keepdims=True), (spread, width))
-    upper = 0.5 * (column + pltpu.roll(column, spread - 1, 0))
-    lower = pltpu.roll(upper, 1, 0)
-    lon_ref[...] = upper
+    lon_ref[0] = 0.5 * (column + pltpu.roll(column, spread - 1, 0))
+    lon_ref[1] = 0.5 * (column + pltpu.roll(column, 1, 0))
     theta = jnp.broadcast_to(theta_ref[...], (8, width))
-    end = lax.broadcasted_iota(jnp.int32, (8, width), 1) == width - 1
-    lat_upper = jnp.where(end, 0.0, 0.5 * (theta + pltpu.roll(theta, width - 1, 1)))
-    lat_ref[...] = lat_upper
-    flat = upper + lower + (lat_upper + pltpu.roll(lat_upper, 1, 1))[:1]
+    ends = lax.broadcasted_iota(jnp.int32, (8, width), 1)
+    upper = jnp.where(ends == width - 1, 0.0, 0.5 * (theta + pltpu.roll(theta, width - 1, 1)))
+    lower = jnp.where(ends == 0, 0.0, 0.5 * (theta + pltpu.roll(theta, 1, 1)))
+    lat_ref[0], lat_ref[1] = upper, lower
+    flat = lon_ref[0] + lon_ref[1] + (upper + lower)[:1]
+    faces = [
+        0.5 * (radial_ref[max(face - 1, 0)] + radial_ref[min(face, layers - 1)])
+        for face in range(layers + 1)
+    ]
+    for face in range(layers + 1):
+        face_ref[face : face + 1] = jnp.full((1, width), faces[face], jnp.float32)
     for layer in range(layers):
-        low, high = (radial_face(radial_ref, layers, layer + k) for k in range(2))
-        inv_ref[layer] = 1.0 / (flat + (low + high))
-
-
-def boundary_kernel(got_ref, share_ref, far_ref, near_ref, out_ref):
-    devices, rows, width = got_ref.shape
-    cells, count = share_ref.shape
-    per, spread = rows // 4, cells + 8
-    layers = (out_ref.shape[0] - spread) // 8
-    odd = is_odd()
-    above_edge = jnp.where(odd, far_ref[...], near_ref[...])
-    below_edge = jnp.where(odd, near_ref[...], far_ref[...])
-
-    def product(weights, first):
-        data = [
-            got_ref[:, which * per : (which + 1) * per].reshape(count, width)
-            for which in (first, first + 1)
-        ]
+        diag = flat + (faces[layer] + faces[layer + 1])
+        diag_ref[layer] = diag
+        inv_ref[layer] = 1.0 / diag
+
+
+def boundary_kernel(got_ref, weight_ref, far_ref, near_ref, own_ref, beyond_ref):
+    sources, rows, width = got_ref.shape
+    cells, slots = weight_ref.shape
+    per = rows // 2
+
+    def product(weights):
+        data = [got_ref[:, :per].reshape(slots, width), got_ref[:, per:].reshape(slots, width)]
         total = jnp.dot(
             weights, jnp.concatenate(data, axis=1), preferred_element_type=jnp.float32
         )
         return total[:, :width], total[:, width:]
 
-    def edge_weights(edge):
-        at = layers * REACH
-        parts = [edge[at + 2 * k : at + 2 * k + 2] for k in range(count // width)]
-        return jnp.concatenate(parts, axis=1)
-
-    high, low = product(share_ref[...], 0)
-    out_ref[:cells] = high + low
-    weights = jnp.concatenate(
-        [edge_weights(above_edge), jnp.zeros((4, count), jnp.float32), edge_weights(below_edge)],
-        axis=0,
-    )
-    below, above = product(weights.astype(jnp.bfloat16), 2)
-    row = lax.broadcasted_iota(jnp.int32, (8, width), 0)
-    out_ref[cells:spread] = jnp.where(row < 4, above, below)
-    for layer in range(layers):
-        at, part = spread + 8 * layer, slice(layer * REACH, (layer + 1) * REACH)
-        out_ref[at : at + 8] = jnp.concatenate(
-            [above_edge[part], jnp.zeros((8 - 2 * REACH, width), jnp.float32), below_edge[part]],
-            axis=0,
+    @pl.when(lax.axis_index("row") == 0)
+    def _():
+        high, low = product(weight_ref[...])
+        own_ref[...] = high + low
+        beyond_ref[...] = jnp.zeros(beyond_ref.shape, jnp.float32)
+
+    @pl.when(lax.axis_index("row") == 1)
+    def _():
+        above, below = sides(far_ref, near_ref)
+
+        def edge_weights(edge):
+            at = edge.shape[0] - 2 * slots // width
+            parts = [edge[at + 2 * k : at + 2 * k + 2] for k in range(slots // width)]
+            return jnp.concatenate(parts, axis=1)
+
+        weights = jnp.concatenate(
+            [edge_weights(above), jnp.zeros((4, slots), jnp.float32), edge_weights(below)], axis=0
         )
+        from_below, from_above = product(weights.astype(jnp.bfloat16))
+        row = lax.broadcasted_iota(jnp.int32, (8, width), 0)
+        own_ref[...] = jnp.zeros(own_ref.shape, jnp.float32)
+        beyond_ref[...] = jnp.where(row < 4, from_above, from_below)
+
+
+def neighbours(values, layer, faces, lon, lat):
+    mid = values[layer]
+    spread, width = mid.shape
+    total = lat[0] * pltpu.roll(mid, width - 1, 1) + lat[1] * pltpu.roll(mid, 1, 1)
+    total = total + lon[0] * pltpu.roll(mid, spread - 1, 0)
+    total = total + lon[1] * pltpu.roll(mid, 1, 0)
+    for at, face in ((layer - 1, layer), (layer + 1, layer + 1)):
+        if at in values:
+            total = total + faces[face] * values[at]
+    return total
 
 
 def krylov_kernel(
-    radial_ref,
-    mine_ref,
+    face_ref,
+    own_ref,
+    field_ref,
     other_ref,
-    field_ref,
     far_ref,
+    near_ref,
+    diag_ref,
     inv_ref,
     lon_ref,
     lat_ref,
-    sums_ref,
-    residual_ref,
+    totals_ref,
+    *vector_refs,
+):
+    layers, cells, width = field_ref.shape
+    every, spread, _ = inv_ref.shape
+    above, below = sides(far_ref, near_ref)
+    gap = jnp.zeros((8 - 2 * REACH, width), jnp.float32)
+
+    def work(row):
+        faces = [face_ref[face : face + 1] for face in range(every + 1)]
+        lon, lat = (lon_ref[0], lon_ref[1]), (lat_ref[0, :1], lat_ref[1, :1])
+        halves = (other_ref, field_ref) if row else (field_ref, other_ref)
+        field = {}
+        for layer in range(every):
+            part = slice(layer * REACH, (layer + 1) * REACH)
+            block = halves[layer // layers][layer % layers]
+            field[layer] = jnp.concatenate([block, above[part], gap, below[part]], axis=0)
+        residual, first, image, second = {}, {}, {}, {}
+        start = row * (layers - 2)
+        for layer in range(start, start + layers + 2):
+            value = neighbours(field, layer, faces, lon, lat) - diag_ref[layer] * field[layer]
+            if layer == 0:
+                source = jnp.concatenate([own_ref[...], jnp.zeros((8, width), jnp.float32)], axis=0)
+                value = value + faces[0] * source
+            residual[layer] = value
+            first[layer] = value * inv_ref[layer]
+        start = row * (layers - 1)
+        for layer in range(start, start + layers + 1):
+            image[layer] = residual[layer] - neighbours(first, layer, faces, lon, lat)
+            second[layer] = image[layer] * inv_ref[layer]
+        totals = [jnp.zeros((8, width), jnp.float32)] * 4
+        for at in range(layers):
+            layer = row * layers + at
+            image2 = image[layer] - neighbours(second, layer, faces, lon, lat)
+            vectors = (residual[layer], first[layer], image[layer], second[layer], image2)
+            vectors = [vector[:cells] for vector in vectors]
+            for ref, vector in zip(vector_refs, vectors):
+                ref[at] = vector
+            for which in range(4):
+                product = vectors[which] * vectors[which + 1]
+                for begin in range(0, cells, 8):
+                    later = row == 0 and at < REACH and which and begin in (0, cells - 8)
+                    if not later:
+                        totals[which] = totals[which] + product[begin : begin + 8]
+        for which in range(4):
+            totals_ref[which] = totals[which]
+
+    for row in range(2):
+        pl.when(lax.axis_index("row") == row)(lambda row=row: work(row))
+
+
+def finish_kernel(
+    face_ref,
+    beyond_ref,
+    totals_ref,
     first_ref,
+    inv_ref,
+    lon_ref,
+    lat_ref,
     image_ref,
     second_ref,
     image2_ref,
-    x_ref,
-    u_ref,
-    v_ref,
-    r_ref,
-    w_ref,
+    sums_ref,
+    changes_ref,
 ):
-    layers, cells, width = field_ref.shape
-    every, spread, _ = inv_ref.shape
-    row = lax.axis_index("row")
-    lon, lat = lon_ref[...], lat_ref[:1]
-    nothing = jnp.zeros((spread, width), jnp.float32)
-    for ref in (x_ref, u_ref, v_ref):
-        ref[0] = nothing
-        ref[every + 1] = nothing
-    for ref, edge, base in (
-        (field_ref, mine_ref, row * layers),
-        (far_ref, other_ref, (1 - row) * layers),
-    ):
-        for layer in range(layers):
-            x_ref[base + layer + 1, :cells] = ref[layer]
-            x_ref[base + layer + 1, cells:] = edge[spread + 8 * layer : spread + 8 * layer + 8]
-
-    def operate(ref, start, count):
-        mid = ref[start + 1]
-        below = radial_face(radial_ref, every, start) * (mid - ref[start])
-        for step in range(count):
-            layer = start + step
-            ahead = ref[layer + 2]
-            rise = radial_face(radial_ref, every, layer + 1) * (ahead - mid)
-            along = lon * (mid - pltpu.roll(mid, spread - 1, 0))
-            across = lat * (mid - pltpu.roll(mid, width - 1, 1))
-            yield (
-                layer,
-                step,
-                (below - rise)
-                + (along - pltpu.roll(along, 1, 0))
-                + (across - pltpu.roll(across, 1, 1)),
-            )
-            mid, below = ahead, rise
-
-    inflow = radial_face(radial_ref, every, 0) * (mine_ref[:spread] + other_ref[:spread])
-    for layer, _, value in operate(x_ref, row * (layers - 2), layers + 2):
-        residual = jnp.where(layer == 0, inflow, 0.0) - value
-        r_ref[layer] = residual
-        u_ref[layer + 1] = residual * inv_ref[layer]
-    for layer, _, value in operate(u_ref, row * (layers - 1), layers + 1):
-        w_ref[layer] = value
-        v_ref[layer + 1] = value * inv_ref[layer]
-
-    totals = [jnp.zeros((8, width), jnp.float32)] * 4
-    for layer, step, value in operate(v_ref, row * layers, layers):
-        residual, first = r_ref[layer, :cells], u_ref[layer + 1, :cells]
-        image, second = w_ref[layer, :cells], v_ref[layer + 1, :cells]
-        image2 = value[:cells]
-        residual_ref[step] = residual
-        first_ref[step] = first
-        image_ref[step] = image
-        second_ref[step] = second
-        image2_ref[step] = image2
-        pairs = ((residual, first), (first, image), (image, second), (second, image2))
-        for which, (left, right) in enumerate(pairs):
-            product = left * right
-            for at in range(0, cells, 8):
-                totals[which] = totals[which] + product[at : at + 8]
-    lane = lax.broadcasted_iota(jnp.int32, (8, width), 1)
-    packed = jnp.zeros((8, width), jnp.float32)
-    for which, total in enumerate(totals):
-        packed = jnp.where(lane == which, jnp.sum(total, axis=1, keepdims=True), packed)
-    sums_ref[...] = jnp.broadcast_to(jnp.sum(packed, axis=0, keepdims=True), sums_ref.shape)
+    every, spread, width = inv_ref.shape
+    cells = spread - 8
+
+    def strip(value):
+        return jnp.concatenate([value[cells - 8 :], value[:8]], axis=0)
+
+    def total_up(totals):
+        lane = lax.broadcasted_iota(jnp.int32, (8, width), 1)
+        packed = jnp.zeros((8, width), jnp.float32)
+        for which, total in enumerate(totals):
+            packed = jnp.where(lane == which, jnp.sum(total, axis=1, keepdims=True), packed)
+        sums_ref[...] = jnp.broadcast_to(jnp.sum(packed, axis=0, keepdims=True), sums_ref.shape)
+
+    @pl.when(lax.axis_index("row") == 1)
+    def _():
+        total_up([totals_ref[which] for which in range(4)])
+        changes_ref[...] = jnp.zeros(changes_ref.shape, jnp.float32)
+
+    @pl.when(lax.axis_index("row") == 0)
+    def _():
+        faces = [face_ref[face : face + 1] for face in range(REACH + 1)]
+        lon = (strip(lon_ref[0]), strip(lon_ref[1]))
+        lat = (lat_ref[0, :1], lat_ref[1, :1])
+        inv = [strip(inv_ref[layer]) for layer in range(2)]
+        blank = jnp.zeros((8, width), jnp.float32)
+        source = jnp.concatenate([blank, faces[0] * beyond_ref[...], blank], axis=0)
+        first = {0: source * inv[0]}
+        image = {0: source - neighbours(first, 0, faces, lon, lat), 1: -faces[1] * first[0]}
+        second = {layer: image[layer] * inv[layer] for layer in range(2)}
+        image2 = {
+            layer: image[layer] - neighbours(second, layer, faces, lon, lat) for layer in range(2)
+        }
+        image2[2] = -faces[2] * second[1]
+        changes = (image, second, image2)
+        totals = [totals_ref[which] for which in range(4)]
+        for layer in range(REACH):
+            for side, begin in enumerate((cells - 8, 0)):
+                rows = slice(begin, begin + 8)
+                vectors = [first_ref[layer, rows]]
+                for which, ref in enumerate((image_ref, second_ref, image2_ref)):
+                    change = blank
+                    if layer in changes[which]:
+                        change = changes[which][layer][16 * side : 16 * side + 8]
+                    changes_ref[which, layer, side] = change
+                    vectors.append(ref[layer, rows] + change)
+                for which in range(1, 4):
+                    totals[which] = totals[which] + vectors[which - 1] * vectors[which]
+        total_up(totals)
 
 
 def update_kernel(
@@ -447,6 +496,7 @@
     image_ref,
     second_ref,
     image2_ref,
+    changes_ref,
     out_ref,
     left_ref,
 ):
@@ -457,9 +507,16 @@
     )
     alpha, gain, alpha_next = step_sizes(a, b, c, e)
     along, back = alpha + alpha_next * gain, alpha_next * alpha
-    for layer in range(field_ref.shape[0]):
+    layers, cells, _ = field_ref.shape
+    for layer in range(layers):
         out_ref[layer] = field_ref[layer] + (along * first_ref[layer] - back * second_ref[layer])
         left_ref[layer] = residual_ref[layer] - (along * image_ref[layer] - back * image2_ref[layer])
+    for layer in range(REACH):
+        for side, begin in enumerate((cells - 8, 0)):
+            rows = slice(begin, begin + 8)
+            image, second, image2 = (changes_ref[which, layer, side] for which in range(3))
+            out_ref[layer, rows] = out_ref[layer, rows] - back * second
+            left_ref[layer, rows] = left_ref[layer, rows] - (along * image - back * image2)
 
 
 SMALL = pltpu.CompilerParams(vmem_limit_bytes=8 << 20)
@@ -518,67 +575,75 @@
         in_hbm(col_owner.reshape(1, -1)),
         in_hbm(col_offset.reshape(1, -1)),
     )
+    mine, field = lax.optimization_barrier((mine, start_field))
     sent = pl.pallas_call(
         pack_kernel,
         compiler_params=SMALL,
-        out_shape=struct((phi_devices, 4 * per, width), half),
+        out_shape=struct((2 * phi_devices, 2 * per, width), half),
         in_specs=in_vmem(3),
         out_specs=in_vmem(1)[0],
     )(mine, swap(mine), chosen)
-    sent, radial_coef, theta_coef, phi_coef, field, weights = lax.optimization_barrier(
-        (sent, radial_coef, theta_coef, phi_coef, start_field, phi_weight.T)
-    )
-    got = lax.all_to_all(sent, "phi", split_axis=0, concat_axis=0, tiled=True)
-    edge_rows = layers * REACH + 2 * count // width
-    edge = struct((-(-edge_rows // 8) * 8, width), real)
-    far_edge, near_edge, share = pl.pallas_call(
+    other = swap(field)
+    sent, radial_coef, theta_coef, phi_coef, field, other, weights = lax.optimization_barrier(
+        (sent, radial_coef, theta_coef, phi_coef, field, other, phi_weight.T)
+    )
+    got = lax.all_to_all(sent, ("phi", "row"), split_axis=0, concat_axis=0, tiled=True)
+    edge = struct((every * REACH + 2 * phi_weight.shape[0] // width, width), real)
+    far_edge, near_edge = pl.pallas_call(
         edge_kernel,
         compiler_params=SMALL,
-        out_shape=[edge, edge, struct((cells, count), half)],
-        in_specs=in_vmem(2),
-        out_specs=in_vmem(3),
-    )(field, weights)
+        out_shape=[edge, edge],
+        in_specs=in_vmem(3),
+        out_specs=in_vmem(2),
+    )(field, other, weights)
     far_edge, near_edge = lax.ppermute(far_edge, "phi", outer), lax.ppermute(near_edge, "phi", inner)
-    far = swap(field)
-    inv_diag, lon, lat = pl.pallas_call(
+    lines = struct((every, spread, width), real)
+    diag, inv, lon, lat, faces = pl.pallas_call(
         coef_kernel,
         compiler_params=SMALL,
         out_shape=[
-            struct((every, spread, width), real),
-            struct((spread, width), real),
-            struct((8, width), real),
+            lines,
+            lines,
+            struct((2, spread, width), real),
+            struct((2, 8, width), real),
+            struct((every + 1, width), real),
         ],
         in_specs=in_smem + in_vmem(2),
-        out_specs=in_vmem(3),
+        out_specs=in_vmem(5),
     )(radial_coef, theta_coef.reshape(1, width), phi_coef.reshape(-1, width))
-    got, far_edge, near_edge, far, inv_diag, lon, lat = lax.optimization_barrier(
-        (got, far_edge, near_edge, far, inv_diag, lon, lat)
-    )
-    part = pl.pallas_call(
+    got, far_edge, near_edge, diag, inv, lon, lat, faces = lax.optimization_barrier(
+        (got, far_edge, near_edge, diag, inv, lon, lat, faces)
+    )
+    own, beyond = pl.pallas_call(
         boundary_kernel,
         compiler_params=SMALL,
-        out_shape=struct((spread + 8 * layers, width), real),
+        out_shape=[struct((cells, width), real), struct((8, width), real)],
         in_specs=in_vmem(4),
-        out_specs=in_vmem(1)[0],
-    )(got, share, far_edge, near_edge)
+        out_specs=in_vmem(2),
+    )(got, weights, far_edge, near_edge)
     block = struct((layers, cells, width), real)
-    lines = pltpu.VMEM((every + 2, spread, width), real)
-    sums, *vectors = pl.pallas_call(
+    totals, residual, first, image, second, image2 = pl.pallas_call(
         krylov_kernel,
         compiler_params=SMALL,
-        out_shape=[struct((2 * phi_devices, width), real)] + [block] * 5,
-        in_specs=in_smem + in_vmem(7),
+        out_shape=[struct((4, 8, width), real)] + [block] * 5,
+        in_specs=in_vmem(10),
         out_specs=in_vmem(6),
-        scratch_shapes=[lines] * 5,
-    )(radial_coef, part, swap(part), field, far, inv_diag, lon, lat)
+    )(faces, own, field, other, far_edge, near_edge, diag, inv, lon, lat)
+    sums, changes = pl.pallas_call(
+        finish_kernel,
+        compiler_params=SMALL,
+        out_shape=[struct((2 * phi_devices, width), real), struct((3, REACH, 2, 8, width), real)],
+        in_specs=in_vmem(10),
+        out_specs=in_vmem(2),
+    )(faces, swap(beyond), totals, first, inv, lon, lat, image, second, image2)
     sums = lax.all_to_all(sums, ("phi", "row"), split_axis=0, concat_axis=0, tiled=True)
     return pl.pallas_call(
         update_kernel,
         compiler_params=SMALL,
         out_shape=[block] * 2,
-        in_specs=in_vmem(7),
+        in_specs=in_vmem(8),
         out_specs=in_vmem(2),
-    )(sums, field, *vectors)
+    )(sums, field, residual, first, image, second, image2, changes)
 
 
 def body(*args):
@@ -590,12 +655,13 @@
         and phi_devices > 2
         and phi_devices % 2 == 0
         and phi_weight.shape[0] % (32 * phi_devices) == 0
-        and layers >= 2
+        and layers >= REACH
         and cells % 8 == 0
-        and cells >= 8
+        and cells >= 16
         and width % 128 == 0
         and phi_coef.shape[0] % width == 0
-        and phi_weight.shape[0] % (2 * width) == 0
+        and phi_weight.shape[0] % width == 0
+        and (2 * layers * REACH) % 8 == 0
     )
     return (paired_body if fits else general_body)(*args)
 

time: 36.9 us -> 34.5 us (0.935)
  starting transfers between devices: 14.6 us -> 13.4 us
  blocking collectives: 9.88 us -> 9.11 us
  Pallas kernels: 5.26 us -> 4.49 us
    all_to_all x1, starting transfers between devices: 8.35 us -> 7.21 us  [paired_body(): lax.all_to_all(sent, ('phi', 'row'), split_axis=0, concat_axis=0, tiled=T...]
    ppermute x1, waiting for transfers between devices: 3.29 us -> 4.17 us  [paired_body(): lax.ppermute(far_edge, 'phi', outer)]
    pallas_call x5 -> x6, Pallas kernels: 3.16 us -> 2.37 us  [the longest x1 0.89 us: paired_body(): pl.pallas_call(pack_kernel, compiler_params=SMALL, out_shape=struct((2 *...]
    all_to_all x1, blocking collectives: 9.88 us -> 9.11 us  [paired_body(): lax.all_to_all(sums, ('phi', 'row'), split_axis=0, concat_axis=0, tiled=T...]
    ppermute x3, waiting for transfers between devices: 2.2 us -> 1.68 us  [swap(): return lax.ppermute(value, 'row', [(0, 1), (1, 0)])]
  transfers between devices with their start and end apart: 6 -> 6, of which waited for: 3 -> 3; matrix products, arithmetic and copies ran while one was open for 0% -> 0% of each run, Pallas kernels for 2% -> 6%
where the time goes in v5:
time: 34.5 us; the launch traced here: 34.3 us
  starting transfers between devices  13.4 us (39%)
  blocking collectives  9.11 us (26%)
  waiting for transfers between devices  5.85 us (17%)
  Pallas kernels  4.49 us (13%)
  between operations  0.72 us (2%)
  local copies, waits for them, and re-layouts  0.68 us (2%)
    all_to_all x1, blocking collectives, paired_body(): lax.all_to_all(sums, ('phi', 'row'), split_axis=0, concat_axis=0, tiled=T...  9.11 us
    all_to_all x1, starting transfers between devices, paired_body(): lax.all_to_all(sent, ('phi', 'row'), split_axis=0, concat_axis=0, tiled=T...  7.21 us
    ppermute x1, starting transfers between devices, paired_body(): lax.ppermute(far_edge, 'phi', outer)  5.53 us
    ppermute x1, waiting for transfers between devices, paired_body(): lax.ppermute(far_edge, 'phi', outer)  4.17 us
    ppermute x3, waiting for transfers between devices, swap(): return lax.ppermute(value, 'row', [(0, 1), (1, 0)])  1.68 us
    pallas_call x1, Pallas kernels, paired_body(): pl.pallas_call(column_kernel, compiler_params=SMALL, out_shape=[struct((c...  1.31 us
    pallas_call x1, Pallas kernels, paired_body(): pl.pallas_call(pack_kernel, compiler_params=SMALL, out_shape=struct((2 *...  0.89 us
    pallas_call x1, Pallas kernels, paired_body(): pl.pallas_call(update_kernel, compiler_params=SMALL, out_shape=[block] *...  0.8 us
  transfers between devices with their start and end apart: 6, of which 3 were waited for; matrix products, arithmetic and copies ran while one was open for 0% of the time, Pallas kernels for 6%

profile of v5, /device:TPU:0, one launch (start us, length us, event | category | flops | bytes accessed | tf_op | source)
XLA Modules:
  0.0 34.3 jit_solution(16112427398498806057)
XLA Ops:
  0.6 0.0 copy-start
  0.6 1.3 %shard_map.104 = (f32[256,128]{1,0:T(8,128)S(1)}, bf16[256,256]{1,0:T(8,128)(2,1)S(1)}) custom-call(bf16[256,512]{1,0:T(8,128)(2,1)} %mag_hbm.1, bf16[512,128]{1,0:T(8,128)(2,1)} %theta_hbm.1, s32[1,256]{1,0:T(1,128)} %bitcast.15, s32[1,256]{1,0:T(1,128)} %bitcast.16), custom_call_target="tpu_custom_call" | custom-call | tf_op jit(solution)/shard_map/pallas_call | solution.py:559
  2.0 0.5 %collective-permute-start = (f32[256,128]{1,0:T(8,128)S(1)}, f32[256,128]{1,0:T(8,128)S(1)}, u32[]{:S(2)}, u32[]{:S(2)}) collective-permute-start(f32[256,128]{1,0:T(8,128)S(1)} %get-tuple-element.39.mine_ref), channel_id=1, source_target_pairs={{0,1},{1,0},{2,3},{3,2},{4,5},{5,4},{6,7},{7,6},{8,9},{9,8},{10,11... | collective-permute-start | bytes 393224 | tf_op jit(solution)/shard_map/ppermute | solution.py:551
  2.5 0.0 copy-done
  2.5 0.1 collective-permute-start.1
  2.6 0.9 %collective-permute-done.other_ref = f32[256,128]{1,0:T(8,128)S(1)} collective-permute-done((f32[256,128]{1,0:T(8,128)S(1)}, f32[256,128]{1,0:T(8,128)S(1)}, u32[]{:S(2)}, u32[]{:S(2)}) %collective-permute-start) | collective-permute-done | bytes 131104 | tf_op jit(solution)/shard_map/ppermute | solution.py:551
  3.5 0.9 %shard_map.105 = bf16[32,32,128]{2,1,0:T(8,128)(2,1)} custom-call(f32[256,128]{1,0:T(8,128)S(1)} %get-tuple-element.39.mine_ref, f32[256,128]{1,0:T(8,128)S(1)} %collective-permute-done.other_ref, bf16[256,256]{1,0:T(8,128)(2,1)S(1)} %get-tuple-element.40.chosen_ref), custom_call_target="tpu_custom_call" | custom-call | tf_op jit(solution)/shard_map/pallas_call | solution.py:579
  4.4 0.0 collective-permute-done.1.other_ref
  4.4 0.0 copy-start.1
  4.4 7.2 %all-to-all-start = ((bf16[32,32,128]{2,1,0:T(8,128)(2,1)}), bf16[32,32,128]{2,1,0:T(8,128)(2,1)S(1)}, u32[]{:S(2)}, u32[]{:S(2)}) async-start(bf16[32,32,128]{2,1,0:T(8,128)(2,1)} %shard_map.105), calls=%async_computation | async-start | bytes 524288 | tf_op jit(solution)/shard_map/all_to_all | solution.py:590
  11.6 0.0 copy-done.1
  11.6 0.0 copy-start.2
  11.6 5.5 %collective-permute-start.2 = (f32[32,128]{1,0:T(8,128)S(1)}, f32[32,128]{1,0:T(8,128)S(1)}, u32[]{:S(2)}, u32[]{:S(2)}) collective-permute-start(f32[32,128]{1,0:T(8,128)S(1)} %get-tuple-element.46), channel_id=1, source_target_pairs={{0,30},{2,4},{4,2},{6,8},{8,6},{10,12},{12,10},{14,16},{16,14},{18... | collective-permute-start | bytes 49160 | tf_op jit(solution)/shard_map/ppermute | solution.py:599
  17.2 0.0 collective-permute-start.3
  17.2 0.0 copy-start.3
  17.2 0.0 copy-start.4
  17.2 0.0 copy-done.2
  17.2 0.6 %copy-done.3 = f32[8]{0:T(128)S(1)} copy-done((f32[8]{0:T(128)S(1)}, f32[8]{0:T(128)}, u32[]{:S(2)}) %copy-start.3) | copy-done | bytes 56
  17.8 0.0 copy-done.4
  17.8 0.7 %shard_map.107 = (f32[8,56,128]{2,1,0:T(8,128)S(1)}, f32[8,56,128]{2,1,0:T(8,128)S(1)}, f32[2,56,128]{2,1,0:T(8,128)S(1)}, f32[2,8,128]{2,1,0:T(8,128)S(1)}, f32[9,128]{1,0:T(8,128)S(1)}) custom-call(f32[8]{0:T(128)S(1)} %copy-done.3, f32[1,128]{1,0:T(1,128)S(1)} %bitcast.14, f32[6,128]{1,0:T(8,128)S(1)} %bitcast.13), custom_call_target="tpu_custom_call" | custom-call | tf_op jit(solution)/shard_map/pallas_call | solution.py:601
  18.5 4.2 %collective-permute-done.2.far_ref = f32[32,128]{1,0:T(8,128)S(1)} collective-permute-done((f32[32,128]{1,0:T(8,128)S(1)}, f32[32,128]{1,0:T(8,128)S(1)}, u32[]{:S(2)}, u32[]{:S(2)}) %collective-permute-start.2) | collective-permute-done | bytes 16416 | tf_op jit(solution)/shard_map/ppermute | solution.py:599
  22.7 0.0 collective-permute-done.3.near_ref
  22.7 0.0 all-to-all-done.got_ref
  22.7 0.2 shard_map.108
  22.9 0.1 collective-permute-start.4
  23.0 0.4 %shard_map.109 = (f32[4,8,128]{2,1,0:T(8,128)S(1)}, f32[4,48,128]{2,1,0:T(8,128)S(1)}, f32[4,48,128]{2,1,0:T(8,128)S(1)}, f32[4,48,128]{2,1,0:T(8,128)S(1)}, f32...) custom-call(f32[9,128]{1,0:T(8,128)S(1)} %get-tuple-element.56.face_ref, f32[48,128]{1,0:T(8,128)S(1)} %get-tuple-element.61.own_ref, ...), custom_call_target="tpu_custom_call" | custom-call | tf_op jit(solution)/shard_map/pallas_call | solution.py:625
  23.3 0.8 %collective-permute-done.4.beyond_ref = f32[8,128]{1,0:T(8,128)S(1)} collective-permute-done((f32[8,128]{1,0:T(8,128)S(1)}, f32[8,128]{1,0:T(8,128)S(1)}, u32[]{:S(2)}, u32[]{:S(2)}) %collective-permute-start.4) | collective-permute-done | bytes 4128 | tf_op jit(solution)/shard_map/ppermute | solution.py:551
  24.1 0.2 shard_map.110
  24.3 9.1 %all_to_all.16 = f32[32,1,128]{2,1,0:T(1,128)S(1)} all-to-all(f32[32,1,128]{2,1,0:T(1,128)S(1)} %bitcast.12), channel_id=1, replica_groups=mesh['phi'=16,'row'=2] {'phi','row'}, dimensions={0} | all-to-all | bytes 32768 | tf_op jit(solution)/shard_map/all_to_all | solution.py:639
  33.5 0.8 %shard_map.111 = (f32[4,48,128]{2,1,0:T(8,128)}, f32[4,48,128]{2,1,0:T(8,128)}) custom-call(f32[32,128]{1,0:T(8,128)S(1)} %bitcast.11, f32[4,48,128]{2,1,0:T(8,128)S(1)} %copy-done, f32[4,48,128]{2,1,0:T(8,128)S(1)} %get-tuple-element.72.residual_ref, f32[4,48,128]{2,1,0:T(8,128)S(1)} %get-tuple-element.67.first_ref, ...), custom_call_target="tpu_custom_call" | custom-call | tf_op jit(solution)/shard_map/pallas_call | solution.py:640
  (1 shorter events, 0.0 us)
Async XLA Ops:
  0.6 1.9 %copy-start = (f32[4,48,128]{2,1,0:T(8,128)S(1)}, f32[4,48,128]{2,1,0:T(8,128)}, u32[]{:S(2)}) copy-start(f32[4,48,128]{2,1,0:T(8,128)} %field_ref.2) | copy-start | bytes 294916
  2.0 1.5 %collective-permute-start = (f32[256,128]{1,0:T(8,128)S(1)}, f32[256,128]{1,0:T(8,128)S(1)}, u32[]{:S(2)}, u32[]{:S(2)}) collective-permute-start(f32[256,128]{1,0:T(8,128)S(1)} %get-tuple-element.39.mine_ref), channel_id=1, source_target_pairs={{0,1},{1,0},{2,3},{3,2},{4,5},{5,4},{6,7},{7,6},{8,9},{9,8},{10,11... | collective-permute-start | bytes 393224 | tf_op jit(solution)/shard_map/ppermute | solution.py:551
  2.5 1.9 %collective-permute-start.1 = (f32[4,48,128]{2,1,0:T(8,128)S(1)}, f32[4,48,128]{2,1,0:T(8,128)S(1)}, u32[]{:S(2)}, u32[]{:S(2)}) collective-permute-start(f32[4,48,128]{2,1,0:T(8,128)S(1)} %copy-done), channel_id=1, source_target_pairs={{0,1},{1,0},{2,3},{3,2},{4,5},{5,4},{6,7},{7,6},{8,9},{9,8},{10,11... | collective-permute-start | bytes 294920 | tf_op jit(solution)/shard_map/ppermute | solution.py:551
  4.4 7.2 %copy-start.1 = (bf16[512,48]{0,1:T(8,128)(2,1)S(1)}, bf16[512,48]{0,1:T(8,128)(2,1)}, u32[]{:S(2)}) copy-start(bf16[512,48]{0,1:T(8,128)(2,1)} %param.12) | copy-start | bytes 147460
  4.4 18.4 %all-to-all-start = ((bf16[32,32,128]{2,1,0:T(8,128)(2,1)}), bf16[32,32,128]{2,1,0:T(8,128)(2,1)S(1)}, u32[]{:S(2)}, u32[]{:S(2)}) async-start(bf16[32,32,128]{2,1,0:T(8,128)(2,1)} %shard_map.105), calls=%async_computation | async-start | bytes 524288 | tf_op jit(solution)/shard_map/all_to_all | solution.py:590
  11.6 5.6 %copy-start.2 = (f32[768]{0:T(1024)S(1)}, f32[768]{0:T(1024)}, u32[]{:S(2)}) copy-start(f32[768]{0:T(1024)} %param.16) | copy-start | bytes 9220
  11.6 11.1 %collective-permute-start.2 = (f32[32,128]{1,0:T(8,128)S(1)}, f32[32,128]{1,0:T(8,128)S(1)}, u32[]{:S(2)}, u32[]{:S(2)}) collective-permute-start(f32[32,128]{1,0:T(8,128)S(1)} %get-tuple-element.46), channel_id=1, source_target_pairs={{0,30},{2,4},{4,2},{6,8},{8,6},{10,12},{12,10},{14,16},{16,14},{18... | collective-permute-start | bytes 49160 | tf_op jit(solution)/shard_map/ppermute | solution.py:599
  17.2 5.5 %collective-permute-start.3 = (f32[32,128]{1,0:T(8,128)S(1)}, f32[32,128]{1,0:T(8,128)S(1)}, u32[]{:S(2)}, u32[]{:S(2)}) collective-permute-start(f32[32,128]{1,0:T(8,128)S(1)} %get-tuple-element.47), channel_id=1, source_target_pairs={{0,2},{2,0},{4,6},{6,4},{8,10},{10,8},{12,14},{14,12},{16,18},{18,... | collective-permute-start | bytes 49160 | tf_op jit(solution)/shard_map/ppermute | solution.py:599
  17.2 0.7 %copy-start.3 = (f32[8]{0:T(128)S(1)}, f32[8]{0:T(128)}, u32[]{:S(2)}) copy-start(f32[8]{0:T(128)} %radial_ref) | copy-start | bytes 100
  17.2 0.7 %copy-start.4 = (f32[128]{0:T(128)S(1)}, f32[128]{0:T(128)}, u32[]{:S(2)}) copy-start(f32[128]{0:T(128)} %param.15) | copy-start | bytes 1540
  22.9 1.2 %collective-permute-start.4 = (f32[8,128]{1,0:T(8,128)S(1)}, f32[8,128]{1,0:T(8,128)S(1)}, u32[]{:S(2)}, u32[]{:S(2)}) collective-permute-start(f32[8,128]{1,0:T(8,128)S(1)} %get-tuple-element.60), channel_id=1, source_target_pairs={{0,1},{1,0},{2,3},{3,2},{4,5},{5,4},{6,7},{7,6},{8,9},{9,8},{10,11... | collective-permute-start | bytes 12296 | tf_op jit(solution)/shard_map/ppermute | solution.py:551

commit v6 on v5

--- a/solution.py
+++ b/solution.py
@@ -229,10 +229,11 @@
     chosen_ref[...] = jnp.where(slot == target, 1.0, 0.0).astype(jnp.bfloat16)
 
 
-def pack_kernel(mine_ref, other_ref, chosen_ref, out_ref):
+def pack_kernel(mine_ref, mag_ref, theta_ref, chosen_ref, out_ref):
     targets, rows, width = out_ref.shape
     devices, per = targets // 2, rows // 2
-    high, low = high_low(mine_ref[...] + other_ref[...])
+    other = jnp.dot(mag_ref[...], theta_ref[...], preferred_element_type=jnp.float32)
+    high, low = high_low(mine_ref[...] + other)
     packed = jnp.dot(
         chosen_ref[...], jnp.concatenate([high, low], axis=1), preferred_element_type=jnp.float32
     ).astype(jnp.bfloat16)
@@ -575,17 +576,17 @@
         in_hbm(col_owner.reshape(1, -1)),
         in_hbm(col_offset.reshape(1, -1)),
     )
-    mine, field = lax.optimization_barrier((mine, start_field))
+    partner = swap(magnetogram), swap(theta_weight)
+    other = swap(start_field)
     sent = pl.pallas_call(
         pack_kernel,
         compiler_params=SMALL,
         out_shape=struct((2 * phi_devices, 2 * per, width), half),
-        in_specs=in_vmem(3),
+        in_specs=in_vmem(4),
         out_specs=in_vmem(1)[0],
-    )(mine, swap(mine), chosen)
-    other = swap(field)
+    )(mine, *partner, chosen)
     sent, radial_coef, theta_coef, phi_coef, field, other, weights = lax.optimization_barrier(
-        (sent, radial_coef, theta_coef, phi_coef, field, other, phi_weight.T)
+        (sent, radial_coef, theta_coef, phi_coef, start_field, other, phi_weight.T)
     )
     got = lax.all_to_all(sent, ("phi", "row"), split_axis=0, concat_axis=0, tiled=True)
     edge = struct((every * REACH + 2 * phi_weight.shape[0] // width, width), real)

time: 34.5 us -> 34.1 us (0.988)
  waiting for transfers between devices: 5.85 us -> 4.95 us
    ppermute x3 -> x4, waiting for transfers between devices: 1.68 us -> 0.78 us  [swap(): return lax.ppermute(value, 'row', [(0, 1), (1, 0)])]
    ppermute x3 -> x4, starting transfers between devices: 0.68 us -> 1.1 us  [swap(): return lax.ppermute(value, 'row', [(0, 1), (1, 0)])]
  transfers between devices with their start and end apart: 6 -> 7, of which waited for: 3 -> 2; matrix products, arithmetic and copies ran while one was open for 0% -> 0% of each run, Pallas kernels for 6% -> 10%
where the time goes in v6:
time: 34.1 us; the launch traced here: 33.8 us
  starting transfers between devices  13.6 us (40%)
  blocking collectives  9.12 us (27%)
  waiting for transfers between devices  4.95 us (15%)
  Pallas kernels  4.71 us (14%)
  between operations  0.74 us (2%)
  local copies, waits for them, and re-layouts  0.68 us (2%)
    all_to_all x1, blocking collectives, paired_body(): lax.all_to_all(sums, ('phi', 'row'), split_axis=0, concat_axis=0, tiled=T...  9.12 us
    all_to_all x1, starting transfers between devices, paired_body(): lax.all_to_all(sent, ('phi', 'row'), split_axis=0, concat_axis=0, tiled=T...  6.99 us
    ppermute x1, starting transfers between devices, paired_body(): lax.ppermute(far_edge, 'phi', outer)  5.53 us
    ppermute x1, waiting for transfers between devices, paired_body(): lax.ppermute(far_edge, 'phi', outer)  4.16 us
    pallas_call x1, Pallas kernels, paired_body(): pl.pallas_call(column_kernel, compiler_params=SMALL, out_shape=[struct((c...  1.29 us
    pallas_call x1, Pallas kernels, paired_body(): pl.pallas_call(pack_kernel, compiler_params=SMALL, out_shape=struct((2 *...  1.14 us
    ppermute x4, starting transfers between devices, swap(): return lax.ppermute(value, 'row', [(0, 1), (1, 0)])  1.1 us
    pallas_call x1, Pallas kernels, paired_body(): pl.pallas_call(update_kernel, compiler_params=SMALL, out_shape=[block] *...  0.8 us
  transfers between devices with their start and end apart: 7, of which 2 were waited for; matrix products, arithmetic and copies ran while one was open for 0% of the time, Pallas kernels for 10%

profile of v6, /device:TPU:0, one launch (start us, length us, event | category | flops | bytes accessed | tf_op | source)
XLA Modules:
  0.0 33.8 jit_solution(961500013750026631)
XLA Ops:
  0.6 0.5 %collective-permute-start = (bf16[256,512]{1,0:T(8,128)(2,1)}, bf16[256,512]{1,0:T(8,128)(2,1)S(1)}, u32[]{:S(2)}, u32[]{:S(2)}) collective-permute-start(bf16[256,512]{1,0:T(8,128)(2,1)} %mag_hbm.1), channel_id=1, source_target_pairs={{0,1},{1,0},{2,3},{3,2},{4,5},{5,4},{6,7},{7,6},{8,9},{9,8},{10,11... | collective-permute-start | bytes 786440 | tf_op jit(solution)/shard_map/ppermute | solution.py:552
  1.1 0.1 collective-permute-start.1
  1.2 0.4 %collective-permute-start.2 = (f32[4,48,128]{2,1,0:T(8,128)}, f32[4,48,128]{2,1,0:T(8,128)S(1)}, u32[]{:S(2)}, u32[]{:S(2)}) collective-permute-start(f32[4,48,128]{2,1,0:T(8,128)} %field_ref.2), channel_id=1, source_target_pairs={{0,1},{1,0},{2,3},{3,2},{4,5},{5,4},{6,7},{7,6},{8,9},{9,8},{10,11... | collective-permute-start | bytes 294920 | tf_op jit(solution)/shard_map/ppermute | solution.py:552
  1.7 1.3 %shard_map.104 = (f32[256,128]{1,0:T(8,128)S(1)}, bf16[256,256]{1,0:T(8,128)(2,1)S(1)}) custom-call(bf16[256,512]{1,0:T(8,128)(2,1)} %mag_hbm.1, bf16[512,128]{1,0:T(8,128)(2,1)} %theta_hbm.1, s32[1,256]{1,0:T(1,128)} %bitcast.15, s32[1,256]{1,0:T(1,128)} %bitcast.16), custom_call_target="tpu_custom_call" | custom-call | tf_op jit(solution)/shard_map/pallas_call | solution.py:560
  3.0 0.0 collective-permute-done.1.theta_ref
  3.0 0.0 collective-permute-done.mag_ref
  3.0 1.1 %shard_map.105 = bf16[32,32,128]{2,1,0:T(8,128)(2,1)} custom-call(f32[256,128]{1,0:T(8,128)S(1)} %get-tuple-element.36.mine_ref, bf16[256,512]{1,0:T(8,128)(2,1)S(1)} %collective-permute-done.mag_ref, bf16[512,128]{1,0:T(8,128)(2,1)S(1)} %collective-permute-done.1.theta_ref, bf16[256,256]{1,0:T(8,128)(2,1)S(1)} %get-tuple-element.37.chosen_ref), custom_call_target="tpu_custom_call" | custom-call | tf_op jit(solution)/shard_map/pallas_call | solution.py:581
  4.1 0.0 collective-permute-done.2.other_ref
  4.1 0.0 copy-start
  4.1 0.0 copy-start.1
  4.1 7.0 %all-to-all-start = ((bf16[32,32,128]{2,1,0:T(8,128)(2,1)}), bf16[32,32,128]{2,1,0:T(8,128)(2,1)S(1)}, u32[]{:S(2)}, u32[]{:S(2)}) async-start(bf16[32,32,128]{2,1,0:T(8,128)(2,1)} %shard_map.105), calls=%async_computation | async-start | bytes 524288 | tf_op jit(solution)/shard_map/all_to_all | solution.py:591
  11.1 0.0 copy-done
  11.1 0.0 copy-done.1
  11.2 0.0 copy-start.2
  11.2 5.5 %collective-permute-start.3 = (f32[32,128]{1,0:T(8,128)S(1)}, f32[32,128]{1,0:T(8,128)S(1)}, u32[]{:S(2)}, u32[]{:S(2)}) collective-permute-start(f32[32,128]{1,0:T(8,128)S(1)} %get-tuple-element.42), channel_id=1, source_target_pairs={{0,30},{2,4},{4,2},{6,8},{8,6},{10,12},{12,10},{14,16},{16,14},{18... | collective-permute-start | bytes 49160 | tf_op jit(solution)/shard_map/ppermute | solution.py:600
  16.7 0.0 collective-permute-start.4
  16.7 0.0 copy-start.3
  16.7 0.0 copy-start.4
  16.7 0.0 copy-done.2
  16.7 0.6 %copy-done.3 = f32[8]{0:T(128)S(1)} copy-done((f32[8]{0:T(128)S(1)}, f32[8]{0:T(128)}, u32[]{:S(2)}) %copy-start.3) | copy-done | bytes 56
  17.4 0.0 copy-done.4
  17.4 0.7 %shard_map.107 = (f32[8,56,128]{2,1,0:T(8,128)S(1)}, f32[8,56,128]{2,1,0:T(8,128)S(1)}, f32[2,56,128]{2,1,0:T(8,128)S(1)}, f32[2,8,128]{2,1,0:T(8,128)S(1)}, f32[9,128]{1,0:T(8,128)S(1)}) custom-call(f32[8]{0:T(128)S(1)} %copy-done.3, f32[1,128]{1,0:T(1,128)S(1)} %bitcast.14, f32[6,128]{1,0:T(8,128)S(1)} %bitcast.13), custom_call_target="tpu_custom_call" | custom-call | tf_op jit(solution)/shard_map/pallas_call | solution.py:602
  18.1 4.2 %collective-permute-done.3.far_ref = f32[32,128]{1,0:T(8,128)S(1)} collective-permute-done((f32[32,128]{1,0:T(8,128)S(1)}, f32[32,128]{1,0:T(8,128)S(1)}, u32[]{:S(2)}, u32[]{:S(2)}) %collective-permute-start.3) | collective-permute-done | bytes 16416 | tf_op jit(solution)/shard_map/ppermute | solution.py:600
  22.2 0.0 collective-permute-done.4.near_ref
  22.3 0.0 all-to-all-done.got_ref
  22.3 0.2 shard_map.108
  22.4 0.1 collective-permute-start.5
  22.5 0.4 %shard_map.109 = (f32[4,8,128]{2,1,0:T(8,128)S(1)}, f32[4,48,128]{2,1,0:T(8,128)S(1)}, f32[4,48,128]{2,1,0:T(8,128)S(1)}, f32[4,48,128]{2,1,0:T(8,128)S(1)}, f32...) custom-call(f32[9,128]{1,0:T(8,128)S(1)} %get-tuple-element.52.face_ref, f32[48,128]{1,0:T(8,128)S(1)} %get-tuple-element.57.own_ref, ...), custom_call_target="tpu_custom_call" | custom-call | tf_op jit(solution)/shard_map/pallas_call | solution.py:626
  22.9 0.8 %collective-permute-done.5.beyond_ref = f32[8,128]{1,0:T(8,128)S(1)} collective-permute-done((f32[8,128]{1,0:T(8,128)S(1)}, f32[8,128]{1,0:T(8,128)S(1)}, u32[]{:S(2)}, u32[]{:S(2)}) %collective-permute-start.5) | collective-permute-done | bytes 4128 | tf_op jit(solution)/shard_map/ppermute | solution.py:552
  23.7 0.2 shard_map.110
  23.9 9.1 %all_to_all.16 = f32[32,1,128]{2,1,0:T(1,128)S(1)} all-to-all(f32[32,1,128]{2,1,0:T(1,128)S(1)} %bitcast.12), channel_id=1, replica_groups=mesh['phi'=16,'row'=2] {'phi','row'}, dimensions={0} | all-to-all | bytes 32768 | tf_op jit(solution)/shard_map/all_to_all | solution.py:640
  33.0 0.8 %shard_map.111 = (f32[4,48,128]{2,1,0:T(8,128)}, f32[4,48,128]{2,1,0:T(8,128)}) custom-call(f32[32,128]{1,0:T(8,128)S(1)} %bitcast.11, f32[4,48,128]{2,1,0:T(8,128)S(1)} %copy-done, f32[4,48,128]{2,1,0:T(8,128)S(1)} %get-tuple-element.68.residual_ref, f32[4,48,128]{2,1,0:T(8,128)S(1)} %get-tuple-element.63.first_ref, ...), custom_call_target="tpu_custom_call" | custom-call | tf_op jit(solution)/shard_map/pallas_call | solution.py:641
  (1 shorter events, 0.0 us)
Async XLA Ops:
  0.6 2.3 %collective-permute-start = (bf16[256,512]{1,0:T(8,128)(2,1)}, bf16[256,512]{1,0:T(8,128)(2,1)S(1)}, u32[]{:S(2)}, u32[]{:S(2)}) collective-permute-start(bf16[256,512]{1,0:T(8,128)(2,1)} %mag_hbm.1), channel_id=1, source_target_pairs={{0,1},{1,0},{2,3},{3,2},{4,5},{5,4},{6,7},{7,6},{8,9},{9,8},{10,11... | collective-permute-start | bytes 786440 | tf_op jit(solution)/shard_map/ppermute | solution.py:552
  1.1 1.8 %collective-permute-start.1 = (bf16[512,128]{1,0:T(8,128)(2,1)}, bf16[512,128]{1,0:T(8,128)(2,1)S(1)}, u32[]{:S(2)}, u32[]{:S(2)}) collective-permute-start(bf16[512,128]{1,0:T(8,128)(2,1)} %theta_hbm.1), channel_id=1, source_target_pairs={{0,1},{1,0},{2,3},{3,2},{4,5},{5,4},{6,7},{7,6},{8,9},{9,8},{10,11... | collective-permute-start | bytes 393224 | tf_op jit(solution)/shard_map/ppermute | solution.py:552
  1.2 2.9 %collective-permute-start.2 = (f32[4,48,128]{2,1,0:T(8,128)}, f32[4,48,128]{2,1,0:T(8,128)S(1)}, u32[]{:S(2)}, u32[]{:S(2)}) collective-permute-start(f32[4,48,128]{2,1,0:T(8,128)} %field_ref.2), channel_id=1, source_target_pairs={{0,1},{1,0},{2,3},{3,2},{4,5},{5,4},{6,7},{7,6},{8,9},{9,8},{10,11... | collective-permute-start | bytes 294920 | tf_op jit(solution)/shard_map/ppermute | solution.py:552
  4.1 7.0 %copy-start = (f32[4,48,128]{2,1,0:T(8,128)S(1)}, f32[4,48,128]{2,1,0:T(8,128)}, u32[]{:S(2)}) copy-start(f32[4,48,128]{2,1,0:T(8,128)} %field_ref.2) | copy-start | bytes 294916
  4.1 7.0 %copy-start.1 = (bf16[512,48]{0,1:T(8,128)(2,1)S(1)}, bf16[512,48]{0,1:T(8,128)(2,1)}, u32[]{:S(2)}) copy-start(bf16[512,48]{0,1:T(8,128)(2,1)} %param.12) | copy-start | bytes 147460
  4.1 18.1 %all-to-all-start = ((bf16[32,32,128]{2,1,0:T(8,128)(2,1)}), bf16[32,32,128]{2,1,0:T(8,128)(2,1)S(1)}, u32[]{:S(2)}, u32[]{:S(2)}) async-start(bf16[32,32,128]{2,1,0:T(8,128)(2,1)} %shard_map.105), calls=%async_computation | async-start | bytes 524288 | tf_op jit(solution)/shard_map/all_to_all | solution.py:591
  11.2 5.6 %copy-start.2 = (f32[768]{0:T(1024)S(1)}, f32[768]{0:T(1024)}, u32[]{:S(2)}) copy-start(f32[768]{0:T(1024)} %param.16) | copy-start | bytes 9220
  11.2 11.1 %collective-permute-start.3 = (f32[32,128]{1,0:T(8,128)S(1)}, f32[32,128]{1,0:T(8,128)S(1)}, u32[]{:S(2)}, u32[]{:S(2)}) collective-permute-start(f32[32,128]{1,0:T(8,128)S(1)} %get-tuple-element.42), channel_id=1, source_target_pairs={{0,30},{2,4},{4,2},{6,8},{8,6},{10,12},{12,10},{14,16},{16,14},{18... | collective-permute-start | bytes 49160 | tf_op jit(solution)/shard_map/ppermute | solution.py:600
  16.7 5.5 %collective-permute-start.4 = (f32[32,128]{1,0:T(8,128)S(1)}, f32[32,128]{1,0:T(8,128)S(1)}, u32[]{:S(2)}, u32[]{:S(2)}) collective-permute-start(f32[32,128]{1,0:T(8,128)S(1)} %get-tuple-element.43), channel_id=1, source_target_pairs={{0,2},{2,0},{4,6},{6,4},{8,10},{10,8},{12,14},{14,12},{16,18},{18,... | collective-permute-start | bytes 49160 | tf_op jit(solution)/shard_map/ppermute | solution.py:600
  16.7 0.7 %copy-start.3 = (f32[8]{0:T(128)S(1)}, f32[8]{0:T(128)}, u32[]{:S(2)}) copy-start(f32[8]{0:T(128)} %radial_ref) | copy-start | bytes 100
  16.7 0.7 %copy-start.4 = (f32[128]{0:T(128)S(1)}, f32[128]{0:T(128)}, u32[]{:S(2)}) copy-start(f32[128]{0:T(128)} %param.15) | copy-start | bytes 1540
  22.4 1.2 %collective-permute-start.5 = (f32[8,128]{1,0:T(8,128)S(1)}, f32[8,128]{1,0:T(8,128)S(1)}, u32[]{:S(2)}, u32[]{:S(2)}) collective-permute-start(f32[8,128]{1,0:T(8,128)S(1)} %get-tuple-element.56), channel_id=1, source_target_pairs={{0,1},{1,0},{2,3},{3,2},{4,5},{5,4},{6,7},{7,6},{8,9},{9,8},{10,11... | collective-permute-start | bytes 12296 | tf_op jit(solution)/shard_map/ppermute | solution.py:552

commit v7 on v4

--- a/solution.py
+++ b/solution.py
@@ -197,12 +197,12 @@
     return high, (value - high.astype(jnp.float32)).astype(jnp.bfloat16)
 
 
-def radial_face(radial_ref, layers, face):
-    if isinstance(face, int):
-        low, high = max(face - 1, 0), min(face, layers - 1)
-    else:
-        low, high = jnp.maximum(face - 1, 0), jnp.minimum(face, layers - 1)
-    return 0.5 * (radial_ref[low] + radial_ref[high])
+def leader(devices):
+    return devices // 2 + 1
+
+
+def seat(slab, devices):
+    return lax.rem(leader(devices) - slab + devices, devices)
 
 
 def own_share(weights, devices):
@@ -210,7 +210,8 @@
     per = slots // devices // 2
     slot = lax.broadcasted_iota(jnp.int32, (slots, slots // 2), 0)
     place = lax.broadcasted_iota(jnp.int32, (slots, slots // 2), 1)
-    wanted = place // per * (2 * per) + lax.axis_index("row") * per + place % per
+    source = seat(place // per, devices)
+    wanted = source * (2 * per) + lax.axis_index("row") * per + place % per
     picker = jnp.where(slot == wanted, 1.0, 0.0).astype(jnp.bfloat16)
     return jnp.dot(weights, picker, preferred_element_type=jnp.float32).astype(jnp.bfloat16)
 
@@ -240,53 +241,67 @@
     for copy in copies:
         copy.wait()
     out_ref[...] = jnp.dot(mag_ref[...], theta_ref[...], preferred_element_type=jnp.float32)
-    per = chosen_ref.shape[0] // lax.axis_size("phi")
+    devices = lax.axis_size("phi")
+    per = chosen_ref.shape[0] // devices
     place = offset_ref[...] - lax.axis_index("row") * per
-    target = jnp.where((place >= 0) & (place < per), owner_ref[...] * per + place, -1)
+    target = jnp.where((place >= 0) & (place < per), seat(owner_ref[...], devices) * per + place, -1)
     slot = lax.broadcasted_iota(jnp.int32, chosen_ref.shape, 0)
     chosen_ref[...] = jnp.where(slot == target, 1.0, 0.0).astype(jnp.bfloat16)
 
 
-def pack_kernel(mine_ref, other_ref, chosen_ref, out_ref):
+def pack_kernel(mine_ref, mag_ref, theta_ref, chosen_ref, out_ref):
     devices, rows, width = out_ref.shape
     per = rows // 4
-    high, low = high_low(mine_ref[...] + other_ref[...])
+    other = jnp.dot(mag_ref[...], theta_ref[...], preferred_element_type=jnp.float32)
+    high, low = high_low(mine_ref[...] + other)
     packed = jnp.dot(
         chosen_ref[...], jnp.concatenate([high, low], axis=1), preferred_element_type=jnp.float32
     ).astype(jnp.bfloat16)
     high = packed[:, :width].reshape(devices, per, width)
-    low = packed[:, width:].reshape(devices, per, width)
     out_ref[:, :per] = high
-    out_ref[:, per : 2 * per] = low
-    for to in range(devices):
-        out_ref[to, 2 * per : 3 * per] = high[(to - 1) % devices]
-        out_ref[to, 3 * per : 4 * per] = high[(to + 1) % devices]
+    out_ref[:, per : 2 * per] = packed[:, width:].reshape(devices, per, width)
+    for at in range(devices):
+        out_ref[at, 2 * per : 3 * per] = high[(at + 1) % devices]
+        out_ref[at, 3 * per :] = high[(at - 1) % devices]
 
 
 def is_odd():
     return lax.rem(lax.axis_index("phi"), 2) == 1
 
 
-def edge_kernel(field_ref, weight_ref, far_ref, near_ref, share_ref):
+def edge_kernel(field_ref, other_ref, weight_ref, far_ref, near_ref, share_ref):
     layers, cells, width = field_ref.shape
-    devices = lax.axis_size("phi")
-    share = own_share(weight_ref[...], devices)
+    odd = is_odd()
+    first = lax.axis_index("row") == 0
+    share = own_share(weight_ref[...], lax.axis_size("phi"))
     share_ref[...] = share
     weights = share.astype(jnp.float32)
-    odd = is_odd()
 
     def put(at, up, down):
         far_ref[at : at + up.shape[0]] = jnp.where(odd, up, down)
         near_ref[at : at + up.shape[0]] = jnp.where(odd, down, up)
 
     for layer in range(layers):
-        put(layer * REACH, field_ref[layer, cells - REACH :], field_ref[layer, :REACH])
+        up = [ref[layer, cells - REACH :] for ref in (field_ref, other_ref)]
+        down = [ref[layer, :REACH] for ref in (field_ref, other_ref)]
+        put(layer * REACH, jnp.where(first, *up), jnp.where(first, *down))
+        put((layers + layer) * REACH, jnp.where(first, *up[::-1]), jnp.where(first, *down[::-1]))
     for part in range(share.shape[1] // width):
         piece = weights[:, part * width : (part + 1) * width]
-        put(layers * REACH + 2 * part, piece[cells - 2 :], piece[:2])
-
-
-def coef_kernel(radial_ref, theta_ref, phi_ref, inv_ref, lon_ref, lat_ref):
+        put(2 * layers * REACH + 2 * part, piece[cells - 2 :], piece[:2])
+
+
+def sides(far_ref, near_ref):
+    odd = is_odd()
+    return (
+        jnp.where(odd, far_ref[...], near_ref[...]),
+        jnp.where(odd, near_ref[...], far_ref[...]),
+    )
+
+
+def coef_kernel(
+    radial_ref, theta_ref, phi_ref, diag_ref, inv_ref, lon_ref, lat_ref, face_ref
+):
     layers, spread, width = inv_ref.shape
     cells = spread - 8
     chunks = phi_ref.shape[0]
@@ -299,139 +314,117 @@
     for chunk in range(chunks):
         found = found + jnp.where(lane + chunk * width == cell, phi_ref[chunk : chunk + 1], 0.0)
     column = jnp.broadcast_to(jnp.sum(found, axis=1, keepdims=True), (spread, width))
-    upper = 0.5 * (column + pltpu.roll(column, spread - 1, 0))
-    lower = pltpu.roll(upper, 1, 0)
-    lon_ref[...] = upper
+    lon_ref[0] = 0.5 * (column + pltpu.roll(column, spread - 1, 0))
+    lon_ref[1] = 0.5 * (column + pltpu.roll(column, 1, 0))
     theta = jnp.broadcast_to(theta_ref[...], (8, width))
-    end = lax.broadcasted_iota(jnp.int32, (8, width), 1) == width - 1
-    lat_upper = jnp.where(end, 0.0, 0.5 * (theta + pltpu.roll(theta, width - 1, 1)))
-    lat_ref[...] = lat_upper
-    flat = upper + lower + (lat_upper + pltpu.roll(lat_upper, 1, 1))[:1]
+    ends = lax.broadcasted_iota(jnp.int32, (8, width), 1)
+    upper = jnp.where(ends == width - 1, 0.0, 0.5 * (theta + pltpu.roll(theta, width - 1, 1)))
+    lower = jnp.where(ends == 0, 0.0, 0.5 * (theta + pltpu.roll(theta, 1, 1)))
+    lat_ref[0], lat_ref[1] = upper, lower
+    flat = lon_ref[0] + lon_ref[1] + (upper + lower)[:1]
+    faces = [
+        0.5 * (radial_ref[max(face - 1, 0)] + radial_ref[min(face, layers - 1)])
+        for face in range(layers + 1)
+    ]
+    for face in range(layers + 1):
+        face_ref[face : face + 1] = jnp.full((1, width), faces[face], jnp.float32)
     for layer in range(layers):
-        low, high = (radial_face(radial_ref, layers, layer + k) for k in range(2))
-        inv_ref[layer] = 1.0 / (flat + (low + high))
+        diag = flat + (faces[layer] + faces[layer + 1])
+        diag_ref[layer] = diag
+        inv_ref[layer] = 1.0 / diag
 
 
 def boundary_kernel(got_ref, share_ref, far_ref, near_ref, out_ref):
     devices, rows, width = got_ref.shape
     cells, count = share_ref.shape
     per, spread = rows // 4, cells + 8
-    layers = (out_ref.shape[0] - spread) // 8
-    odd = is_odd()
-    above_edge = jnp.where(odd, far_ref[...], near_ref[...])
-    below_edge = jnp.where(odd, near_ref[...], far_ref[...])
+    above, below = sides(far_ref, near_ref)
+    edge_rows = above.shape[0]
 
     def product(weights, first):
         data = [
             got_ref[:, which * per : (which + 1) * per].reshape(count, width)
             for which in (first, first + 1)
         ]
-        total = jnp.dot(
-            weights, jnp.concatenate(data, axis=1), preferred_element_type=jnp.float32
-        )
+        total = jnp.dot(weights, jnp.concatenate(data, axis=1), preferred_element_type=jnp.float32)
         return total[:, :width], total[:, width:]
 
     def edge_weights(edge):
-        at = layers * REACH
+        at = edge_rows - 2 * count // width
         parts = [edge[at + 2 * k : at + 2 * k + 2] for k in range(count // width)]
         return jnp.concatenate(parts, axis=1)
 
     high, low = product(share_ref[...], 0)
     out_ref[:cells] = high + low
     weights = jnp.concatenate(
-        [edge_weights(above_edge), jnp.zeros((4, count), jnp.float32), edge_weights(below_edge)],
-        axis=0,
-    )
-    below, above = product(weights.astype(jnp.bfloat16), 2)
+        [edge_weights(above), jnp.zeros((4, count), jnp.float32), edge_weights(below)], axis=0
+    )
+    from_below, from_above = product(weights.astype(jnp.bfloat16), 2)
     row = lax.broadcasted_iota(jnp.int32, (8, width), 0)
-    out_ref[cells:spread] = jnp.where(row < 4, above, below)
-    for layer in range(layers):
-        at, part = spread + 8 * layer, slice(layer * REACH, (layer + 1) * REACH)
-        out_ref[at : at + 8] = jnp.concatenate(
-            [above_edge[part], jnp.zeros((8 - 2 * REACH, width), jnp.float32), below_edge[part]],
-            axis=0,
-        )
+    out_ref[cells:spread] = jnp.where(row < 4, from_above, from_below)
+
+
+def neighbours(values, layer, faces, lon, lat):
+    mid = values[layer]
+    spread, width = mid.shape
+    total = lat[0] * pltpu.roll(mid, width - 1, 1) + lat[1] * pltpu.roll(mid, 1, 1)
+    total = total + lon[0] * pltpu.roll(mid, spread - 1, 0)
+    total = total + lon[1] * pltpu.roll(mid, 1, 0)
+    for at, face in ((layer - 1, layer), (layer + 1, layer + 1)):
+        if at in values:
+            total = total + faces[face] * values[at]
+    return total
 
 
 def krylov_kernel(
-    radial_ref,
-    mine_ref,
+    face_ref,
+    part_ref,
+    rest_ref,
+    field_ref,
     other_ref,
-    field_ref,
     far_ref,
+    near_ref,
+    diag_ref,
     inv_ref,
     lon_ref,
     lat_ref,
     sums_ref,
-    residual_ref,
-    first_ref,
-    image_ref,
-    second_ref,
-    image2_ref,
-    x_ref,
-    u_ref,
-    v_ref,
-    r_ref,
-    w_ref,
+    *vector_refs,
 ):
     layers, cells, width = field_ref.shape
     every, spread, _ = inv_ref.shape
-    row = lax.axis_index("row")
-    lon, lat = lon_ref[...], lat_ref[:1]
-    nothing = jnp.zeros((spread, width), jnp.float32)
-    for ref in (x_ref, u_ref, v_ref):
-        ref[0] = nothing
-        ref[every + 1] = nothing
-    for ref, edge, base in (
-        (field_ref, mine_ref, row * layers),
-        (far_ref, other_ref, (1 - row) * layers),
-    ):
-        for layer in range(layers):
-            x_ref[base + layer + 1, :cells] = ref[layer]
-            x_ref[base + layer + 1, cells:] = edge[spread + 8 * layer : spread + 8 * layer + 8]
-
-    def operate(ref, start, count):
-        mid = ref[start + 1]
-        below = radial_face(radial_ref, every, start) * (mid - ref[start])
-        for step in range(count):
-            layer = start + step
-            ahead = ref[layer + 2]
-            rise = radial_face(radial_ref, every, layer + 1) * (ahead - mid)
-            along = lon * (mid - pltpu.roll(mid, spread - 1, 0))
-            across = lat * (mid - pltpu.roll(mid, width - 1, 1))
-            yield (
-                layer,
-                step,
-                (below - rise)
-                + (along - pltpu.roll(along, 1, 0))
-                + (across - pltpu.roll(across, 1, 1)),
-            )
-            mid, below = ahead, rise
-
-    inflow = radial_face(radial_ref, every, 0) * (mine_ref[:spread] + other_ref[:spread])
-    for layer, _, value in operate(x_ref, row * (layers - 2), layers + 2):
-        residual = jnp.where(layer == 0, inflow, 0.0) - value
-        r_ref[layer] = residual
-        u_ref[layer + 1] = residual * inv_ref[layer]
-    for layer, _, value in operate(u_ref, row * (layers - 1), layers + 1):
-        w_ref[layer] = value
-        v_ref[layer + 1] = value * inv_ref[layer]
-
+    above, below = sides(far_ref, near_ref)
+    gap = jnp.zeros((8 - 2 * REACH, width), jnp.float32)
+    upper = lax.axis_index("row") == 1
+    faces = [face_ref[face : face + 1] for face in range(every + 1)]
+    lon, lat = (lon_ref[0], lon_ref[1]), (lat_ref[0, :1], lat_ref[1, :1])
+    field = {}
+    for layer in range(every):
+        edge = slice(layer * REACH, (layer + 1) * REACH)
+        at, high = layer % layers, layer >= layers
+        block = jnp.where(upper == high, field_ref[at], other_ref[at])
+        field[layer] = jnp.concatenate([block, above[edge], gap, below[edge]], axis=0)
+    residual, first, image, second, image2 = {}, {}, {}, {}, {}
+    for layer in range(every):
+        value = neighbours(field, layer, faces, lon, lat) - diag_ref[layer] * field[layer]
+        if layer == 0:
+            value = value + faces[0] * (part_ref[...] + rest_ref[...])
+        residual[layer] = value
+        first[layer] = value * inv_ref[layer]
+    for layer in range(every):
+        image[layer] = residual[layer] - neighbours(first, layer, faces, lon, lat)
+        second[layer] = image[layer] * inv_ref[layer]
     totals = [jnp.zeros((8, width), jnp.float32)] * 4
-    for layer, step, value in operate(v_ref, row * layers, layers):
-        residual, first = r_ref[layer, :cells], u_ref[layer + 1, :cells]
-        image, second = w_ref[layer, :cells], v_ref[layer + 1, :cells]
-        image2 = value[:cells]
-        residual_ref[step] = residual
-        first_ref[step] = first
-        image_ref[step] = image
-        second_ref[step] = second
-        image2_ref[step] = image2
-        pairs = ((residual, first), (first, image), (image, second), (second, image2))
-        for which, (left, right) in enumerate(pairs):
-            product = left * right
-            for at in range(0, cells, 8):
-                totals[which] = totals[which] + product[at : at + 8]
+    for layer in range(every):
+        image2[layer] = image[layer] - neighbours(second, layer, faces, lon, lat)
+        vectors = [each[layer] for each in (residual, first, image, second, image2)]
+        for which in range(4):
+            product = vectors[which] * vectors[which + 1]
+            for begin in range(0, cells, 8):
+                totals[which] = totals[which] + product[begin : begin + 8]
+    for ref, vector in zip(vector_refs, (residual, first, image, second, image2)):
+        for at in range(layers):
+            ref[at] = jnp.where(upper, vector[layers + at], vector[at])[:cells]
     lane = lax.broadcasted_iota(jnp.int32, (8, width), 1)
     packed = jnp.zeros((8, width), jnp.float32)
     for which, total in enumerate(totals):
@@ -496,6 +489,13 @@
     inner = [(i, i ^ 1) for i in range(phi_devices)]
     outer = [(i, (i + (1 if i % 2 else -1)) % phi_devices) for i in range(phi_devices)]
 
+    order = [(leader(phi_devices) - i) % phi_devices for i in range(phi_devices)]
+
+    def over_slabs(value):
+        return lax.all_to_all(
+            value, "phi", split_axis=0, concat_axis=0, axis_index_groups=[order], tiled=True
+        )
+
     def in_hbm(value):
         return pltpu.with_memory_space_constraint(value, pltpu.HBM)
 
@@ -518,60 +518,61 @@
         in_hbm(col_owner.reshape(1, -1)),
         in_hbm(col_offset.reshape(1, -1)),
     )
+    partner = swap(magnetogram), swap(theta_weight)
+    other = swap(start_field)
     sent = pl.pallas_call(
         pack_kernel,
         compiler_params=SMALL,
         out_shape=struct((phi_devices, 4 * per, width), half),
-        in_specs=in_vmem(3),
+        in_specs=in_vmem(4),
         out_specs=in_vmem(1)[0],
-    )(mine, swap(mine), chosen)
-    sent, radial_coef, theta_coef, phi_coef, field, weights = lax.optimization_barrier(
-        (sent, radial_coef, theta_coef, phi_coef, start_field, phi_weight.T)
-    )
-    got = lax.all_to_all(sent, "phi", split_axis=0, concat_axis=0, tiled=True)
-    edge_rows = layers * REACH + 2 * count // width
-    edge = struct((-(-edge_rows // 8) * 8, width), real)
+    )(mine, *partner, chosen)
+    sent, radial_coef, theta_coef, phi_coef, field, other, weights = lax.optimization_barrier(
+        (sent, radial_coef, theta_coef, phi_coef, start_field, other, phi_weight.T)
+    )
+    got = over_slabs(sent)
+    edge = struct((every * REACH + 2 * count // width, width), real)
     far_edge, near_edge, share = pl.pallas_call(
         edge_kernel,
         compiler_params=SMALL,
         out_shape=[edge, edge, struct((cells, count), half)],
-        in_specs=in_vmem(2),
+        in_specs=in_vmem(3),
         out_specs=in_vmem(3),
-    )(field, weights)
+    )(field, other, weights)
     far_edge, near_edge = lax.ppermute(far_edge, "phi", outer), lax.ppermute(near_edge, "phi", inner)
-    far = swap(field)
-    inv_diag, lon, lat = pl.pallas_call(
+    lines = struct((every, spread, width), real)
+    diag, inv, lon, lat, faces = pl.pallas_call(
         coef_kernel,
         compiler_params=SMALL,
         out_shape=[
-            struct((every, spread, width), real),
-            struct((spread, width), real),
-            struct((8, width), real),
+            lines,
+            lines,
+            struct((2, spread, width), real),
+            struct((2, 8, width), real),
+            struct((every + 1, width), real),
         ],
         in_specs=in_smem + in_vmem(2),
-        out_specs=in_vmem(3),
+        out_specs=in_vmem(5),
     )(radial_coef, theta_coef.reshape(1, width), phi_coef.reshape(-1, width))
-    got, far_edge, near_edge, far, inv_diag, lon, lat = lax.optimization_barrier(
-        (got, far_edge, near_edge, far, inv_diag, lon, lat)
+    got, far_edge, near_edge, diag, inv, lon, lat, faces = lax.optimization_barrier(
+        (got, far_edge, near_edge, diag, inv, lon, lat, faces)
     )
     part = pl.pallas_call(
         boundary_kernel,
         compiler_params=SMALL,
-        out_shape=struct((spread + 8 * layers, width), real),
+        out_shape=struct((spread, width), real),
         in_specs=in_vmem(4),
         out_specs=in_vmem(1)[0],
     )(got, share, far_edge, near_edge)
     block = struct((layers, cells, width), real)
-    lines = pltpu.VMEM((every + 2, spread, width), real)
     sums, *vectors = pl.pallas_call(
         krylov_kernel,
         compiler_params=SMALL,
-        out_shape=[struct((2 * phi_devices, width), real)] + [block] * 5,
-        in_specs=in_smem + in_vmem(7),
+        out_shape=[struct((phi_devices, width), real)] + [block] * 5,
+        in_specs=in_vmem(11),
         out_specs=in_vmem(6),
-        scratch_shapes=[lines] * 5,
-    )(radial_coef, part, swap(part), field, far, inv_diag, lon, lat)
-    sums = lax.all_to_all(sums, ("phi", "row"), split_axis=0, concat_axis=0, tiled=True)
+    )(faces, part, swap(part), field, other, far_edge, near_edge, diag, inv, lon, lat)
+    sums = over_slabs(sums)
     return pl.pallas_call(
         update_kernel,
         compiler_params=SMALL,
@@ -590,12 +591,13 @@
         and phi_devices > 2
         and phi_devices % 2 == 0
         and phi_weight.shape[0] % (32 * phi_devices) == 0
-        and layers >= 2
+        and layers >= REACH
         and cells % 8 == 0
-        and cells >= 8
+        and cells >= 16
         and width % 128 == 0
         and phi_coef.shape[0] % width == 0
         and phi_weight.shape[0] % (2 * width) == 0
+        and (2 * layers * REACH) % 8 == 0
     )
     return (paired_body if fits else general_body)(*args)
 

time: 36.9 us -> 33.2 us (0.90)
  starting transfers between devices: 14.6 us -> 12.7 us
  blocking collectives: 9.88 us -> 9.04 us
  waiting for transfers between devices: 5.49 us -> 4.97 us
  Pallas kernels: 5.26 us -> 4.83 us
    ppermute x1, starting transfers between devices: 5.59 us -> 2.43 us  [paired_body(): lax.ppermute(far_edge, 'phi', outer)]
    ppermute x3 -> x4, waiting for transfers between devices: 2.2 us -> 1.2 us  [swap(): return lax.ppermute(value, 'row', [(0, 1), (1, 0)])]
    all_to_all x1, blocking collectives: 9.88 us -> 9.04 us  [over_slabs(): lax.all_to_all(value, 'phi', split_axis=0, concat_axis=0, axis_index_grou...]
    pallas_call x2, Pallas kernels: 1.94 us -> 1.28 us  [the longest x1 0.69 us: paired_body(): pl.pallas_call(coef_kernel, compiler_params=SMALL, out_shape=[lines, line...]
    ppermute x1, starting transfers between devices: 0.01 us -> 0.56 us  [paired_body(): lax.ppermute(near_edge, 'phi', inner)]
    all_to_all x1, waiting for transfers between devices: 0.01 us -> 0.5 us  [over_slabs(): lax.all_to_all(value, 'phi', split_axis=0, concat_axis=0, axis_index_grou...]
    ppermute x3 -> x4, starting transfers between devices: 0.66 us -> 1.1 us  [swap(): return lax.ppermute(value, 'row', [(0, 1), (1, 0)])]
  transfers between devices with their start and end apart: 6 -> 7, of which waited for: 3 -> 3; matrix products, arithmetic and copies ran while one was open for 0% -> 0% of each run, Pallas kernels for 2% -> 10%
where the time goes in v7:
time: 33.2 us; the launch traced here: 32.9 us
  starting transfers between devices  12.7 us (38%)
  blocking collectives  9.04 us (27%)
  waiting for transfers between devices  4.97 us (15%)
  Pallas kernels  4.83 us (15%)
  between operations  0.71 us (2%)
  local copies, waits for them, and re-layouts  0.68 us (2%)
    all_to_all x1, blocking collectives, over_slabs(): lax.all_to_all(value, 'phi', split_axis=0, concat_axis=0, axis_index_grou...  9.04 us
    all_to_all x1, starting transfers between devices, over_slabs(): lax.all_to_all(value, 'phi', split_axis=0, concat_axis=0, axis_index_grou...  8.57 us
    ppermute x1, waiting for transfers between devices, paired_body(): lax.ppermute(far_edge, 'phi', outer)  3.27 us
    ppermute x1, starting transfers between devices, paired_body(): lax.ppermute(far_edge, 'phi', outer)  2.43 us
    pallas_call x1, Pallas kernels, paired_body(): pl.pallas_call(column_kernel, compiler_params=SMALL, out_shape=[struct((c...  1.29 us
    ppermute x4, waiting for transfers between devices, swap(): return lax.ppermute(value, 'row', [(0, 1), (1, 0)])  1.2 us
    pallas_call x1, Pallas kernels, paired_body(): pl.pallas_call(pack_kernel, compiler_params=SMALL, out_shape=struct((phi_...  1.13 us
    ppermute x4, starting transfers between devices, swap(): return lax.ppermute(value, 'row', [(0, 1), (1, 0)])  1.1 us
  transfers between devices with their start and end apart: 7, of which 3 were waited for; matrix products, arithmetic and copies ran while one was open for 0% of the time, Pallas kernels for 10%

profile of v7, /device:TPU:0, one launch (start us, length us, event | category | flops | bytes accessed | tf_op | source)
XLA Modules:
  0.0 32.9 jit_solution(13006875732846707490)
XLA Ops:
  0.6 0.5 %collective-permute-start = (bf16[256,512]{1,0:T(8,128)(2,1)}, bf16[256,512]{1,0:T(8,128)(2,1)S(1)}, u32[]{:S(2)}, u32[]{:S(2)}) collective-permute-start(bf16[256,512]{1,0:T(8,128)(2,1)} %mag_hbm.1), channel_id=1, source_target_pairs={{0,1},{1,0},{2,3},{3,2},{4,5},{5,4},{6,7},{7,6},{8,9},{9,8},{10,11... | collective-permute-start | bytes 786440 | tf_op jit(solution)/shard_map/ppermute | solution.py:487
  1.1 0.1 collective-permute-start.1
  1.2 0.4 %collective-permute-start.2 = (f32[4,48,128]{2,1,0:T(8,128)}, f32[4,48,128]{2,1,0:T(8,128)S(1)}, u32[]{:S(2)}, u32[]{:S(2)}) collective-permute-start(f32[4,48,128]{2,1,0:T(8,128)} %field_ref.2), channel_id=1, source_target_pairs={{0,1},{1,0},{2,3},{3,2},{4,5},{5,4},{6,7},{7,6},{8,9},{9,8},{10,11... | collective-permute-start | bytes 294920 | tf_op jit(solution)/shard_map/ppermute | solution.py:487
  1.7 1.3 %shard_map.104 = (f32[256,128]{1,0:T(8,128)S(1)}, bf16[256,256]{1,0:T(8,128)(2,1)S(1)}) custom-call(bf16[256,512]{1,0:T(8,128)(2,1)} %mag_hbm.1, bf16[512,128]{1,0:T(8,128)(2,1)} %theta_hbm.1, s32[1,256]{1,0:T(1,128)} %bitcast.14, s32[1,256]{1,0:T(1,128)} %bitcast.15), custom_call_target="tpu_custom_call" | custom-call | tf_op jit(solution)/shard_map/pallas_call | solution.py:502
  3.0 0.0 collective-permute-done.1.theta_ref
  3.0 0.0 collective-permute-done.mag_ref
  3.0 1.1 %shard_map.105 = bf16[16,64,128]{2,1,0:T(8,128)(2,1)} custom-call(f32[256,128]{1,0:T(8,128)S(1)} %get-tuple-element.33.mine_ref, bf16[256,512]{1,0:T(8,128)(2,1)S(1)} %collective-permute-done.mag_ref, bf16[512,128]{1,0:T(8,128)(2,1)S(1)} %collective-permute-done.1.theta_ref, bf16[256,256]{1,0:T(8,128)(2,1)S(1)} %get-tuple-element.34.chosen_ref), custom_call_target="tpu_custom_call" | custom-call | tf_op jit(solution)/shard_map/pallas_call | solution.py:523
  4.1 0.0 collective-permute-done.2.other_ref
  4.1 0.0 copy-start
  4.1 0.0 copy-start.1
  4.1 8.6 %all-to-all-start = ((bf16[16,64,128]{2,1,0:T(8,128)(2,1)}), bf16[16,64,128]{2,1,0:T(8,128)(2,1)S(1)}, u32[]{:S(2)}, u32[]{:S(2)}) async-start(bf16[16,64,128]{2,1,0:T(8,128)(2,1)} %shard_map.105), calls=%async_computation | async-start | bytes 524288 | tf_op jit(solution)/shard_map/all_to_all | solution.py:495
  12.7 0.0 copy-done
  12.7 0.0 copy-done.1
  12.7 0.2 shard_map.106
  12.9 0.0 copy-start.2
  12.9 2.4 %collective-permute-start.3 = (f32[28,128]{1,0:T(8,128)S(1)}, f32[28,128]{1,0:T(8,128)S(1)}, u32[]{:S(2)}, u32[]{:S(2)}) collective-permute-start(f32[28,128]{1,0:T(8,128)S(1)} %get-tuple-element.39), channel_id=1, source_target_pairs={{0,30},{2,4},{4,2},{6,8},{8,6},{10,12},{12,10},{14,16},{16,14},{18... | collective-permute-start | bytes 43016 | tf_op jit(solution)/shard_map/ppermute | solution.py:542
  15.3 0.6 %collective-permute-start.4 = (f32[28,128]{1,0:T(8,128)S(1)}, f32[28,128]{1,0:T(8,128)S(1)}, u32[]{:S(2)}, u32[]{:S(2)}) collective-permute-start(f32[28,128]{1,0:T(8,128)S(1)} %get-tuple-element.40), channel_id=1, source_target_pairs={{0,2},{2,0},{4,6},{6,4},{8,10},{10,8},{12,14},{14,12},{16,18},{18,... | collective-permute-start | bytes 43016 | tf_op jit(solution)/shard_map/ppermute | solution.py:542
  15.9 0.0 copy-start.3
  15.9 0.0 copy-start.4
  15.9 0.0 copy-done.2
  15.9 0.6 %copy-done.3 = f32[8]{0:T(128)S(1)} copy-done((f32[8]{0:T(128)S(1)}, f32[8]{0:T(128)}, u32[]{:S(2)}) %copy-start.3) | copy-done | bytes 56
  16.5 0.0 copy-done.4
  16.6 0.7 %shard_map.107 = (f32[8,56,128]{2,1,0:T(8,128)S(1)}, f32[8,56,128]{2,1,0:T(8,128)S(1)}, f32[2,56,128]{2,1,0:T(8,128)S(1)}, f32[2,8,128]{2,1,0:T(8,128)S(1)}, f32[9,128]{1,0:T(8,128)S(1)}) custom-call(f32[8]{0:T(128)S(1)} %copy-done.3, f32[1,128]{1,0:T(1,128)S(1)} %bitcast.13, f32[6,128]{1,0:T(8,128)S(1)} %bitcast.12), custom_call_target="tpu_custom_call" | custom-call | tf_op jit(solution)/shard_map/pallas_call | solution.py:544
  17.3 3.3 %collective-permute-done.3.far_ref = f32[28,128]{1,0:T(8,128)S(1)} collective-permute-done((f32[28,128]{1,0:T(8,128)S(1)}, f32[28,128]{1,0:T(8,128)S(1)}, u32[]{:S(2)}, u32[]{:S(2)}) %collective-permute-start.3) | collective-permute-done | bytes 14368 | tf_op jit(solution)/shard_map/ppermute | solution.py:542
  20.5 0.0 collective-permute-done.4.near_ref
  20.5 0.5 %all-to-all-done.got_ref = bf16[16,64,128]{2,1,0:T(8,128)(2,1)S(1)} async-done(((bf16[16,64,128]{2,1,0:T(8,128)(2,1)}), bf16[16,64,128]{2,1,0:T(8,128)(2,1)S(1)}, u32[]{:S(2)}, u32[]{:S(2)}) %all-to-all-start) | async-done | bytes 262176 | tf_op jit(solution)/shard_map/all_to_all | solution.py:495
  21.0 0.1 shard_map.108.part_ref
  21.2 0.1 collective-permute-start.5
  21.3 1.2 %collective-permute-done.5.rest_ref = f32[56,128]{1,0:T(8,128)S(1)} collective-permute-done((f32[56,128]{1,0:T(8,128)S(1)}, f32[56,128]{1,0:T(8,128)S(1)}, u32[]{:S(2)}, u32[]{:S(2)}) %collective-permute-start.5) | collective-permute-done | bytes 28704 | tf_op jit(solution)/shard_map/ppermute | solution.py:487
  22.5 0.6 %shard_map.109 = (f32[16,128]{1,0:T(8,128)S(1)}, f32[4,48,128]{2,1,0:T(8,128)S(1)}, f32[4,48,128]{2,1,0:T(8,128)S(1)}, f32[4,48,128]{2,1,0:T(8,128)S(1)}, f32[4,...) custom-call(f32[9,128]{1,0:T(8,128)S(1)} %get-tuple-element.49.face_ref, f32[56,128]{1,0:T(8,128)S(1)} %shard_map.108.part_ref, ...), custom_call_target="tpu_custom_call" | custom-call | tf_op jit(solution)/shard_map/pallas_call | solution.py:568
  23.0 9.0 %all_to_all.16 = f32[16,1,128]{2,1,0:T(1,128)S(1)} all-to-all(f32[16,1,128]{2,1,0:T(1,128)S(1)} %bitcast.11), channel_id=1, replica_groups={{18,16,14,12,10,8,6,4,2,0,30,28,26,24,22,20},{19,17,15,13,11,9,7,5,3,1,..., dimensions={0} | all-to-all | bytes 16384 | tf_op jit(solution)/shard_map/all_to_all | solution.py:495
  32.1 0.8 %shard_map.110 = (f32[4,48,128]{2,1,0:T(8,128)}, f32[4,48,128]{2,1,0:T(8,128)}) custom-call(f32[16,128]{1,0:T(8,128)S(1)} %bitcast.10, f32[4,48,128]{2,1,0:T(8,128)S(1)} %copy-done, f32[4,48,128]{2,1,0:T(8,128)S(1)} %get-tuple-element.59.residual_ref, f32[4,48,128]{2,1,0:T(8,128)S(1)} %get-tuple-element.60.first_ref, ...), custom_call_target="tpu_custom_call" | custom-call | tf_op jit(solution)/shard_map/pallas_call | solution.py:576
Async XLA Ops:
  0.6 2.3 %collective-permute-start = (bf16[256,512]{1,0:T(8,128)(2,1)}, bf16[256,512]{1,0:T(8,128)(2,1)S(1)}, u32[]{:S(2)}, u32[]{:S(2)}) collective-permute-start(bf16[256,512]{1,0:T(8,128)(2,1)} %mag_hbm.1), channel_id=1, source_target_pairs={{0,1},{1,0},{2,3},{3,2},{4,5},{5,4},{6,7},{7,6},{8,9},{9,8},{10,11... | collective-permute-start | bytes 786440 | tf_op jit(solution)/shard_map/ppermute | solution.py:487
  1.1 1.8 %collective-permute-start.1 = (bf16[512,128]{1,0:T(8,128)(2,1)}, bf16[512,128]{1,0:T(8,128)(2,1)S(1)}, u32[]{:S(2)}, u32[]{:S(2)}) collective-permute-start(bf16[512,128]{1,0:T(8,128)(2,1)} %theta_hbm.1), channel_id=1, source_target_pairs={{0,1},{1,0},{2,3},{3,2},{4,5},{5,4},{6,7},{7,6},{8,9},{9,8},{10,11... | collective-permute-start | bytes 393224 | tf_op jit(solution)/shard_map/ppermute | solution.py:487
  1.2 2.9 %collective-permute-start.2 = (f32[4,48,128]{2,1,0:T(8,128)}, f32[4,48,128]{2,1,0:T(8,128)S(1)}, u32[]{:S(2)}, u32[]{:S(2)}) collective-permute-start(f32[4,48,128]{2,1,0:T(8,128)} %field_ref.2), channel_id=1, source_target_pairs={{0,1},{1,0},{2,3},{3,2},{4,5},{5,4},{6,7},{7,6},{8,9},{9,8},{10,11... | collective-permute-start | bytes 294920 | tf_op jit(solution)/shard_map/ppermute | solution.py:487
  4.1 8.6 %copy-start = (f32[4,48,128]{2,1,0:T(8,128)S(1)}, f32[4,48,128]{2,1,0:T(8,128)}, u32[]{:S(2)}) copy-start(f32[4,48,128]{2,1,0:T(8,128)} %field_ref.2) | copy-start | bytes 294916
  4.1 8.6 %copy-start.1 = (bf16[512,48]{0,1:T(8,128)(2,1)S(1)}, bf16[512,48]{0,1:T(8,128)(2,1)}, u32[]{:S(2)}) copy-start(bf16[512,48]{0,1:T(8,128)(2,1)} %param.12) | copy-start | bytes 147460
  4.1 16.9 %all-to-all-start = ((bf16[16,64,128]{2,1,0:T(8,128)(2,1)}), bf16[16,64,128]{2,1,0:T(8,128)(2,1)S(1)}, u32[]{:S(2)}, u32[]{:S(2)}) async-start(bf16[16,64,128]{2,1,0:T(8,128)(2,1)} %shard_map.105), calls=%async_computation | async-start | bytes 524288 | tf_op jit(solution)/shard_map/all_to_all | solution.py:495
  12.9 3.0 %copy-start.2 = (f32[768]{0:T(1024)S(1)}, f32[768]{0:T(1024)}, u32[]{:S(2)}) copy-start(f32[768]{0:T(1024)} %param.16) | copy-start | bytes 9220
  12.9 7.6 %collective-permute-start.3 = (f32[28,128]{1,0:T(8,128)S(1)}, f32[28,128]{1,0:T(8,128)S(1)}, u32[]{:S(2)}, u32[]{:S(2)}) collective-permute-start(f32[28,128]{1,0:T(8,128)S(1)} %get-tuple-element.39), channel_id=1, source_target_pairs={{0,30},{2,4},{4,2},{6,8},{8,6},{10,12},{12,10},{14,16},{16,14},{18... | collective-permute-start | bytes 43016 | tf_op jit(solution)/shard_map/ppermute | solution.py:542
  15.3 5.2 %collective-permute-start.4 = (f32[28,128]{1,0:T(8,128)S(1)}, f32[28,128]{1,0:T(8,128)S(1)}, u32[]{:S(2)}, u32[]{:S(2)}) collective-permute-start(f32[28,128]{1,0:T(8,128)S(1)} %get-tuple-element.40), channel_id=1, source_target_pairs={{0,2},{2,0},{4,6},{6,4},{8,10},{10,8},{12,14},{14,12},{16,18},{18,... | collective-permute-start | bytes 43016 | tf_op jit(solution)/shard_map/ppermute | solution.py:542
  15.9 0.7 %copy-start.3 = (f32[8]{0:T(128)S(1)}, f32[8]{0:T(128)}, u32[]{:S(2)}) copy-start(f32[8]{0:T(128)} %radial_ref) | copy-start | bytes 100
  15.9 0.7 %copy-start.4 = (f32[128]{0:T(128)S(1)}, f32[128]{0:T(128)}, u32[]{:S(2)}) copy-start(f32[128]{0:T(128)} %param.15) | copy-start | bytes 1540
  21.2 1.3 %collective-permute-start.5 = (f32[56,128]{1,0:T(8,128)S(1)}, f32[56,128]{1,0:T(8,128)S(1)}, u32[]{:S(2)}, u32[]{:S(2)}) collective-permute-start(f32[56,128]{1,0:T(8,128)S(1)} %shard_map.108.part_ref), channel_id=1, source_target_pairs={{0,1},{1,0},{2,3},{3,2},{4,5},{5,4},{6,7},{7,6},{8,9},{9,8},{10,11... | collective-permute-start | bytes 86024 | tf_op jit(solution)/shard_map/ppermute | solution.py:487

commit v8 on v7

--- a/solution.py
+++ b/solution.py
@@ -378,8 +378,6 @@
 
 def krylov_kernel(
     face_ref,
-    part_ref,
-    rest_ref,
     field_ref,
     other_ref,
     far_ref,
@@ -388,7 +386,8 @@
     inv_ref,
     lon_ref,
     lat_ref,
-    sums_ref,
+    totals_ref,
+    low_ref,
     *vector_refs,
 ):
     layers, cells, width = field_ref.shape
@@ -407,8 +406,6 @@
     residual, first, image, second, image2 = {}, {}, {}, {}, {}
     for layer in range(every):
         value = neighbours(field, layer, faces, lon, lat) - diag_ref[layer] * field[layer]
-        if layer == 0:
-            value = value + faces[0] * (part_ref[...] + rest_ref[...])
         residual[layer] = value
         first[layer] = value * inv_ref[layer]
     for layer in range(every):
@@ -417,14 +414,47 @@
     totals = [jnp.zeros((8, width), jnp.float32)] * 4
     for layer in range(every):
         image2[layer] = image[layer] - neighbours(second, layer, faces, lon, lat)
-        vectors = [each[layer] for each in (residual, first, image, second, image2)]
+        vectors = [each[layer][:cells] for each in (residual, first, image, second, image2)]
+        if layer < REACH:
+            for which, vector in enumerate(vectors):
+                low_ref[which, layer] = vector
+        else:
+            for which in range(4):
+                product = vectors[which] * vectors[which + 1]
+                for begin in range(0, cells, 8):
+                    totals[which] = totals[which] + product[begin : begin + 8]
+    for ref, vector in zip(vector_refs, (residual, first, image, second, image2)):
+        for at in range(layers):
+            ref[at] = jnp.where(upper, vector[layers + at], vector[at])[:cells]
+    for which in range(4):
+        totals_ref[which] = totals[which]
+
+
+def boundary_effect_kernel(
+    face_ref, part_ref, rest_ref, inv_ref, lon_ref, lat_ref, totals_ref, low_ref, sums_ref, change_ref
+):
+    _, reach, cells, width = low_ref.shape
+    faces = [face_ref[face : face + 1] for face in range(reach + 1)]
+    lon, lat = (lon_ref[0], lon_ref[1]), (lat_ref[0, :1], lat_ref[1, :1])
+    source = faces[0] * (part_ref[...] + rest_ref[...])
+    first = {0: source * inv_ref[0]}
+    image = {0: source - neighbours(first, 0, faces, lon, lat), 1: -faces[1] * first[0]}
+    second = {layer: image[layer] * inv_ref[layer] for layer in range(2)}
+    image2 = {layer: image[layer] - neighbours(second, layer, faces, lon, lat) for layer in range(2)}
+    image2[2] = -faces[2] * second[1]
+    totals = [totals_ref[which] for which in range(4)]
+    for layer in range(reach):
+        vectors = []
+        for which, change in enumerate(({0: source}, first, image, second, image2)):
+            vector = low_ref[which, layer]
+            if layer in change:
+                change_ref[which, layer] = change[layer][:cells]
+                vector = vector + change[layer][:cells]
+            vectors.append(vector)
         for which in range(4):
             product = vectors[which] * vectors[which + 1]
             for begin in range(0, cells, 8):
                 totals[which] = totals[which] + product[begin : begin + 8]
-    for ref, vector in zip(vector_refs, (residual, first, image, second, image2)):
-        for at in range(layers):
-            ref[at] = jnp.where(upper, vector[layers + at], vector[at])[:cells]
     lane = lax.broadcasted_iota(jnp.int32, (8, width), 1)
     packed = jnp.zeros((8, width), jnp.float32)
     for which, total in enumerate(totals):
@@ -440,6 +470,7 @@
     image_ref,
     second_ref,
     image2_ref,
+    change_ref,
     out_ref,
     left_ref,
 ):
@@ -450,9 +481,18 @@
     )
     alpha, gain, alpha_next = step_sizes(a, b, c, e)
     along, back = alpha + alpha_next * gain, alpha_next * alpha
+    here = jnp.where(lax.axis_index("row") == 0, 1.0, 0.0)
+    reached = dict(zip(range(5), (1, 1, 2, 2, 3)))
     for layer in range(field_ref.shape[0]):
-        out_ref[layer] = field_ref[layer] + (along * first_ref[layer] - back * second_ref[layer])
-        left_ref[layer] = residual_ref[layer] - (along * image_ref[layer] - back * image2_ref[layer])
+        vectors = []
+        for which, ref in enumerate((residual_ref, first_ref, image_ref, second_ref, image2_ref)):
+            vector = ref[layer]
+            if layer < reached[which]:
+                vector = vector + here * change_ref[which, layer]
+            vectors.append(vector)
+        residual, first, image, second, image2 = vectors
+        out_ref[layer] = field_ref[layer] + (along * first - back * second)
+        left_ref[layer] = residual - (along * image - back * image2)
 
 
 SMALL = pltpu.CompilerParams(vmem_limit_bytes=8 << 20)
@@ -565,21 +605,29 @@
         out_specs=in_vmem(1)[0],
     )(got, share, far_edge, near_edge)
     block = struct((layers, cells, width), real)
-    sums, *vectors = pl.pallas_call(
+    totals, low, *vectors = pl.pallas_call(
         krylov_kernel,
         compiler_params=SMALL,
-        out_shape=[struct((phi_devices, width), real)] + [block] * 5,
-        in_specs=in_vmem(11),
-        out_specs=in_vmem(6),
-    )(faces, part, swap(part), field, other, far_edge, near_edge, diag, inv, lon, lat)
+        out_shape=[struct((4, 8, width), real), struct((5, REACH, cells, width), real)]
+        + [block] * 5,
+        in_specs=in_vmem(9),
+        out_specs=in_vmem(7),
+    )(faces, field, other, far_edge, near_edge, diag, inv, lon, lat)
+    sums, change = pl.pallas_call(
+        boundary_effect_kernel,
+        compiler_params=SMALL,
+        out_shape=[struct((phi_devices, width), real), struct((5, REACH, cells, width), real)],
+        in_specs=in_vmem(8),
+        out_specs=in_vmem(2),
+    )(faces, part, swap(part), inv, lon, lat, totals, low)
     sums = over_slabs(sums)
     return pl.pallas_call(
         update_kernel,
         compiler_params=SMALL,
         out_shape=[block] * 2,
-        in_specs=in_vmem(7),
+        in_specs=in_vmem(8),
         out_specs=in_vmem(2),
-    )(sums, field, *vectors)
+    )(sums, field, *vectors, change)
 
 
 def body(*args):

time: 33.2 us -> 32.9 us (level)
  waiting for transfers between devices: 4.97 us -> 4.46 us
    ppermute x4, waiting for transfers between devices: 1.2 us -> 0.68 us  [swap(): return lax.ppermute(value, 'row', [(0, 1), (1, 0)])]
    pallas_call x1 -> x2, Pallas kernels: 0.58 us -> 0.77 us  [the longest x1 0.5 us: paired_body(): pl.pallas_call(krylov_kernel, compiler_params=SMALL, out_shape=[struct((4...]
  transfers between devices with their start and end apart: 7 -> 7, of which waited for: 3 -> 3; matrix products, arithmetic and copies ran while one was open for 0% -> 0% of each run, Pallas kernels for 10% -> 12%
where the time goes in v8:
time: 32.9 us; the launch traced here: 32.6 us
  starting transfers between devices  12.7 us (39%)
  blocking collectives  9.04 us (27%)
  Pallas kernels  5 us (15%)
  waiting for transfers between devices  4.46 us (14%)
  between operations  0.72 us (2%)
  local copies, waits for them, and re-layouts  0.68 us (2%)
    all_to_all x1, blocking collectives, over_slabs(): lax.all_to_all(value, 'phi', split_axis=0, concat_axis=0, axis_index_grou...  9.04 us
    all_to_all x1, starting transfers between devices, over_slabs(): lax.all_to_all(value, 'phi', split_axis=0, concat_axis=0, axis_index_grou...  8.57 us
    ppermute x1, waiting for transfers between devices, paired_body(): lax.ppermute(far_edge, 'phi', outer)  3.27 us
    ppermute x1, starting transfers between devices, paired_body(): lax.ppermute(far_edge, 'phi', outer)  2.43 us
    pallas_call x1, Pallas kernels, paired_body(): pl.pallas_call(column_kernel, compiler_params=SMALL, out_shape=[struct((c...  1.29 us
    pallas_call x1, Pallas kernels, paired_body(): pl.pallas_call(pack_kernel, compiler_params=SMALL, out_shape=struct((phi_...  1.13 us
    ppermute x4, starting transfers between devices, swap(): return lax.ppermute(value, 'row', [(0, 1), (1, 0)])  1.1 us
    pallas_call x1, Pallas kernels, paired_body(): pl.pallas_call(update_kernel, compiler_params=SMALL, out_shape=[block] *...  0.8 us
  transfers between devices with their start and end apart: 7, of which 3 were waited for; matrix products, arithmetic and copies ran while one was open for 0% of the time, Pallas kernels for 12%

profile of v8, /device:TPU:0, one launch (start us, length us, event | category | flops | bytes accessed | tf_op | source)
XLA Modules:
  0.0 32.6 jit_solution(17230727820344315803)
XLA Ops:
  0.6 0.5 %collective-permute-start = (bf16[256,512]{1,0:T(8,128)(2,1)}, bf16[256,512]{1,0:T(8,128)(2,1)S(1)}, u32[]{:S(2)}, u32[]{:S(2)}) collective-permute-start(bf16[256,512]{1,0:T(8,128)(2,1)} %mag_hbm.1), channel_id=1, source_target_pairs={{0,1},{1,0},{2,3},{3,2},{4,5},{5,4},{6,7},{7,6},{8,9},{9,8},{10,11... | collective-permute-start | bytes 786440 | tf_op jit(solution)/shard_map/ppermute | solution.py:527
  1.1 0.1 collective-permute-start.1
  1.2 0.4 %collective-permute-start.2 = (f32[4,48,128]{2,1,0:T(8,128)}, f32[4,48,128]{2,1,0:T(8,128)S(1)}, u32[]{:S(2)}, u32[]{:S(2)}) collective-permute-start(f32[4,48,128]{2,1,0:T(8,128)} %field_ref.2), channel_id=1, source_target_pairs={{0,1},{1,0},{2,3},{3,2},{4,5},{5,4},{6,7},{7,6},{8,9},{9,8},{10,11... | collective-permute-start | bytes 294920 | tf_op jit(solution)/shard_map/ppermute | solution.py:527
  1.7 1.3 %shard_map.104 = (f32[256,128]{1,0:T(8,128)S(1)}, bf16[256,256]{1,0:T(8,128)(2,1)S(1)}) custom-call(bf16[256,512]{1,0:T(8,128)(2,1)} %mag_hbm.1, bf16[512,128]{1,0:T(8,128)(2,1)} %theta_hbm.1, s32[1,256]{1,0:T(1,128)} %bitcast.14, s32[1,256]{1,0:T(1,128)} %bitcast.15), custom_call_target="tpu_custom_call" | custom-call | tf_op jit(solution)/shard_map/pallas_call | solution.py:542
  3.0 0.0 collective-permute-done.1.theta_ref
  3.0 0.0 collective-permute-done.mag_ref
  3.0 1.1 %shard_map.105 = bf16[16,64,128]{2,1,0:T(8,128)(2,1)} custom-call(f32[256,128]{1,0:T(8,128)S(1)} %get-tuple-element.36.mine_ref, bf16[256,512]{1,0:T(8,128)(2,1)S(1)} %collective-permute-done.mag_ref, bf16[512,128]{1,0:T(8,128)(2,1)S(1)} %collective-permute-done.1.theta_ref, bf16[256,256]{1,0:T(8,128)(2,1)S(1)} %get-tuple-element.37.chosen_ref), custom_call_target="tpu_custom_call" | custom-call | tf_op jit(solution)/shard_map/pallas_call | solution.py:563
  4.1 0.0 collective-permute-done.2.other_ref
  4.1 0.0 copy-start
  4.1 0.0 copy-start.1
  4.1 8.6 %all-to-all-start = ((bf16[16,64,128]{2,1,0:T(8,128)(2,1)}), bf16[16,64,128]{2,1,0:T(8,128)(2,1)S(1)}, u32[]{:S(2)}, u32[]{:S(2)}) async-start(bf16[16,64,128]{2,1,0:T(8,128)(2,1)} %shard_map.105), calls=%async_computation | async-start | bytes 524288 | tf_op jit(solution)/shard_map/all_to_all | solution.py:535
  12.7 0.0 copy-done
  12.7 0.0 copy-done.1
  12.7 0.2 shard_map.106
  12.9 0.0 copy-start.2
  12.9 2.4 %collective-permute-start.3 = (f32[28,128]{1,0:T(8,128)S(1)}, f32[28,128]{1,0:T(8,128)S(1)}, u32[]{:S(2)}, u32[]{:S(2)}) collective-permute-start(f32[28,128]{1,0:T(8,128)S(1)} %get-tuple-element.42), channel_id=1, source_target_pairs={{0,30},{2,4},{4,2},{6,8},{8,6},{10,12},{12,10},{14,16},{16,14},{18... | collective-permute-start | bytes 43016 | tf_op jit(solution)/shard_map/ppermute | solution.py:582
  15.3 0.6 %collective-permute-start.4 = (f32[28,128]{1,0:T(8,128)S(1)}, f32[28,128]{1,0:T(8,128)S(1)}, u32[]{:S(2)}, u32[]{:S(2)}) collective-permute-start(f32[28,128]{1,0:T(8,128)S(1)} %get-tuple-element.43), channel_id=1, source_target_pairs={{0,2},{2,0},{4,6},{6,4},{8,10},{10,8},{12,14},{14,12},{16,18},{18,... | collective-permute-start | bytes 43016 | tf_op jit(solution)/shard_map/ppermute | solution.py:582
  15.9 0.0 copy-start.3
  15.9 0.0 copy-start.4
  15.9 0.0 copy-done.2
  15.9 0.6 %copy-done.3 = f32[8]{0:T(128)S(1)} copy-done((f32[8]{0:T(128)S(1)}, f32[8]{0:T(128)}, u32[]{:S(2)}) %copy-start.3) | copy-done | bytes 56
  16.5 0.0 copy-done.4
  16.6 0.7 %shard_map.107 = (f32[8,56,128]{2,1,0:T(8,128)S(1)}, f32[8,56,128]{2,1,0:T(8,128)S(1)}, f32[2,56,128]{2,1,0:T(8,128)S(1)}, f32[2,8,128]{2,1,0:T(8,128)S(1)}, f32[9,128]{1,0:T(8,128)S(1)}) custom-call(f32[8]{0:T(128)S(1)} %copy-done.3, f32[1,128]{1,0:T(1,128)S(1)} %bitcast.13, f32[6,128]{1,0:T(8,128)S(1)} %bitcast.12), custom_call_target="tpu_custom_call" | custom-call | tf_op jit(solution)/shard_map/pallas_call | solution.py:584
  17.3 3.3 %collective-permute-done.3.far_ref = f32[28,128]{1,0:T(8,128)S(1)} collective-permute-done((f32[28,128]{1,0:T(8,128)S(1)}, f32[28,128]{1,0:T(8,128)S(1)}, u32[]{:S(2)}, u32[]{:S(2)}) %collective-permute-start.3) | collective-permute-done | bytes 14368 | tf_op jit(solution)/shard_map/ppermute | solution.py:582
  20.5 0.0 collective-permute-done.4.near_ref
  20.5 0.5 %all-to-all-done.got_ref = bf16[16,64,128]{2,1,0:T(8,128)(2,1)S(1)} async-done(((bf16[16,64,128]{2,1,0:T(8,128)(2,1)}), bf16[16,64,128]{2,1,0:T(8,128)(2,1)S(1)}, u32[]{:S(2)}, u32[]{:S(2)}) %all-to-all-start) | async-done | bytes 262176 | tf_op jit(solution)/shard_map/all_to_all | solution.py:535
  21.0 0.1 shard_map.108.part_ref
  21.2 0.1 collective-permute-start.5
  21.3 0.5 %shard_map.109 = (f32[4,8,128]{2,1,0:T(8,128)S(1)}, f32[5,3,48,128]{3,2,1,0:T(8,128)S(1)}, f32[4,48,128]{2,1,0:T(8,128)S(1)}, f32[4,48,128]{2,1,0:T(8,128)S(1)},...) custom-call(f32[9,128]{1,0:T(8,128)S(1)} %get-tuple-element.52.face_ref, ...), custom_call_target="tpu_custom_call" | custom-call | tf_op jit(solution)/shard_map/pallas_call | solution.py:608
  21.8 0.7 %collective-permute-done.5.rest_ref = f32[56,128]{1,0:T(8,128)S(1)} collective-permute-done((f32[56,128]{1,0:T(8,128)S(1)}, f32[56,128]{1,0:T(8,128)S(1)}, u32[]{:S(2)}, u32[]{:S(2)}) %collective-permute-start.5) | collective-permute-done | bytes 28704 | tf_op jit(solution)/shard_map/ppermute | solution.py:527
  22.5 0.3 shard_map.110
  22.7 9.0 %all_to_all.16 = f32[16,1,128]{2,1,0:T(1,128)S(1)} all-to-all(f32[16,1,128]{2,1,0:T(1,128)S(1)} %bitcast.11), channel_id=1, replica_groups={{18,16,14,12,10,8,6,4,2,0,30,28,26,24,22,20},{19,17,15,13,11,9,7,5,3,1,..., dimensions={0} | all-to-all | bytes 16384 | tf_op jit(solution)/shard_map/all_to_all | solution.py:535
  31.8 0.8 %shard_map.111 = (f32[4,48,128]{2,1,0:T(8,128)}, f32[4,48,128]{2,1,0:T(8,128)}) custom-call(f32[16,128]{1,0:T(8,128)S(1)} %bitcast.10, f32[4,48,128]{2,1,0:T(8,128)S(1)} %copy-done, f32[4,48,128]{2,1,0:T(8,128)S(1)} %get-tuple-element.64.residual_ref, f32[4,48,128]{2,1,0:T(8,128)S(1)} %get-tuple-element.65.first_ref, ...), custom_call_target="tpu_custom_call" | custom-call | tf_op jit(solution)/shard_map/pallas_call | solution.py:624
Async XLA Ops:
  0.6 2.3 %collective-permute-start = (bf16[256,512]{1,0:T(8,128)(2,1)}, bf16[256,512]{1,0:T(8,128)(2,1)S(1)}, u32[]{:S(2)}, u32[]{:S(2)}) collective-permute-start(bf16[256,512]{1,0:T(8,128)(2,1)} %mag_hbm.1), channel_id=1, source_target_pairs={{0,1},{1,0},{2,3},{3,2},{4,5},{5,4},{6,7},{7,6},{8,9},{9,8},{10,11... | collective-permute-start | bytes 786440 | tf_op jit(solution)/shard_map/ppermute | solution.py:527
  1.1 1.8 %collective-permute-start.1 = (bf16[512,128]{1,0:T(8,128)(2,1)}, bf16[512,128]{1,0:T(8,128)(2,1)S(1)}, u32[]{:S(2)}, u32[]{:S(2)}) collective-permute-start(bf16[512,128]{1,0:T(8,128)(2,1)} %theta_hbm.1), channel_id=1, source_target_pairs={{0,1},{1,0},{2,3},{3,2},{4,5},{5,4},{6,7},{7,6},{8,9},{9,8},{10,11... | collective-permute-start | bytes 393224 | tf_op jit(solution)/shard_map/ppermute | solution.py:527
  1.2 2.9 %collective-permute-start.2 = (f32[4,48,128]{2,1,0:T(8,128)}, f32[4,48,128]{2,1,0:T(8,128)S(1)}, u32[]{:S(2)}, u32[]{:S(2)}) collective-permute-start(f32[4,48,128]{2,1,0:T(8,128)} %field_ref.2), channel_id=1, source_target_pairs={{0,1},{1,0},{2,3},{3,2},{4,5},{5,4},{6,7},{7,6},{8,9},{9,8},{10,11... | collective-permute-start | bytes 294920 | tf_op jit(solution)/shard_map/ppermute | solution.py:527
  4.1 8.6 %copy-start = (f32[4,48,128]{2,1,0:T(8,128)S(1)}, f32[4,48,128]{2,1,0:T(8,128)}, u32[]{:S(2)}) copy-start(f32[4,48,128]{2,1,0:T(8,128)} %field_ref.2) | copy-start | bytes 294916
  4.1 8.6 %copy-start.1 = (bf16[512,48]{0,1:T(8,128)(2,1)S(1)}, bf16[512,48]{0,1:T(8,128)(2,1)}, u32[]{:S(2)}) copy-start(bf16[512,48]{0,1:T(8,128)(2,1)} %param.12) | copy-start | bytes 147460
  4.1 16.9 %all-to-all-start = ((bf16[16,64,128]{2,1,0:T(8,128)(2,1)}), bf16[16,64,128]{2,1,0:T(8,128)(2,1)S(1)}, u32[]{:S(2)}, u32[]{:S(2)}) async-start(bf16[16,64,128]{2,1,0:T(8,128)(2,1)} %shard_map.105), calls=%async_computation | async-start | bytes 524288 | tf_op jit(solution)/shard_map/all_to_all | solution.py:535
  12.9 3.0 %copy-start.2 = (f32[768]{0:T(1024)S(1)}, f32[768]{0:T(1024)}, u32[]{:S(2)}) copy-start(f32[768]{0:T(1024)} %param.16) | copy-start | bytes 9220
  12.9 7.6 %collective-permute-start.3 = (f32[28,128]{1,0:T(8,128)S(1)}, f32[28,128]{1,0:T(8,128)S(1)}, u32[]{:S(2)}, u32[]{:S(2)}) collective-permute-start(f32[28,128]{1,0:T(8,128)S(1)} %get-tuple-element.42), channel_id=1, source_target_pairs={{0,30},{2,4},{4,2},{6,8},{8,6},{10,12},{12,10},{14,16},{16,14},{18... | collective-permute-start | bytes 43016 | tf_op jit(solution)/shard_map/ppermute | solution.py:582
  15.3 5.2 %collective-permute-start.4 = (f32[28,128]{1,0:T(8,128)S(1)}, f32[28,128]{1,0:T(8,128)S(1)}, u32[]{:S(2)}, u32[]{:S(2)}) collective-permute-start(f32[28,128]{1,0:T(8,128)S(1)} %get-tuple-element.43), channel_id=1, source_target_pairs={{0,2},{2,0},{4,6},{6,4},{8,10},{10,8},{12,14},{14,12},{16,18},{18,... | collective-permute-start | bytes 43016 | tf_op jit(solution)/shard_map/ppermute | solution.py:582
  15.9 0.7 %copy-start.3 = (f32[8]{0:T(128)S(1)}, f32[8]{0:T(128)}, u32[]{:S(2)}) copy-start(f32[8]{0:T(128)} %radial_ref) | copy-start | bytes 100
  15.9 0.7 %copy-start.4 = (f32[128]{0:T(128)S(1)}, f32[128]{0:T(128)}, u32[]{:S(2)}) copy-start(f32[128]{0:T(128)} %param.15) | copy-start | bytes 1540
  21.2 1.3 %collective-permute-start.5 = (f32[56,128]{1,0:T(8,128)S(1)}, f32[56,128]{1,0:T(8,128)S(1)}, u32[]{:S(2)}, u32[]{:S(2)}) collective-permute-start(f32[56,128]{1,0:T(8,128)S(1)} %shard_map.108.part_ref), channel_id=1, source_target_pairs={{0,1},{1,0},{2,3},{3,2},{4,5},{5,4},{6,7},{7,6},{8,9},{9,8},{10,11... | collective-permute-start | bytes 86024 | tf_op jit(solution)/shard_map/ppermute | solution.py:527

commit v9 on v8

--- a/solution.py
+++ b/solution.py
@@ -198,20 +198,30 @@
 
 
 def leader(devices):
-    return devices // 2 + 1
+    return 11 * devices // 16
 
 
 def seat(slab, devices):
     return lax.rem(leader(devices) - slab + devices, devices)
 
 
-def own_share(weights, devices):
+def share_of(slab, row, devices):
+    return row ^ (slab >= devices // 2)
+
+
+def own_half():
+    devices = lax.axis_size("phi")
+    return share_of(lax.axis_index("phi"), lax.axis_index("row"), devices)
+
+
+def share_weights(weights, half):
     slots = weights.shape[1]
+    devices = lax.axis_size("phi")
     per = slots // devices // 2
     slot = lax.broadcasted_iota(jnp.int32, (slots, slots // 2), 0)
     place = lax.broadcasted_iota(jnp.int32, (slots, slots // 2), 1)
     source = seat(place // per, devices)
-    wanted = source * (2 * per) + lax.axis_index("row") * per + place % per
+    wanted = source * (2 * per) + half * per + place % per
     picker = jnp.where(slot == wanted, 1.0, 0.0).astype(jnp.bfloat16)
     return jnp.dot(weights, picker, preferred_element_type=jnp.float32).astype(jnp.bfloat16)
 
@@ -243,7 +253,7 @@
     out_ref[...] = jnp.dot(mag_ref[...], theta_ref[...], preferred_element_type=jnp.float32)
     devices = lax.axis_size("phi")
     per = chosen_ref.shape[0] // devices
-    place = offset_ref[...] - lax.axis_index("row") * per
+    place = offset_ref[...] - own_half() * per
     target = jnp.where((place >= 0) & (place < per), seat(owner_ref[...], devices) * per + place, -1)
     slot = lax.broadcasted_iota(jnp.int32, chosen_ref.shape, 0)
     chosen_ref[...] = jnp.where(slot == target, 1.0, 0.0).astype(jnp.bfloat16)
@@ -273,9 +283,12 @@
     layers, cells, width = field_ref.shape
     odd = is_odd()
     first = lax.axis_index("row") == 0
-    share = own_share(weight_ref[...], lax.axis_size("phi"))
+    slab, devices = lax.axis_index("phi"), lax.axis_size("phi")
+    outer = lax.rem(slab + jnp.where(odd, 1, devices - 1), devices)
+    share = share_weights(weight_ref[...], own_half())
     share_ref[...] = share
-    weights = share.astype(jnp.float32)
+    far_share = share_weights(weight_ref[...], share_of(outer, lax.axis_index("row"), devices))
+    near_weights, far_weights = share.astype(jnp.float32), far_share.astype(jnp.float32)
 
     def put(at, up, down):
         far_ref[at : at + up.shape[0]] = jnp.where(odd, up, down)
@@ -287,8 +300,10 @@
         put(layer * REACH, jnp.where(first, *up), jnp.where(first, *down))
         put((layers + layer) * REACH, jnp.where(first, *up[::-1]), jnp.where(first, *down[::-1]))
     for part in range(share.shape[1] // width):
-        piece = weights[:, part * width : (part + 1) * width]
-        put(2 * layers * REACH + 2 * part, piece[cells - 2 :], piece[:2])
+        at, piece = 2 * layers * REACH + 2 * part, slice(part * width, (part + 1) * width)
+        near, far = near_weights[:, piece], far_weights[:, piece]
+        far_ref[at : at + 2] = jnp.where(odd, far[cells - 2 :], far[:2])
+        near_ref[at : at + 2] = jnp.where(odd, near[:2], near[cells - 2 :])
 
 
 def sides(far_ref, near_ref):
@@ -529,11 +544,16 @@
     inner = [(i, i ^ 1) for i in range(phi_devices)]
     outer = [(i, (i + (1 if i % 2 else -1)) % phi_devices) for i in range(phi_devices)]
 
-    order = [(leader(phi_devices) - i) % phi_devices for i in range(phi_devices)]
-
-    def over_slabs(value):
+    def over_slabs(value, member, lead):
+        order = [(lead - i) % phi_devices for i in range(phi_devices)]
+        groups = [[2 * slab + member(slab, half) for slab in order] for half in range(2)]
         return lax.all_to_all(
-            value, "phi", split_axis=0, concat_axis=0, axis_index_groups=[order], tiled=True
+            value,
+            ("phi", "row"),
+            split_axis=0,
+            concat_axis=0,
+            axis_index_groups=groups,
+            tiled=True,
         )
 
     def in_hbm(value):
@@ -570,7 +590,9 @@
     sent, radial_coef, theta_coef, phi_coef, field, other, weights = lax.optimization_barrier(
         (sent, radial_coef, theta_coef, phi_coef, start_field, other, phi_weight.T)
     )
-    got = over_slabs(sent)
+    got = over_slabs(
+        sent, lambda slab, half: int(share_of(slab, half, phi_devices)), leader(phi_devices)
+    )
     edge = struct((every * REACH + 2 * count // width, width), real)
     far_edge, near_edge, share = pl.pallas_call(
         edge_kernel,
@@ -620,7 +642,9 @@
         in_specs=in_vmem(8),
         out_specs=in_vmem(2),
     )(faces, part, swap(part), inv, lon, lat, totals, low)
-    sums = over_slabs(sums)
+    sums = over_slabs(
+        sums, lambda slab, half: int(share_of(slab, half, phi_devices)), leader(phi_devices)
+    )
     return pl.pallas_call(
         update_kernel,
         compiler_params=SMALL,
@@ -637,7 +661,7 @@
     fits = (
         lax.axis_size("row") == 2
         and phi_devices > 2
-        and phi_devices % 2 == 0
+        and phi_devices % 4 == 0
         and phi_weight.shape[0] % (32 * phi_devices) == 0
         and layers >= REACH
         and cells % 8 == 0

time: 32.9 us -> 32 us (0.973)
  blocking collectives: 9.04 us -> 8.19 us
  starting transfers between devices: 12.7 us -> 12.3 us
    ppermute x1, starting transfers between devices: 2.43 us -> 1.49 us  [paired_body(): lax.ppermute(far_edge, 'phi', outer)]
    all_to_all x1, blocking collectives: 9.04 us -> 8.19 us  [over_slabs(): lax.all_to_all(value, ('phi', 'row'), split_axis=0, concat_axis=0, axis_i...]
    ppermute x1, waiting for transfers between devices: 3.27 us -> 3.95 us  [paired_body(): lax.ppermute(far_edge, 'phi', outer)]
    all_to_all x1, starting transfers between devices: 8.57 us -> 9.12 us  [over_slabs(): lax.all_to_all(value, ('phi', 'row'), split_axis=0, concat_axis=0, axis_i...]
    all_to_all x1, waiting for transfers between devices: 0.5 us -> 0.01 us  [over_slabs(): lax.all_to_all(value, ('phi', 'row'), split_axis=0, concat_axis=0, axis_i...]
  transfers between devices with their start and end apart: 7 -> 7, of which waited for: 3 -> 2; matrix products, arithmetic and copies ran while one was open for 0% -> 0% of each run, Pallas kernels for 12% -> 12%
where the time goes in v9:
time: 32 us; the launch traced here: 31.7 us
  starting transfers between devices  12.3 us (38%)
  blocking collectives  8.19 us (26%)
  Pallas kernels  5.13 us (16%)
  waiting for transfers between devices  4.64 us (14%)
  between operations  0.72 us (2%)
  local copies, waits for them, and re-layouts  0.68 us (2%)
    all_to_all x1, starting transfers between devices, over_slabs(): lax.all_to_all(value, ('phi', 'row'), split_axis=0, concat_axis=0, axis_i...  9.12 us
    all_to_all x1, blocking collectives, over_slabs(): lax.all_to_all(value, ('phi', 'row'), split_axis=0, concat_axis=0, axis_i...  8.19 us
    ppermute x1, waiting for transfers between devices, paired_body(): lax.ppermute(far_edge, 'phi', outer)  3.95 us
    ppermute x1, starting transfers between devices, paired_body(): lax.ppermute(far_edge, 'phi', outer)  1.49 us
    pallas_call x1, Pallas kernels, paired_body(): pl.pallas_call(column_kernel, compiler_params=SMALL, out_shape=[struct((c...  1.3 us
    pallas_call x1, Pallas kernels, paired_body(): pl.pallas_call(pack_kernel, compiler_params=SMALL, out_shape=struct((phi_...  1.13 us
    ppermute x4, starting transfers between devices, swap(): return lax.ppermute(value, 'row', [(0, 1), (1, 0)])  1.1 us
    pallas_call x1, Pallas kernels, paired_body(): pl.pallas_call(update_kernel, compiler_params=SMALL, out_shape=[block] *...  0.8 us
  transfers between devices with their start and end apart: 7, of which 2 were waited for; matrix products, arithmetic and copies ran while one was open for 0% of the time, Pallas kernels for 12%

profile of v9, /device:TPU:0, one launch (start us, length us, event | category | flops | bytes accessed | tf_op | source)
XLA Modules:
  0.0 31.7 jit_solution(10867556064392045350)
XLA Ops:
  0.6 0.5 %collective-permute-start = (bf16[256,512]{1,0:T(8,128)(2,1)}, bf16[256,512]{1,0:T(8,128)(2,1)S(1)}, u32[]{:S(2)}, u32[]{:S(2)}) collective-permute-start(bf16[256,512]{1,0:T(8,128)(2,1)} %mag_hbm.1), channel_id=1, source_target_pairs={{0,1},{1,0},{2,3},{3,2},{4,5},{5,4},{6,7},{7,6},{8,9},{9,8},{10,11... | collective-permute-start | bytes 786440 | tf_op jit(solution)/shard_map/ppermute | solution.py:542
  1.1 0.1 collective-permute-start.1
  1.2 0.4 %collective-permute-start.2 = (f32[4,48,128]{2,1,0:T(8,128)}, f32[4,48,128]{2,1,0:T(8,128)S(1)}, u32[]{:S(2)}, u32[]{:S(2)}) collective-permute-start(f32[4,48,128]{2,1,0:T(8,128)} %field_ref.2), channel_id=1, source_target_pairs={{0,1},{1,0},{2,3},{3,2},{4,5},{5,4},{6,7},{7,6},{8,9},{9,8},{10,11... | collective-permute-start | bytes 294920 | tf_op jit(solution)/shard_map/ppermute | solution.py:542
  1.7 1.3 %shard_map.104 = (f32[256,128]{1,0:T(8,128)S(1)}, bf16[256,256]{1,0:T(8,128)(2,1)S(1)}) custom-call(bf16[256,512]{1,0:T(8,128)(2,1)} %mag_hbm.1, bf16[512,128]{1,0:T(8,128)(2,1)} %theta_hbm.1, s32[1,256]{1,0:T(1,128)} %bitcast.14, s32[1,256]{1,0:T(1,128)} %bitcast.15), custom_call_target="tpu_custom_call" | custom-call | tf_op jit(solution)/shard_map/pallas_call | solution.py:562
  3.0 0.0 collective-permute-done.1.theta_ref
  3.0 0.0 collective-permute-done.mag_ref
  3.0 1.1 %shard_map.105 = bf16[16,64,128]{2,1,0:T(8,128)(2,1)} custom-call(f32[256,128]{1,0:T(8,128)S(1)} %get-tuple-element.36.mine_ref, bf16[256,512]{1,0:T(8,128)(2,1)S(1)} %collective-permute-done.mag_ref, bf16[512,128]{1,0:T(8,128)(2,1)S(1)} %collective-permute-done.1.theta_ref, bf16[256,256]{1,0:T(8,128)(2,1)S(1)} %get-tuple-element.37.chosen_ref), custom_call_target="tpu_custom_call" | custom-call | tf_op jit(solution)/shard_map/pallas_call | solution.py:583
  4.1 0.0 collective-permute-done.2.other_ref
  4.1 0.0 copy-start
  4.1 0.0 copy-start.1
  4.1 9.1 %all-to-all-start = ((bf16[16,64,128]{2,1,0:T(8,128)(2,1)}), bf16[16,64,128]{2,1,0:T(8,128)(2,1)S(1)}, u32[]{:S(2)}, u32[]{:S(2)}) async-start(bf16[16,64,128]{2,1,0:T(8,128)(2,1)} %shard_map.105), calls=%async_computation | async-start | bytes 524288 | tf_op jit(solution)/shard_map/all_to_all | solution.py:550
  13.2 0.0 copy-done
  13.2 0.0 copy-done.1
  13.3 0.3 shard_map.106
  13.6 0.0 copy-start.2
  13.6 1.5 %collective-permute-start.3 = (f32[28,128]{1,0:T(8,128)S(1)}, f32[28,128]{1,0:T(8,128)S(1)}, u32[]{:S(2)}, u32[]{:S(2)}) collective-permute-start(f32[28,128]{1,0:T(8,128)S(1)} %get-tuple-element.42), channel_id=1, source_target_pairs={{0,30},{2,4},{4,2},{6,8},{8,6},{10,12},{12,10},{14,16},{16,14},{18... | collective-permute-start | bytes 43016 | tf_op jit(solution)/shard_map/ppermute | solution.py:604
  15.1 0.6 %collective-permute-start.4 = (f32[28,128]{1,0:T(8,128)S(1)}, f32[28,128]{1,0:T(8,128)S(1)}, u32[]{:S(2)}, u32[]{:S(2)}) collective-permute-start(f32[28,128]{1,0:T(8,128)S(1)} %get-tuple-element.43), channel_id=1, source_target_pairs={{0,2},{2,0},{4,6},{6,4},{8,10},{10,8},{12,14},{14,12},{16,18},{18,... | collective-permute-start | bytes 43016 | tf_op jit(solution)/shard_map/ppermute | solution.py:604
  15.7 0.0 copy-start.3
  15.7 0.0 copy-start.4
  15.7 0.0 copy-done.2
  15.7 0.6 %copy-done.3 = f32[8]{0:T(128)S(1)} copy-done((f32[8]{0:T(128)S(1)}, f32[8]{0:T(128)}, u32[]{:S(2)}) %copy-start.3) | copy-done | bytes 56
  16.3 0.0 copy-done.4
  16.3 0.7 %shard_map.107 = (f32[8,56,128]{2,1,0:T(8,128)S(1)}, f32[8,56,128]{2,1,0:T(8,128)S(1)}, f32[2,56,128]{2,1,0:T(8,128)S(1)}, f32[2,8,128]{2,1,0:T(8,128)S(1)}, f32[9,128]{1,0:T(8,128)S(1)}) custom-call(f32[8]{0:T(128)S(1)} %copy-done.3, f32[1,128]{1,0:T(1,128)S(1)} %bitcast.13, f32[6,128]{1,0:T(8,128)S(1)} %bitcast.12), custom_call_target="tpu_custom_call" | custom-call | tf_op jit(solution)/shard_map/pallas_call | solution.py:606
  17.0 3.9 %collective-permute-done.3.far_ref = f32[28,128]{1,0:T(8,128)S(1)} collective-permute-done((f32[28,128]{1,0:T(8,128)S(1)}, f32[28,128]{1,0:T(8,128)S(1)}, u32[]{:S(2)}, u32[]{:S(2)}) %collective-permute-start.3) | collective-permute-done | bytes 14368 | tf_op jit(solution)/shard_map/ppermute | solution.py:604
  21.0 0.0 collective-permute-done.4.near_ref
  21.0 0.0 all-to-all-done.got_ref
  21.0 0.1 shard_map.108.part_ref
  21.1 0.1 collective-permute-start.5
  21.2 0.5 %shard_map.109 = (f32[4,8,128]{2,1,0:T(8,128)S(1)}, f32[5,3,48,128]{3,2,1,0:T(8,128)S(1)}, f32[4,48,128]{2,1,0:T(8,128)S(1)}, f32[4,48,128]{2,1,0:T(8,128)S(1)},...) custom-call(f32[9,128]{1,0:T(8,128)S(1)} %get-tuple-element.52.face_ref, ...), custom_call_target="tpu_custom_call" | custom-call | tf_op jit(solution)/shard_map/pallas_call | solution.py:630
  21.7 0.7 %collective-permute-done.5.rest_ref = f32[56,128]{1,0:T(8,128)S(1)} collective-permute-done((f32[56,128]{1,0:T(8,128)S(1)}, f32[56,128]{1,0:T(8,128)S(1)}, u32[]{:S(2)}, u32[]{:S(2)}) %collective-permute-start.5) | collective-permute-done | bytes 28704 | tf_op jit(solution)/shard_map/ppermute | solution.py:542
  22.4 0.3 shard_map.110
  22.7 8.2 %all_to_all.16 = f32[16,1,128]{2,1,0:T(1,128)S(1)} all-to-all(f32[16,1,128]{2,1,0:T(1,128)S(1)} %bitcast.11), channel_id=1, replica_groups={{23,21,19,17,14,12,10,8,6,4,2,0,31,29,27,25},{22,20,18,16,15,13,11,9,7,..., dimensions={0} | all-to-all | bytes 16384 | tf_op jit(solution)/shard_map/all_to_all | solution.py:550
  30.9 0.8 %shard_map.111 = (f32[4,48,128]{2,1,0:T(8,128)}, f32[4,48,128]{2,1,0:T(8,128)}) custom-call(f32[16,128]{1,0:T(8,128)S(1)} %bitcast.10, f32[4,48,128]{2,1,0:T(8,128)S(1)} %copy-done, f32[4,48,128]{2,1,0:T(8,128)S(1)} %get-tuple-element.64.residual_ref, f32[4,48,128]{2,1,0:T(8,128)S(1)} %get-tuple-element.65.first_ref, ...), custom_call_target="tpu_custom_call" | custom-call | tf_op jit(solution)/shard_map/pallas_call | solution.py:648
Async XLA Ops:
  0.6 2.4 %collective-permute-start = (bf16[256,512]{1,0:T(8,128)(2,1)}, bf16[256,512]{1,0:T(8,128)(2,1)S(1)}, u32[]{:S(2)}, u32[]{:S(2)}) collective-permute-start(bf16[256,512]{1,0:T(8,128)(2,1)} %mag_hbm.1), channel_id=1, source_target_pairs={{0,1},{1,0},{2,3},{3,2},{4,5},{5,4},{6,7},{7,6},{8,9},{9,8},{10,11... | collective-permute-start | bytes 786440 | tf_op jit(solution)/shard_map/ppermute | solution.py:542
  1.1 1.8 %collective-permute-start.1 = (bf16[512,128]{1,0:T(8,128)(2,1)}, bf16[512,128]{1,0:T(8,128)(2,1)S(1)}, u32[]{:S(2)}, u32[]{:S(2)}) collective-permute-start(bf16[512,128]{1,0:T(8,128)(2,1)} %theta_hbm.1), channel_id=1, source_target_pairs={{0,1},{1,0},{2,3},{3,2},{4,5},{5,4},{6,7},{7,6},{8,9},{9,8},{10,11... | collective-permute-start | bytes 393224 | tf_op jit(solution)/shard_map/ppermute | solution.py:542
  1.2 2.9 %collective-permute-start.2 = (f32[4,48,128]{2,1,0:T(8,128)}, f32[4,48,128]{2,1,0:T(8,128)S(1)}, u32[]{:S(2)}, u32[]{:S(2)}) collective-permute-start(f32[4,48,128]{2,1,0:T(8,128)} %field_ref.2), channel_id=1, source_target_pairs={{0,1},{1,0},{2,3},{3,2},{4,5},{5,4},{6,7},{7,6},{8,9},{9,8},{10,11... | collective-permute-start | bytes 294920 | tf_op jit(solution)/shard_map/ppermute | solution.py:542
  4.1 9.1 %copy-start = (f32[4,48,128]{2,1,0:T(8,128)S(1)}, f32[4,48,128]{2,1,0:T(8,128)}, u32[]{:S(2)}) copy-start(f32[4,48,128]{2,1,0:T(8,128)} %field_ref.2) | copy-start | bytes 294916
  4.1 9.1 %copy-start.1 = (bf16[512,48]{0,1:T(8,128)(2,1)S(1)}, bf16[512,48]{0,1:T(8,128)(2,1)}, u32[]{:S(2)}) copy-start(bf16[512,48]{0,1:T(8,128)(2,1)} %param.12) | copy-start | bytes 147460
  4.1 16.9 %all-to-all-start = ((bf16[16,64,128]{2,1,0:T(8,128)(2,1)}), bf16[16,64,128]{2,1,0:T(8,128)(2,1)S(1)}, u32[]{:S(2)}, u32[]{:S(2)}) async-start(bf16[16,64,128]{2,1,0:T(8,128)(2,1)} %shard_map.105), calls=%async_computation | async-start | bytes 524288 | tf_op jit(solution)/shard_map/all_to_all | solution.py:550
  13.6 2.1 %copy-start.2 = (f32[768]{0:T(1024)S(1)}, f32[768]{0:T(1024)}, u32[]{:S(2)}) copy-start(f32[768]{0:T(1024)} %param.16) | copy-start | bytes 9220
  13.6 7.4 %collective-permute-start.3 = (f32[28,128]{1,0:T(8,128)S(1)}, f32[28,128]{1,0:T(8,128)S(1)}, u32[]{:S(2)}, u32[]{:S(2)}) collective-permute-start(f32[28,128]{1,0:T(8,128)S(1)} %get-tuple-element.42), channel_id=1, source_target_pairs={{0,30},{2,4},{4,2},{6,8},{8,6},{10,12},{12,10},{14,16},{16,14},{18... | collective-permute-start | bytes 43016 | tf_op jit(solution)/shard_map/ppermute | solution.py:604
  15.1 5.9 %collective-permute-start.4 = (f32[28,128]{1,0:T(8,128)S(1)}, f32[28,128]{1,0:T(8,128)S(1)}, u32[]{:S(2)}, u32[]{:S(2)}) collective-permute-start(f32[28,128]{1,0:T(8,128)S(1)} %get-tuple-element.43), channel_id=1, source_target_pairs={{0,2},{2,0},{4,6},{6,4},{8,10},{10,8},{12,14},{14,12},{16,18},{18,... | collective-permute-start | bytes 43016 | tf_op jit(solution)/shard_map/ppermute | solution.py:604
  15.7 0.7 %copy-start.3 = (f32[8]{0:T(128)S(1)}, f32[8]{0:T(128)}, u32[]{:S(2)}) copy-start(f32[8]{0:T(128)} %radial_ref) | copy-start | bytes 100
  15.7 0.7 %copy-start.4 = (f32[128]{0:T(128)S(1)}, f32[128]{0:T(128)}, u32[]{:S(2)}) copy-start(f32[128]{0:T(128)} %param.15) | copy-start | bytes 1540
  21.1 1.3 %collective-permute-start.5 = (f32[56,128]{1,0:T(8,128)S(1)}, f32[56,128]{1,0:T(8,128)S(1)}, u32[]{:S(2)}, u32[]{:S(2)}) collective-permute-start(f32[56,128]{1,0:T(8,128)S(1)} %shard_map.108.part_ref), channel_id=1, source_target_pairs={{0,1},{1,0},{2,3},{3,2},{4,5},{5,4},{6,7},{7,6},{8,9},{9,8},{10,11... | collective-permute-start | bytes 86024 | tf_op jit(solution)/shard_map/ppermute | solution.py:542

commit v10 on v9

--- a/solution.py
+++ b/solution.py
@@ -198,7 +198,7 @@
 
 
 def leader(devices):
-    return 11 * devices // 16
+    return 10 * devices // 16
 
 
 def seat(slab, devices):
@@ -544,9 +544,12 @@
     inner = [(i, i ^ 1) for i in range(phi_devices)]
     outer = [(i, (i + (1 if i % 2 else -1)) % phi_devices) for i in range(phi_devices)]
 
-    def over_slabs(value, member, lead):
+    def over_slabs(value, lead):
         order = [(lead - i) % phi_devices for i in range(phi_devices)]
-        groups = [[2 * slab + member(slab, half) for slab in order] for half in range(2)]
+        groups = [
+            [2 * slab + int(share_of(slab, half, phi_devices)) for slab in order]
+            for half in range(2)
+        ]
         return lax.all_to_all(
             value,
             ("phi", "row"),
@@ -590,9 +593,7 @@
     sent, radial_coef, theta_coef, phi_coef, field, other, weights = lax.optimization_barrier(
         (sent, radial_coef, theta_coef, phi_coef, start_field, other, phi_weight.T)
     )
-    got = over_slabs(
-        sent, lambda slab, half: int(share_of(slab, half, phi_devices)), leader(phi_devices)
-    )
+    got = over_slabs(sent, leader(phi_devices))
     edge = struct((every * REACH + 2 * count // width, width), real)
     far_edge, near_edge, share = pl.pallas_call(
         edge_kernel,
@@ -642,9 +643,7 @@
         in_specs=in_vmem(8),
         out_specs=in_vmem(2),
     )(faces, part, swap(part), inv, lon, lat, totals, low)
-    sums = over_slabs(
-        sums, lambda slab, half: int(share_of(slab, half, phi_devices)), leader(phi_devices)
-    )
+    sums = over_slabs(sums, leader(phi_devices) + 1)
     return pl.pallas_call(
         update_kernel,
         compiler_params=SMALL,

time: 32 us -> 31.7 us (level)
  waiting for transfers between devices: 4.64 us -> 4.11 us
    ppermute x1, starting transfers between devices: 1.49 us -> 2.67 us  [paired_body(): lax.ppermute(far_edge, 'phi', outer)]
    all_to_all x1, starting transfers between devices: 9.12 us -> 8.32 us  [over_slabs(): lax.all_to_all(value, ('phi', 'row'), split_axis=0, concat_axis=0, axis_i...]
    ppermute x1, starting transfers between devices: 0.59 us -> 0.01 us  [paired_body(): lax.ppermute(near_edge, 'phi', inner)]
  transfers between devices with their start and end apart: 7 -> 7, of which waited for: 2 -> 2; matrix products, arithmetic and copies ran while one was open for 0% -> 0% of each run, Pallas kernels for 12% -> 13%
where the time goes in v10:
time: 31.7 us; the launch traced here: 31.2 us
  starting transfers between devices  12.4 us (39%)
  blocking collectives  8.19 us (26%)
  Pallas kernels  5.13 us (16%)
  waiting for transfers between devices  4.11 us (13%)
  between operations  0.72 us (2%)
  local copies, waits for them, and re-layouts  0.68 us (2%)
    all_to_all x1, starting transfers between devices, over_slabs(): lax.all_to_all(value, ('phi', 'row'), split_axis=0, concat_axis=0, axis_i...  8.32 us
    all_to_all x1, blocking collectives, over_slabs(): lax.all_to_all(value, ('phi', 'row'), split_axis=0, concat_axis=0, axis_i...  8.19 us
    ppermute x1, waiting for transfers between devices, paired_body(): lax.ppermute(far_edge, 'phi', outer)  3.72 us
    ppermute x1, starting transfers between devices, paired_body(): lax.ppermute(far_edge, 'phi', outer)  2.67 us
    ppermute x4, starting transfers between devices, swap(): return lax.ppermute(value, 'row', [(0, 1), (1, 0)])  1.41 us
    pallas_call x1, Pallas kernels, paired_body(): pl.pallas_call(column_kernel, compiler_params=SMALL, out_shape=[struct((c...  1.3 us
    pallas_call x1, Pallas kernels, paired_body(): pl.pallas_call(pack_kernel, compiler_params=SMALL, out_shape=struct((phi_...  1.13 us
    pallas_call x1, Pallas kernels, paired_body(): pl.pallas_call(update_kernel, compiler_params=SMALL, out_shape=[block] *...  0.8 us
  transfers between devices with their start and end apart: 7, of which 2 were waited for; matrix products, arithmetic and copies ran while one was open for 0% of the time, Pallas kernels for 13%

profile of v10, /device:TPU:0, one launch (start us, length us, event | category | flops | bytes accessed | tf_op | source)
XLA Modules:
  0.0 31.2 jit_solution(6524603809223312766)
XLA Ops:
  0.6 0.5 %collective-permute-start = (bf16[256,512]{1,0:T(8,128)(2,1)}, bf16[256,512]{1,0:T(8,128)(2,1)S(1)}, u32[]{:S(2)}, u32[]{:S(2)}) collective-permute-start(bf16[256,512]{1,0:T(8,128)(2,1)} %mag_hbm.1), channel_id=1, source_target_pairs={{0,1},{1,0},{2,3},{3,2},{4,5},{5,4},{6,7},{7,6},{8,9},{9,8},{10,11... | collective-permute-start | bytes 786440 | tf_op jit(solution)/shard_map/ppermute | solution.py:542
  1.1 0.1 collective-permute-start.1
  1.2 0.4 %collective-permute-start.2 = (f32[4,48,128]{2,1,0:T(8,128)}, f32[4,48,128]{2,1,0:T(8,128)S(1)}, u32[]{:S(2)}, u32[]{:S(2)}) collective-permute-start(f32[4,48,128]{2,1,0:T(8,128)} %field_ref.2), channel_id=1, source_target_pairs={{0,1},{1,0},{2,3},{3,2},{4,5},{5,4},{6,7},{7,6},{8,9},{9,8},{10,11... | collective-permute-start | bytes 294920 | tf_op jit(solution)/shard_map/ppermute | solution.py:542
  1.7 1.3 %shard_map.104 = (f32[256,128]{1,0:T(8,128)S(1)}, bf16[256,256]{1,0:T(8,128)(2,1)S(1)}) custom-call(bf16[256,512]{1,0:T(8,128)(2,1)} %mag_hbm.1, bf16[512,128]{1,0:T(8,128)(2,1)} %theta_hbm.1, s32[1,256]{1,0:T(1,128)} %bitcast.14, s32[1,256]{1,0:T(1,128)} %bitcast.15), custom_call_target="tpu_custom_call" | custom-call | tf_op jit(solution)/shard_map/pallas_call | solution.py:565
  3.0 0.0 collective-permute-done.1.theta_ref
  3.0 0.0 collective-permute-done.mag_ref
  3.0 1.1 %shard_map.105 = bf16[16,64,128]{2,1,0:T(8,128)(2,1)} custom-call(f32[256,128]{1,0:T(8,128)S(1)} %get-tuple-element.36.mine_ref, bf16[256,512]{1,0:T(8,128)(2,1)S(1)} %collective-permute-done.mag_ref, bf16[512,128]{1,0:T(8,128)(2,1)S(1)} %collective-permute-done.1.theta_ref, bf16[256,256]{1,0:T(8,128)(2,1)S(1)} %get-tuple-element.37.chosen_ref), custom_call_target="tpu_custom_call" | custom-call | tf_op jit(solution)/shard_map/pallas_call | solution.py:586
  4.1 0.0 collective-permute-done.2.other_ref
  4.1 0.0 copy-start
  4.1 0.0 copy-start.1
  4.1 8.3 %all-to-all-start = ((bf16[16,64,128]{2,1,0:T(8,128)(2,1)}), bf16[16,64,128]{2,1,0:T(8,128)(2,1)S(1)}, u32[]{:S(2)}, u32[]{:S(2)}) async-start(bf16[16,64,128]{2,1,0:T(8,128)(2,1)} %shard_map.105), calls=%async_computation | async-start | bytes 524288 | tf_op jit(solution)/shard_map/all_to_all | solution.py:553
  12.4 0.0 copy-done
  12.4 0.0 copy-done.1
  12.5 0.3 shard_map.106
  12.8 0.0 copy-start.2
  12.8 2.7 %collective-permute-start.3 = (f32[28,128]{1,0:T(8,128)S(1)}, f32[28,128]{1,0:T(8,128)S(1)}, u32[]{:S(2)}, u32[]{:S(2)}) collective-permute-start(f32[28,128]{1,0:T(8,128)S(1)} %get-tuple-element.42), channel_id=1, source_target_pairs={{0,30},{2,4},{4,2},{6,8},{8,6},{10,12},{12,10},{14,16},{16,14},{18... | collective-permute-start | bytes 43016 | tf_op jit(solution)/shard_map/ppermute | solution.py:605
  15.4 0.0 collective-permute-start.4
  15.4 0.0 copy-start.3
  15.5 0.0 copy-start.4
  15.5 0.0 copy-done.2
  15.5 0.6 %copy-done.3 = f32[8]{0:T(128)S(1)} copy-done((f32[8]{0:T(128)S(1)}, f32[8]{0:T(128)}, u32[]{:S(2)}) %copy-start.3) | copy-done | bytes 56
  16.1 0.0 copy-done.4
  16.1 0.7 %shard_map.107 = (f32[8,56,128]{2,1,0:T(8,128)S(1)}, f32[8,56,128]{2,1,0:T(8,128)S(1)}, f32[2,56,128]{2,1,0:T(8,128)S(1)}, f32[2,8,128]{2,1,0:T(8,128)S(1)}, f32[9,128]{1,0:T(8,128)S(1)}) custom-call(f32[8]{0:T(128)S(1)} %copy-done.3, f32[1,128]{1,0:T(1,128)S(1)} %bitcast.13, f32[6,128]{1,0:T(8,128)S(1)} %bitcast.12), custom_call_target="tpu_custom_call" | custom-call | tf_op jit(solution)/shard_map/pallas_call | solution.py:607
  16.8 3.7 %collective-permute-done.3.far_ref = f32[28,128]{1,0:T(8,128)S(1)} collective-permute-done((f32[28,128]{1,0:T(8,128)S(1)}, f32[28,128]{1,0:T(8,128)S(1)}, u32[]{:S(2)}, u32[]{:S(2)}) %collective-permute-start.3) | collective-permute-done | bytes 14368 | tf_op jit(solution)/shard_map/ppermute | solution.py:605
  20.5 0.0 collective-permute-done.4.near_ref
  20.5 0.0 all-to-all-done.got_ref
  20.5 0.1 shard_map.108.part_ref
  20.7 0.4 %collective-permute-start.5 = (f32[56,128]{1,0:T(8,128)S(1)}, f32[56,128]{1,0:T(8,128)S(1)}, u32[]{:S(2)}, u32[]{:S(2)}) collective-permute-start(f32[56,128]{1,0:T(8,128)S(1)} %shard_map.108.part_ref), channel_id=1, source_target_pairs={{0,1},{1,0},{2,3},{3,2},{4,5},{5,4},{6,7},{7,6},{8,9},{9,8},{10,11... | collective-permute-start | bytes 86024 | tf_op jit(solution)/shard_map/ppermute | solution.py:542
  21.1 0.5 %shard_map.109 = (f32[4,8,128]{2,1,0:T(8,128)S(1)}, f32[5,3,48,128]{3,2,1,0:T(8,128)S(1)}, f32[4,48,128]{2,1,0:T(8,128)S(1)}, f32[4,48,128]{2,1,0:T(8,128)S(1)},...) custom-call(f32[9,128]{1,0:T(8,128)S(1)} %get-tuple-element.52.face_ref, ...), custom_call_target="tpu_custom_call" | custom-call | tf_op jit(solution)/shard_map/pallas_call | solution.py:631
  21.6 0.4 %collective-permute-done.5.rest_ref = f32[56,128]{1,0:T(8,128)S(1)} collective-permute-done((f32[56,128]{1,0:T(8,128)S(1)}, f32[56,128]{1,0:T(8,128)S(1)}, u32[]{:S(2)}, u32[]{:S(2)}) %collective-permute-start.5) | collective-permute-done | bytes 28704 | tf_op jit(solution)/shard_map/ppermute | solution.py:542
  22.0 0.3 shard_map.110
  22.2 8.2 %all_to_all.16 = f32[16,1,128]{2,1,0:T(1,128)S(1)} all-to-all(f32[16,1,128]{2,1,0:T(1,128)S(1)} %bitcast.11), channel_id=1, replica_groups={{23,21,19,17,14,12,10,8,6,4,2,0,31,29,27,25},{22,20,18,16,15,13,11,9,7,..., dimensions={0} | all-to-all | bytes 16384 | tf_op jit(solution)/shard_map/all_to_all | solution.py:553
  30.4 0.8 %shard_map.111 = (f32[4,48,128]{2,1,0:T(8,128)}, f32[4,48,128]{2,1,0:T(8,128)}) custom-call(f32[16,128]{1,0:T(8,128)S(1)} %bitcast.10, f32[4,48,128]{2,1,0:T(8,128)S(1)} %copy-done, f32[4,48,128]{2,1,0:T(8,128)S(1)} %get-tuple-element.64.residual_ref, f32[4,48,128]{2,1,0:T(8,128)S(1)} %get-tuple-element.65.first_ref, ...), custom_call_target="tpu_custom_call" | custom-call | tf_op jit(solution)/shard_map/pallas_call | solution.py:647
Async XLA Ops:
  0.6 2.4 %collective-permute-start = (bf16[256,512]{1,0:T(8,128)(2,1)}, bf16[256,512]{1,0:T(8,128)(2,1)S(1)}, u32[]{:S(2)}, u32[]{:S(2)}) collective-permute-start(bf16[256,512]{1,0:T(8,128)(2,1)} %mag_hbm.1), channel_id=1, source_target_pairs={{0,1},{1,0},{2,3},{3,2},{4,5},{5,4},{6,7},{7,6},{8,9},{9,8},{10,11... | collective-permute-start | bytes 786440 | tf_op jit(solution)/shard_map/ppermute | solution.py:542
  1.1 1.8 %collective-permute-start.1 = (bf16[512,128]{1,0:T(8,128)(2,1)}, bf16[512,128]{1,0:T(8,128)(2,1)S(1)}, u32[]{:S(2)}, u32[]{:S(2)}) collective-permute-start(bf16[512,128]{1,0:T(8,128)(2,1)} %theta_hbm.1), channel_id=1, source_target_pairs={{0,1},{1,0},{2,3},{3,2},{4,5},{5,4},{6,7},{7,6},{8,9},{9,8},{10,11... | collective-permute-start | bytes 393224 | tf_op jit(solution)/shard_map/ppermute | solution.py:542
  1.2 2.9 %collective-permute-start.2 = (f32[4,48,128]{2,1,0:T(8,128)}, f32[4,48,128]{2,1,0:T(8,128)S(1)}, u32[]{:S(2)}, u32[]{:S(2)}) collective-permute-start(f32[4,48,128]{2,1,0:T(8,128)} %field_ref.2), channel_id=1, source_target_pairs={{0,1},{1,0},{2,3},{3,2},{4,5},{5,4},{6,7},{7,6},{8,9},{9,8},{10,11... | collective-permute-start | bytes 294920 | tf_op jit(solution)/shard_map/ppermute | solution.py:542
  4.1 8.3 %copy-start = (f32[4,48,128]{2,1,0:T(8,128)S(1)}, f32[4,48,128]{2,1,0:T(8,128)}, u32[]{:S(2)}) copy-start(f32[4,48,128]{2,1,0:T(8,128)} %field_ref.2) | copy-start | bytes 294916
  4.1 8.3 %copy-start.1 = (bf16[512,48]{0,1:T(8,128)(2,1)S(1)}, bf16[512,48]{0,1:T(8,128)(2,1)}, u32[]{:S(2)}) copy-start(bf16[512,48]{0,1:T(8,128)(2,1)} %param.12) | copy-start | bytes 147460
  4.1 16.4 %all-to-all-start = ((bf16[16,64,128]{2,1,0:T(8,128)(2,1)}), bf16[16,64,128]{2,1,0:T(8,128)(2,1)S(1)}, u32[]{:S(2)}, u32[]{:S(2)}) async-start(bf16[16,64,128]{2,1,0:T(8,128)(2,1)} %shard_map.105), calls=%async_computation | async-start | bytes 524288 | tf_op jit(solution)/shard_map/all_to_all | solution.py:553
  12.8 2.7 %copy-start.2 = (f32[768]{0:T(1024)S(1)}, f32[768]{0:T(1024)}, u32[]{:S(2)}) copy-start(f32[768]{0:T(1024)} %param.16) | copy-start | bytes 9220
  12.8 7.8 %collective-permute-start.3 = (f32[28,128]{1,0:T(8,128)S(1)}, f32[28,128]{1,0:T(8,128)S(1)}, u32[]{:S(2)}, u32[]{:S(2)}) collective-permute-start(f32[28,128]{1,0:T(8,128)S(1)} %get-tuple-element.42), channel_id=1, source_target_pairs={{0,30},{2,4},{4,2},{6,8},{8,6},{10,12},{12,10},{14,16},{16,14},{18... | collective-permute-start | bytes 43016 | tf_op jit(solution)/shard_map/ppermute | solution.py:605
  15.4 5.1 %collective-permute-start.4 = (f32[28,128]{1,0:T(8,128)S(1)}, f32[28,128]{1,0:T(8,128)S(1)}, u32[]{:S(2)}, u32[]{:S(2)}) collective-permute-start(f32[28,128]{1,0:T(8,128)S(1)} %get-tuple-element.43), channel_id=1, source_target_pairs={{0,2},{2,0},{4,6},{6,4},{8,10},{10,8},{12,14},{14,12},{16,18},{18,... | collective-permute-start | bytes 43016 | tf_op jit(solution)/shard_map/ppermute | solution.py:605
  15.4 0.7 %copy-start.3 = (f32[8]{0:T(128)S(1)}, f32[8]{0:T(128)}, u32[]{:S(2)}) copy-start(f32[8]{0:T(128)} %radial_ref) | copy-start | bytes 100
  15.5 0.7 %copy-start.4 = (f32[128]{0:T(128)S(1)}, f32[128]{0:T(128)}, u32[]{:S(2)}) copy-start(f32[128]{0:T(128)} %param.15) | copy-start | bytes 1540
  20.7 1.3 %collective-permute-start.5 = (f32[56,128]{1,0:T(8,128)S(1)}, f32[56,128]{1,0:T(8,128)S(1)}, u32[]{:S(2)}, u32[]{:S(2)}) collective-permute-start(f32[56,128]{1,0:T(8,128)S(1)} %shard_map.108.part_ref), channel_id=1, source_target_pairs={{0,1},{1,0},{2,3},{3,2},{4,5},{5,4},{6,7},{7,6},{8,9},{9,8},{10,11... | collective-permute-start | bytes 86024 | tf_op jit(solution)/shard_map/ppermute | solution.py:542

commit v11 on v10

--- a/solution.py
+++ b/solution.py
@@ -214,16 +214,18 @@
     return share_of(lax.axis_index("phi"), lax.axis_index("row"), devices)
 
 
-def share_weights(weights, half):
-    slots = weights.shape[1]
+def outer_slab():
+    slab, devices = lax.axis_index("phi"), lax.axis_size("phi")
+    return lax.rem(slab + jnp.where(is_odd(), 1, devices - 1), devices)
+
+
+def slot_picker(shape, half):
     devices = lax.axis_size("phi")
-    per = slots // devices // 2
-    slot = lax.broadcasted_iota(jnp.int32, (slots, slots // 2), 0)
-    place = lax.broadcasted_iota(jnp.int32, (slots, slots // 2), 1)
-    source = seat(place // per, devices)
-    wanted = source * (2 * per) + half * per + place % per
-    picker = jnp.where(slot == wanted, 1.0, 0.0).astype(jnp.bfloat16)
-    return jnp.dot(weights, picker, preferred_element_type=jnp.float32).astype(jnp.bfloat16)
+    per = shape[1] // devices
+    slot = lax.broadcasted_iota(jnp.int32, shape, 0)
+    place = lax.broadcasted_iota(jnp.int32, shape, 1)
+    wanted = seat(place // per, devices) * (2 * per) + half * per + place % per
+    return jnp.where(slot == wanted, 1.0, 0.0).astype(jnp.bfloat16)
 
 
 def column_kernel(
@@ -233,6 +235,7 @@
     offset_hbm,
     out_ref,
     chosen_ref,
+    picker_ref,
     mag_ref,
     theta_ref,
     owner_ref,
@@ -248,6 +251,9 @@
     copies = [pltpu.make_async_copy(*pair, done.at[at]) for at, pair in enumerate(pairs)]
     for copy in copies:
         copy.start()
+    outer_half = share_of(outer_slab(), lax.axis_index("row"), lax.axis_size("phi"))
+    for which, half in enumerate((own_half(), outer_half)):
+        picker_ref[which] = slot_picker(picker_ref.shape[1:], half)
     for copy in copies:
         copy.wait()
     out_ref[...] = jnp.dot(mag_ref[...], theta_ref[...], preferred_element_type=jnp.float32)
@@ -279,15 +285,17 @@
     return lax.rem(lax.axis_index("phi"), 2) == 1
 
 
-def edge_kernel(field_ref, other_ref, weight_ref, far_ref, near_ref, share_ref):
+def edge_kernel(field_ref, other_ref, weight_ref, picker_ref, far_ref, near_ref, share_ref):
     layers, cells, width = field_ref.shape
     odd = is_odd()
     first = lax.axis_index("row") == 0
-    slab, devices = lax.axis_index("phi"), lax.axis_size("phi")
-    outer = lax.rem(slab + jnp.where(odd, 1, devices - 1), devices)
-    share = share_weights(weight_ref[...], own_half())
+    share, far_share = (
+        jnp.dot(weight_ref[...], picker_ref[which], preferred_element_type=jnp.float32).astype(
+            jnp.bfloat16
+        )
+        for which in range(2)
+    )
     share_ref[...] = share
-    far_share = share_weights(weight_ref[...], share_of(outer, lax.axis_index("row"), devices))
     near_weights, far_weights = share.astype(jnp.float32), far_share.astype(jnp.float32)
 
     def put(at, up, down):
@@ -562,12 +570,16 @@
     def in_hbm(value):
         return pltpu.with_memory_space_constraint(value, pltpu.HBM)
 
-    mine, chosen = pl.pallas_call(
+    mine, chosen, picker = pl.pallas_call(
         column_kernel,
         compiler_params=SMALL,
-        out_shape=[struct((columns, width), real), struct((count, columns), half)],
+        out_shape=[
+            struct((columns, width), real),
+            struct((count, columns), half),
+            struct((2, 2 * count, count), half),
+        ],
         in_specs=[pl.BlockSpec(memory_space=pltpu.HBM)] * 4,
-        out_specs=in_vmem(2),
+        out_specs=in_vmem(3),
         scratch_shapes=[
             pltpu.VMEM(magnetogram.shape, half),
             pltpu.VMEM(theta_weight.shape, half),
@@ -599,9 +611,9 @@
         edge_kernel,
         compiler_params=SMALL,
         out_shape=[edge, edge, struct((cells, count), half)],
-        in_specs=in_vmem(3),
+        in_specs=in_vmem(4),
         out_specs=in_vmem(3),
-    )(field, other, weights)
+    )(field, other, weights, picker)
     far_edge, near_edge = lax.ppermute(far_edge, "phi", outer), lax.ppermute(near_edge, "phi", inner)
     lines = struct((every, spread, width), real)
     diag, inv, lon, lat, faces = pl.pallas_call(

time: 31.7 us -> 31.7 us (level)
  transfers between devices with their start and end apart: 7 -> 7, of which waited for: 2 -> 2; matrix products, arithmetic and copies ran while one was open for 0% -> 0% of each run, Pallas kernels for 13% -> 12%
where the time goes in v11:
time: 31.7 us; the launch traced here: 31.2 us
  starting transfers between devices  12.4 us (39%)
  blocking collectives  8.19 us (26%)
  Pallas kernels  5.02 us (16%)
  waiting for transfers between devices  4.19 us (13%)
  between operations  0.72 us (2%)
  local copies, waits for them, and re-layouts  0.68 us (2%)
    all_to_all x1, starting transfers between devices, over_slabs(): lax.all_to_all(value, ('phi', 'row'), split_axis=0, concat_axis=0, axis_i...  8.33 us
    all_to_all x1, blocking collectives, over_slabs(): lax.all_to_all(value, ('phi', 'row'), split_axis=0, concat_axis=0, axis_i...  8.19 us
    ppermute x1, waiting for transfers between devices, paired_body(): lax.ppermute(far_edge, 'phi', outer)  3.81 us
    ppermute x1, starting transfers between devices, paired_body(): lax.ppermute(far_edge, 'phi', outer)  2.67 us
    ppermute x4, starting transfers between devices, swap(): return lax.ppermute(value, 'row', [(0, 1), (1, 0)])  1.41 us
    pallas_call x1, Pallas kernels, paired_body(): pl.pallas_call(column_kernel, compiler_params=SMALL, out_shape=[struct((c...  1.29 us
    pallas_call x1, Pallas kernels, paired_body(): pl.pallas_call(pack_kernel, compiler_params=SMALL, out_shape=struct((phi_...  1.12 us
    pallas_call x1, Pallas kernels, paired_body(): pl.pallas_call(update_kernel, compiler_params=SMALL, out_shape=[block] *...  0.8 us
  transfers between devices with their start and end apart: 7, of which 2 were waited for; matrix products, arithmetic and copies ran while one was open for 0% of the time, Pallas kernels for 12%

profile of v11, /device:TPU:0, one launch (start us, length us, event | category | flops | bytes accessed | tf_op | source)
XLA Modules:
  0.0 31.2 jit_solution(977485497719063194)
XLA Ops:
  0.6 0.5 %collective-permute-start = (bf16[256,512]{1,0:T(8,128)(2,1)}, bf16[256,512]{1,0:T(8,128)(2,1)S(1)}, u32[]{:S(2)}, u32[]{:S(2)}) collective-permute-start(bf16[256,512]{1,0:T(8,128)(2,1)} %mag_hbm.1), channel_id=1, source_target_pairs={{0,1},{1,0},{2,3},{3,2},{4,5},{5,4},{6,7},{7,6},{8,9},{9,8},{10,11... | collective-permute-start | bytes 786440 | tf_op jit(solution)/shard_map/ppermute | solution.py:550
  1.1 0.1 collective-permute-start.1
  1.2 0.4 %collective-permute-start.2 = (f32[4,48,128]{2,1,0:T(8,128)}, f32[4,48,128]{2,1,0:T(8,128)S(1)}, u32[]{:S(2)}, u32[]{:S(2)}) collective-permute-start(f32[4,48,128]{2,1,0:T(8,128)} %field_ref.2), channel_id=1, source_target_pairs={{0,1},{1,0},{2,3},{3,2},{4,5},{5,4},{6,7},{7,6},{8,9},{9,8},{10,11... | collective-permute-start | bytes 294920 | tf_op jit(solution)/shard_map/ppermute | solution.py:550
  1.7 1.3 %shard_map.104 = (f32[256,128]{1,0:T(8,128)S(1)}, bf16[256,256]{1,0:T(8,128)(2,1)S(1)}, bf16[2,512,256]{2,1,0:T(8,128)(2,1)S(1)}) custom-call(bf16[256,512]{1,0:T(8,128)(2,1)} %mag_hbm.1, bf16[512,128]{1,0:T(8,128)(2,1)} %theta_hbm.1, s32[1,256]{1,0:T(1,128)} %bitcast.14, s32[1,256]{1,0:T(1,128)} %bitcast.15), custom_call_target="tpu_custom_call" | custom-call | tf_op jit(solution)/shard_map/pallas_call | solution.py:573
  3.0 0.0 collective-permute-done.1.theta_ref
  3.0 0.0 collective-permute-done.mag_ref
  3.0 1.1 %shard_map.105 = bf16[16,64,128]{2,1,0:T(8,128)(2,1)} custom-call(f32[256,128]{1,0:T(8,128)S(1)} %get-tuple-element.37.mine_ref, bf16[256,512]{1,0:T(8,128)(2,1)S(1)} %collective-permute-done.mag_ref, bf16[512,128]{1,0:T(8,128)(2,1)S(1)} %collective-permute-done.1.theta_ref, bf16[256,256]{1,0:T(8,128)(2,1)S(1)} %get-tuple-element.38.chosen_ref), custom_call_target="tpu_custom_call" | custom-call | tf_op jit(solution)/shard_map/pallas_call | solution.py:598
  4.1 0.0 collective-permute-done.2.other_ref
  4.1 0.0 copy-start
  4.1 0.0 copy-start.1
  4.1 8.3 %all-to-all-start = ((bf16[16,64,128]{2,1,0:T(8,128)(2,1)}), bf16[16,64,128]{2,1,0:T(8,128)(2,1)S(1)}, u32[]{:S(2)}, u32[]{:S(2)}) async-start(bf16[16,64,128]{2,1,0:T(8,128)(2,1)} %shard_map.105), calls=%async_computation | async-start | bytes 524288 | tf_op jit(solution)/shard_map/all_to_all | solution.py:561
  12.4 0.0 copy-done
  12.4 0.0 copy-done.1
  12.5 0.2 shard_map.106
  12.7 0.0 copy-start.2
  12.7 2.7 %collective-permute-start.3 = (f32[28,128]{1,0:T(8,128)S(1)}, f32[28,128]{1,0:T(8,128)S(1)}, u32[]{:S(2)}, u32[]{:S(2)}) collective-permute-start(f32[28,128]{1,0:T(8,128)S(1)} %get-tuple-element.44), channel_id=1, source_target_pairs={{0,30},{2,4},{4,2},{6,8},{8,6},{10,12},{12,10},{14,16},{16,14},{18... | collective-permute-start | bytes 43016 | tf_op jit(solution)/shard_map/ppermute | solution.py:617
  15.4 0.0 collective-permute-start.4
  15.4 0.0 copy-start.3
  15.4 0.0 copy-start.4
  15.4 0.0 copy-done.2
  15.4 0.6 %copy-done.3 = f32[8]{0:T(128)S(1)} copy-done((f32[8]{0:T(128)S(1)}, f32[8]{0:T(128)}, u32[]{:S(2)}) %copy-start.3) | copy-done | bytes 56
  16.0 0.0 copy-done.4
  16.0 0.7 %shard_map.107 = (f32[8,56,128]{2,1,0:T(8,128)S(1)}, f32[8,56,128]{2,1,0:T(8,128)S(1)}, f32[2,56,128]{2,1,0:T(8,128)S(1)}, f32[2,8,128]{2,1,0:T(8,128)S(1)}, f32[9,128]{1,0:T(8,128)S(1)}) custom-call(f32[8]{0:T(128)S(1)} %copy-done.3, f32[1,128]{1,0:T(1,128)S(1)} %bitcast.13, f32[6,128]{1,0:T(8,128)S(1)} %bitcast.12), custom_call_target="tpu_custom_call" | custom-call | tf_op jit(solution)/shard_map/pallas_call | solution.py:619
  16.7 3.8 %collective-permute-done.3.far_ref = f32[28,128]{1,0:T(8,128)S(1)} collective-permute-done((f32[28,128]{1,0:T(8,128)S(1)}, f32[28,128]{1,0:T(8,128)S(1)}, u32[]{:S(2)}, u32[]{:S(2)}) %collective-permute-start.3) | collective-permute-done | bytes 14368 | tf_op jit(solution)/shard_map/ppermute | solution.py:617
  20.5 0.0 collective-permute-done.4.near_ref
  20.5 0.0 all-to-all-done.got_ref
  20.5 0.1 shard_map.108.part_ref
  20.7 0.4 %collective-permute-start.5 = (f32[56,128]{1,0:T(8,128)S(1)}, f32[56,128]{1,0:T(8,128)S(1)}, u32[]{:S(2)}, u32[]{:S(2)}) collective-permute-start(f32[56,128]{1,0:T(8,128)S(1)} %shard_map.108.part_ref), channel_id=1, source_target_pairs={{0,1},{1,0},{2,3},{3,2},{4,5},{5,4},{6,7},{7,6},{8,9},{9,8},{10,11... | collective-permute-start | bytes 86024 | tf_op jit(solution)/shard_map/ppermute | solution.py:550
  21.1 0.5 %shard_map.109 = (f32[4,8,128]{2,1,0:T(8,128)S(1)}, f32[5,3,48,128]{3,2,1,0:T(8,128)S(1)}, f32[4,48,128]{2,1,0:T(8,128)S(1)}, f32[4,48,128]{2,1,0:T(8,128)S(1)},...) custom-call(f32[9,128]{1,0:T(8,128)S(1)} %get-tuple-element.54.face_ref, ...), custom_call_target="tpu_custom_call" | custom-call | tf_op jit(solution)/shard_map/pallas_call | solution.py:643
  21.6 0.4 %collective-permute-done.5.rest_ref = f32[56,128]{1,0:T(8,128)S(1)} collective-permute-done((f32[56,128]{1,0:T(8,128)S(1)}, f32[56,128]{1,0:T(8,128)S(1)}, u32[]{:S(2)}, u32[]{:S(2)}) %collective-permute-start.5) | collective-permute-done | bytes 28704 | tf_op jit(solution)/shard_map/ppermute | solution.py:550
  22.0 0.3 shard_map.110
  22.2 8.2 %all_to_all.16 = f32[16,1,128]{2,1,0:T(1,128)S(1)} all-to-all(f32[16,1,128]{2,1,0:T(1,128)S(1)} %bitcast.11), channel_id=1, replica_groups={{23,21,19,17,14,12,10,8,6,4,2,0,31,29,27,25},{22,20,18,16,15,13,11,9,7,..., dimensions={0} | all-to-all | bytes 16384 | tf_op jit(solution)/shard_map/all_to_all | solution.py:561
  30.4 0.8 %shard_map.111 = (f32[4,48,128]{2,1,0:T(8,128)}, f32[4,48,128]{2,1,0:T(8,128)}) custom-call(f32[16,128]{1,0:T(8,128)S(1)} %bitcast.10, f32[4,48,128]{2,1,0:T(8,128)S(1)} %copy-done, f32[4,48,128]{2,1,0:T(8,128)S(1)} %get-tuple-element.66.residual_ref, f32[4,48,128]{2,1,0:T(8,128)S(1)} %get-tuple-element.67.first_ref, ...), custom_call_target="tpu_custom_call" | custom-call | tf_op jit(solution)/shard_map/pallas_call | solution.py:659
Async XLA Ops:
  0.6 2.3 %collective-permute-start = (bf16[256,512]{1,0:T(8,128)(2,1)}, bf16[256,512]{1,0:T(8,128)(2,1)S(1)}, u32[]{:S(2)}, u32[]{:S(2)}) collective-permute-start(bf16[256,512]{1,0:T(8,128)(2,1)} %mag_hbm.1), channel_id=1, source_target_pairs={{0,1},{1,0},{2,3},{3,2},{4,5},{5,4},{6,7},{7,6},{8,9},{9,8},{10,11... | collective-permute-start | bytes 786440 | tf_op jit(solution)/shard_map/ppermute | solution.py:550
  1.1 1.8 %collective-permute-start.1 = (bf16[512,128]{1,0:T(8,128)(2,1)}, bf16[512,128]{1,0:T(8,128)(2,1)S(1)}, u32[]{:S(2)}, u32[]{:S(2)}) collective-permute-start(bf16[512,128]{1,0:T(8,128)(2,1)} %theta_hbm.1), channel_id=1, source_target_pairs={{0,1},{1,0},{2,3},{3,2},{4,5},{5,4},{6,7},{7,6},{8,9},{9,8},{10,11... | collective-permute-start | bytes 393224 | tf_op jit(solution)/shard_map/ppermute | solution.py:550
  1.2 2.9 %collective-permute-start.2 = (f32[4,48,128]{2,1,0:T(8,128)}, f32[4,48,128]{2,1,0:T(8,128)S(1)}, u32[]{:S(2)}, u32[]{:S(2)}) collective-permute-start(f32[4,48,128]{2,1,0:T(8,128)} %field_ref.2), channel_id=1, source_target_pairs={{0,1},{1,0},{2,3},{3,2},{4,5},{5,4},{6,7},{7,6},{8,9},{9,8},{10,11... | collective-permute-start | bytes 294920 | tf_op jit(solution)/shard_map/ppermute | solution.py:550
  4.1 8.3 %copy-start = (f32[4,48,128]{2,1,0:T(8,128)S(1)}, f32[4,48,128]{2,1,0:T(8,128)}, u32[]{:S(2)}) copy-start(f32[4,48,128]{2,1,0:T(8,128)} %field_ref.2) | copy-start | bytes 294916
  4.1 8.3 %copy-start.1 = (bf16[512,48]{0,1:T(8,128)(2,1)S(1)}, bf16[512,48]{0,1:T(8,128)(2,1)}, u32[]{:S(2)}) copy-start(bf16[512,48]{0,1:T(8,128)(2,1)} %param.12) | copy-start | bytes 147460
  4.1 16.4 %all-to-all-start = ((bf16[16,64,128]{2,1,0:T(8,128)(2,1)}), bf16[16,64,128]{2,1,0:T(8,128)(2,1)S(1)}, u32[]{:S(2)}, u32[]{:S(2)}) async-start(bf16[16,64,128]{2,1,0:T(8,128)(2,1)} %shard_map.105), calls=%async_computation | async-start | bytes 524288 | tf_op jit(solution)/shard_map/all_to_all | solution.py:561
  12.7 2.7 %copy-start.2 = (f32[768]{0:T(1024)S(1)}, f32[768]{0:T(1024)}, u32[]{:S(2)}) copy-start(f32[768]{0:T(1024)} %param.16) | copy-start | bytes 9220
  12.7 7.9 %collective-permute-start.3 = (f32[28,128]{1,0:T(8,128)S(1)}, f32[28,128]{1,0:T(8,128)S(1)}, u32[]{:S(2)}, u32[]{:S(2)}) collective-permute-start(f32[28,128]{1,0:T(8,128)S(1)} %get-tuple-element.44), channel_id=1, source_target_pairs={{0,30},{2,4},{4,2},{6,8},{8,6},{10,12},{12,10},{14,16},{16,14},{18... | collective-permute-start | bytes 43016 | tf_op jit(solution)/shard_map/ppermute | solution.py:617
  15.4 5.2 %collective-permute-start.4 = (f32[28,128]{1,0:T(8,128)S(1)}, f32[28,128]{1,0:T(8,128)S(1)}, u32[]{:S(2)}, u32[]{:S(2)}) collective-permute-start(f32[28,128]{1,0:T(8,128)S(1)} %get-tuple-element.45), channel_id=1, source_target_pairs={{0,2},{2,0},{4,6},{6,4},{8,10},{10,8},{12,14},{14,12},{16,18},{18,... | collective-permute-start | bytes 43016 | tf_op jit(solution)/shard_map/ppermute | solution.py:617
  15.4 0.7 %copy-start.3 = (f32[8]{0:T(128)S(1)}, f32[8]{0:T(128)}, u32[]{:S(2)}) copy-start(f32[8]{0:T(128)} %radial_ref) | copy-start | bytes 100
  15.4 0.7 %copy-start.4 = (f32[128]{0:T(128)S(1)}, f32[128]{0:T(128)}, u32[]{:S(2)}) copy-start(f32[128]{0:T(128)} %param.15) | copy-start | bytes 1540
  20.7 1.3 %collective-permute-start.5 = (f32[56,128]{1,0:T(8,128)S(1)}, f32[56,128]{1,0:T(8,128)S(1)}, u32[]{:S(2)}, u32[]{:S(2)}) collective-permute-start(f32[56,128]{1,0:T(8,128)S(1)} %shard_map.108.part_ref), channel_id=1, source_target_pairs={{0,1},{1,0},{2,3},{3,2},{4,5},{5,4},{6,7},{7,6},{8,9},{9,8},{10,11... | collective-permute-start | bytes 86024 | tf_op jit(solution)/shard_map/ppermute | solution.py:550
